TPU v7x, 32 devices: a whole 2x2x4 slice. The times are simulated.
32 devices in a mesh: fsdp: 8 (over z, x), ctx: 4 (over y, core).
Axes of the slice: x: 2, y: 2, z: 4, core: 2. Of those that a mesh axis runs over, the one named last changes fastest.
Arguments:
- loaded: bfloat16 [8192, 12288], P(('fsdp', 'ctx')), may hold values from -6 to 6
- route: int32 [32, 8], P(('fsdp', 'ctx')), may hold values from 0 to 7, each once within a row
- doc_ids: int32 [8, 1024], P('fsdp'), may hold values from 0 to 7, never falling along the last dimension, each value on 1 to 512 neighbouring positions
- short_filter: float32 [7, 768], replicated, may hold values from -2 to 2
- medium_filter: bfloat16 [128, 256], replicated, may hold values from -0.5 to 0.5
- out_weight: bfloat16 [4096, 8192], P('fsdp', 'ctx'), may hold values from -0.09375 to 0.09375
Outputs:
- mixed: bfloat16 [8192, 8192], P(('fsdp', 'ctx'))
Inputs may be any that keep to these rules, and one draw needn't show every extreme that they name: Each row of route names every sequence 0 to 7 exactly once. `doc_ids`: along each sequence the document numbers never fall; each document spans 1 to 512 positions and one spans exactly 512.
All inputs are finite; a program needn't handle non-finite values.
Results may differ from a plain program's by a relative error of at most 0.0058.
Values may be sent and summed in bfloat16 or wider, within the bound.
No kernel may reach another device: no remote copies, remote signals or barrier semaphores. Data moves between devices by JAX's collectives and lax.ppermute only.
A program may use at most 128 MiB of HBM per device.

v0:
```python
import functools

import jax
import jax.numpy as jnp
from jax import lax
from jax.experimental import pallas as pl
from jax.experimental.pallas import tpu as pltpu
from jax.sharding import Mesh
from jax.sharding import PartitionSpec as P

FSDP = ("fh", "fx")
CTX = ("y", "core")
PLANE = ("fx", "y", "core")
EVERY = ("fh", "fx", "y", "core")
SWAP = [(0, 1), (1, 0)]
CHUNKS = 4
QUARTERS = 4
PANEL_STEPS = (("keep", 0, 2, 1, 3), ("keep", 2, 2, 3, 5), ("got", 0, 2, 4, 6), ("got", 2, 2, 5, 9))
FENCED = 5
PROJECTS = ((0, 2), (2, 2))
ROWS = 128
LANES = 128
MIB = 1 << 20
LIGHT = pl.CostEstimate(flops=1, bytes_accessed=1, transcendentals=0)


def short_kernel(order, order_prev, q, k, v, hq, hk, hv, fq, fk, fv, mask, out, ext):
    rows, wide = q.shape[1], q.shape[2]
    taps = hq.shape[1] + 1
    pad = 8
    linked = [jnp.broadcast_to(mask[0, :, i : i + 1], (rows, LANES)) for i in range(1, taps)]
    for first in range(0, wide, LANES):
        cols = slice(first, first + LANES)

        def conv(slot, block, halo, taps_ref):
            ext[slot, pad - (taps - 1) : pad] = halo[0, :, cols].astype(jnp.float32)
            own = block[0, :, cols].astype(jnp.float32)
            ext[slot, pad : pad + rows] = own
            total = taps_ref[0:1, cols] * own
            for i in range(1, taps):
                near = ext[slot, pad - i : pad - i + rows] * linked[i - 1]
                total = total + taps_ref[i : i + 1, cols] * near
            return total

        out[0, :, first : first + LANES] = conv(0, q, hq, fq).astype(jnp.bfloat16)
        gate = conv(1, k, hk, fk) * conv(2, v, hv, fv)
        out[0, :, wide + first : wide + first + LANES] = gate.astype(jnp.bfloat16)


def short_call(order, order_prev, blocks, halo, taps_full, mask, chunk):
    count, rows, wide = blocks.shape
    cols = wide // 3 // CHUNKS

    def of_block(part):
        return pl.BlockSpec((1, rows, cols), lambda g, o, p: (o[g], 0, part * CHUNKS + chunk))

    def of_halo(part):
        return pl.BlockSpec((1, halo.shape[1], cols), lambda g, o, p: (p[g], 0, part * CHUNKS + chunk))

    def of_taps(part):
        return pl.BlockSpec((taps_full.shape[0], cols), lambda g, o, p: (0, part * CHUNKS + chunk))

    parts = range(3)
    return pl.pallas_call(
        short_kernel,
        grid_spec=pltpu.PrefetchScalarGridSpec(
            num_scalar_prefetch=2,
            grid=(count,),
            in_specs=[of_block(p) for p in parts]
            + [of_halo(p) for p in parts]
            + [of_taps(p) for p in parts]
            + [pl.BlockSpec((1,) + mask.shape[1:], lambda g, o, p: (g, 0, 0))],
            out_specs=pl.BlockSpec((1, rows, 2 * cols), lambda g, o, p: (g, 0, 0)),
            scratch_shapes=[pltpu.VMEM((3, 8 + rows, LANES), jnp.float32)],
        ),
        out_shape=jax.ShapeDtypeStruct((count, rows, 2 * cols), jnp.bfloat16),
        cost_estimate=LIGHT,
        name="short_conv",
    )(order, order_prev, blocks, blocks, blocks, halo, halo, halo, taps_full, taps_full, taps_full, mask)


def medium_kernel(group_size, q, gate, halo, taps, same, out):
    blocks = gate.shape[0] // ROWS
    lane = lax.broadcasted_iota(jnp.int32, (ROWS, LANES), 1) // group_size
    windows, totals = [], []
    for a in range(blocks):
        before = halo[...] if a == 0 else gate[(a - 1) * ROWS : a * ROWS]
        windows.append(jnp.concatenate([before, gate[a * ROWS : (a + 1) * ROWS]], axis=0))
        totals.append(jnp.zeros((ROWS, LANES), jnp.float32))
    for n in range(taps.shape[0]):
        row = jnp.broadcast_to(taps[n : n + 1], (ROWS, 2 * ROWS))
        matrix = pltpu.roll(row, 0, 1, stride=1, stride_axis=0).astype(jnp.bfloat16)
        for a in range(blocks):
            result = jnp.dot(matrix * same[a], windows[a], preferred_element_type=jnp.float32)
            totals[a] = jnp.where(lane == n, result, totals[a])
    for a in range(blocks):
        rows = slice(a * ROWS, (a + 1) * ROWS)
        out[rows] = (q[rows].astype(jnp.float32) * totals[a]).astype(jnp.bfloat16)


def medium_call(routed, halo, taps, same, chunk, group_size):
    rows, cols = routed.shape[0], routed.shape[1] // 2
    steps = cols // LANES
    groups = LANES // group_size
    return pl.pallas_call(
        functools.partial(medium_kernel, group_size),
        grid=(steps,),
        in_specs=[
            pl.BlockSpec((rows, LANES), lambda t: (0, t)),
            pl.BlockSpec((rows, LANES), lambda t: (0, steps + t)),
            pl.BlockSpec((ROWS, LANES), lambda t: (0, t)),
            pl.BlockSpec((groups, 2 * ROWS), lambda t: (chunk * steps + t, 0)),
            pl.BlockSpec(same.shape, lambda t: (0, 0, 0)),
        ],
        out_specs=pl.BlockSpec((rows, LANES), lambda t: (0, t)),
        out_shape=jax.ShapeDtypeStruct((rows, cols), jnp.bfloat16),
        cost_estimate=LIGHT,
        name="medium_conv",
    )(routed, routed, halo, taps, same)


def project_kernel(count, side, dest, *refs):
    pieces, panels, out = refs[:-3], refs[-3:-1], refs[-1]
    held, depth = pieces[0].shape
    tile = out.shape[0] // count
    for half in range(2):
        given = pieces[half * len(pieces) // 2 : (half + 1) * len(pieces) // 2]
        total = None
        for m, piece in enumerate(given):
            i, other = m // 2, m % 2
            rows = panels[other][i * depth : (i + 1) * depth]
            term = jnp.dot(piece[...], rows, preferred_element_type=jnp.float32)
            total = term if total is None else total + term
        total = total.astype(jnp.bfloat16)
        for m in range(held // tile):
            at = pl.multiple_of(dest[half * held // tile + m] * tile, tile)
            out[pl.ds(at, tile)] = total[m * tile : (m + 1) * tile]


def project_call(side, dest, here, there, panels, cols, depth):
    held, wide = here[0].shape
    tile = min(256, cols)

    def specs():
        for i in range(wide // (2 * depth)):
            for other in range(2):
                yield pl.BlockSpec(
                    (held, depth),
                    lambda n, s, d, i=i, other=other: (0, 2 * i + (s[0] + other) % 2),
                    pipeline_mode=pl.Buffered(1),
                )

    given = [x for x in list(here) + list(there) for _ in range(wide // depth)]
    return pl.pallas_call(
        functools.partial(project_kernel, dest.shape[0]),
        grid_spec=pltpu.PrefetchScalarGridSpec(
            num_scalar_prefetch=2,
            grid=(cols // tile,),
            in_specs=[spec for _ in list(here) + list(there) for spec in specs()]
            + [
                pl.BlockSpec((p.shape[0], tile), lambda n, s, d, at=at // tile: (0, at + n))
                for p, at in panels
            ],
            out_specs=pl.BlockSpec((2 * held, tile), lambda n, s, d: (0, n)),
        ),
        out_shape=jax.ShapeDtypeStruct((2 * held, cols), jnp.bfloat16),
        compiler_params=pltpu.CompilerParams(vmem_limit_bytes=56 * MIB),
        cost_estimate=LIGHT,
        name="project",
    )(side, dest, *given, *(p for p, _ in panels))


def stack_kernel(*refs):
    out = refs[-1]
    rows = refs[0].shape[0]
    for m, piece in enumerate(refs[:-1]):
        out[m * rows : (m + 1) * rows] = piece[...]


def stack_call(pieces):
    rows, cols = pieces[0].shape
    tile = min(256, cols)
    return pl.pallas_call(
        stack_kernel,
        grid=(cols // tile,),
        in_specs=[pl.BlockSpec((rows, tile), lambda n: (0, n)) for _ in pieces],
        out_specs=pl.BlockSpec((len(pieces) * rows, tile), lambda n: (0, n)),
        out_shape=jax.ShapeDtypeStruct((len(pieces) * rows, cols), pieces[0].dtype),
        cost_estimate=LIGHT,
        name="stack",
    )(*pieces)


def place_kernel(*refs):
    out, at = refs[-1], 0
    for part in refs[:-1]:
        out[:, at : at + part.shape[2]] = part[0]
        at += part.shape[2]


def place_call(parts, ctx_count):
    count, rows = parts[0].shape[:2]
    wide = sum(p.shape[2] for p in parts)
    return pl.pallas_call(
        place_kernel,
        grid=(count,),
        in_specs=[pl.BlockSpec((1, rows, p.shape[2]), lambda s: (s, 0, 0)) for p in parts],
        out_specs=pl.BlockSpec(
            (rows, wide), lambda s: (0, (s % ctx_count) * (count // ctx_count) + s // ctx_count)
        ),
        out_shape=jax.ShapeDtypeStruct((rows, count * wide), parts[0].dtype),
        compiler_params=pltpu.CompilerParams(vmem_limit_bytes=16 * MIB),
        cost_estimate=LIGHT,
        name="place",
    )(*parts)


def after(value, *others):
    return lax.optimization_barrier((value,) + others)[0]


def on_device(loaded, route, doc_ids, short_filter, medium_filter, out_weight):
    tok_rows, wide = loaded.shape
    channels = wide // 3
    count = lax.axis_size(FSDP)
    ctx_count = lax.axis_size(CTX)
    blk = tok_rows // count
    short_len = short_filter.shape[0]
    depth = short_len - 1
    medium_len = medium_filter.shape[0]
    group_size = wide // short_filter.shape[1]
    length = doc_ids.shape[1]
    cols = channels // CHUNKS
    ctx_at = lax.axis_index(CTX)
    f_at = lax.axis_index(FSDP)
    x_at = lax.axis_index("fx")

    shift = []
    for f in range(count):
        for c in range(ctx_count):
            if f + 1 < count:
                shift.append((f * ctx_count + c, (f + 1) * ctx_count + c))
            elif c + 1 < ctx_count:
                shift.append((f * ctx_count + c, c + 1))

    seqs = jnp.arange(count, dtype=jnp.int32)
    order = jnp.sum(jnp.where(route[0][None, :] == seqs[:, None], seqs[None, :], 0), axis=1)
    order_prev = lax.ppermute(order, EVERY, shift)
    blocks = loaded.reshape(count, blk, wide)
    tail = blocks[:, blk - depth :].reshape(count * depth, wide)
    halo = lax.ppermute(tail, EVERY, shift).reshape(count, depth, wide)
    own_ids = jnp.concatenate([jnp.full((depth,), -1, jnp.int32), doc_ids[0]])
    own_ids = lax.dynamic_slice_in_dim(own_ids, ctx_at * tok_rows, depth + tok_rows, 0)
    near = jnp.stack([own_ids[f * blk : (f + 1) * blk + depth] for f in range(count)])
    near = after(near, tail)
    near = lax.all_to_all(near, FSDP, split_axis=0, concat_axis=0, tiled=True)


    taps_full = jnp.repeat(short_filter, group_size, axis=1)

    half = out_weight.shape[1] // 2
    keep = lax.dynamic_slice_in_dim(out_weight, x_at * half, half, 1)
    give = lax.dynamic_slice_in_dim(out_weight, (1 - x_at) * half, half, 1)

    reach = ROWS - medium_len
    medium_rows = jnp.pad(
        medium_filter.astype(jnp.float32)[::-1].T, ((0, 0), (reach + 1, ROWS - 1))
    )
    own = jnp.concatenate([jnp.full((ROWS,), -1, jnp.int32), doc_ids[0]])
    own = lax.dynamic_slice_in_dim(own, ctx_at * tok_rows, ROWS + tok_rows, 0)
    same = jnp.stack(
        [
            own[ROWS + a : 2 * ROWS + a][:, None] == own[a : 2 * ROWS + a][None, :]
            for a in range(0, tok_rows, ROWS)
        ]
    ).astype(jnp.bfloat16)

    next_ctx = [(c, c + 1) for c in range(ctx_count - 1)]

    def exchange(sent):
        routed = lax.all_to_all(sent, FSDP, split_axis=0, concat_axis=0, tiled=True)
        return routed.reshape(tok_rows, 2 * cols)

    live, flying = {}, {}
    def cut_panels(kind, value):
        for k, first, wide, _, _ in PANEL_STEPS:
            if k == kind:
                at = half // QUARTERS * first
                live["part", kind, first] = value[:, at : at + half // QUARTERS * wide]

    cut_panels("keep", keep)

    def fence(step):
        for key in [k for k, (due, _) in flying.items() if due <= step]:
            live[key] = flying.pop(key)[1]
        if step > FENCED:
            return
        keys = list(live)
        for key, value in zip(keys, lax.optimization_barrier([live[k] for k in keys])):
            live[key] = value

    def start_panels(step):
        for kind, first, wide, begin, due in PANEL_STEPS:
            if begin == step:
                source = live.pop(("part", kind, first))
                flying[kind, first, wide] = (due, lax.all_gather(source, "fh", axis=0, tiled=True))

    start_panels(0)
    halo, near, order_prev = lax.optimization_barrier((halo, near, order_prev))
    mask = jnp.stack(
        [near[:, depth - i : depth - i + blk] == near[:, depth:] for i in range(short_len)], axis=-1
    ).astype(jnp.float32)
    live["give"] = give
    live["sent", 0] = short_call(order, order_prev, blocks, halo, taps_full, mask, 0)
    live["mask"] = mask
    live["prior"] = order_prev
    live["medium"] = medium_rows
    live["same"] = same
    last = CHUNKS + 4
    for step in range(1, last + 1):
        if "got" in live:
            cut_panels("got", live.pop("got"))
        fence(step)
        start_panels(step)
        if step == 1:
            flying["got"] = (3, lax.ppermute(live.pop("give"), "fx", SWAP))
        if step <= CHUNKS:
            flying["routed", step - 1] = (step, exchange(live.pop(("sent", step - 1))))
        j = step - 5
        if 0 <= j < CHUNKS:
            here = stack_call([live.pop((k, j)) for k in ("gated", "by_y", "by_x", "by_both")])
            flying["here", j] = (step, here)
            flying["there", j] = (step + 1, lax.ppermute(here, "core", SWAP))
        j = step - 4
        if 0 <= j < CHUNKS:
            flying["by_both", j] = (step, lax.ppermute(live["by_x", j], "y", SWAP))
        j = step - 3
        if 0 <= j < CHUNKS:
            flying["by_x", j] = (step, lax.ppermute(live["gated", j], "fx", SWAP))
            flying["by_y", j] = (step, lax.ppermute(live["gated", j], "y", SWAP))
        j = step - 2
        if 0 <= j < CHUNKS:
            routed = live.pop(("routed", j))
            before = lax.ppermute(routed[tok_rows - ROWS :, cols:], CTX, next_ctx)
            gated = medium_call(routed, before, live["medium"], live["same"], j, group_size)
            flying["gated", j] = (step, gated)
        if step < CHUNKS:
            sent = short_call(
                order, live["prior"], blocks, halo, taps_full, live["mask"], step
            )
            flying["sent", step] = (step, sent)
    fence(last + 1)
    live.update({k: v for k, (_, v) in flying.items()})

    place = jnp.arange(2 * ctx_count, dtype=jnp.int32)
    dest = x_at * ctx_count + ctx_at
    dest = dest ^ ((place & 4) // 4 + (place & 2) * 2 + (place & 1) * 2)
    side = x_at.reshape(1)
    here = [live["here", j] for j in range(CHUNKS)]
    there = [live["there", j] for j in range(CHUNKS)]
    parts = []
    unit = half // QUARTERS
    for first, wide in PROJECTS:
        panels = []
        for kind in ("keep", "got"):
            for key in [k for k in live if isinstance(k, tuple) and len(k) == 3 and k[0] != "part"]:
                if key[0] == kind and key[1] <= first < key[1] + key[2]:
                    panels.append((live[key], (first - key[1]) * unit))
        if parts:
            here[0] = after(here[0], product)
        product = project_call(side, dest, here, there, panels, unit * wide, out_weight.shape[0])
        given = product.reshape(-1, tok_rows, product.shape[1])
        if parts:
            given = after(given, parts[-1])
        parts.append(lax.all_to_all(given, PLANE, split_axis=0, concat_axis=0, tiled=True))
    return place_call(parts, ctx_count)


def solution(mesh):
    count, ctx_count = mesh.devices.shape
    fine = Mesh(mesh.devices.reshape(count // 2, 2, ctx_count // 2, 2), EVERY)
    placed = (
        P(EVERY, None),
        P(EVERY, None),
        P(FSDP, None),
        P(),
        P(),
        P(FSDP, CTX),
    )
    return jax.shard_map(
        on_device, mesh=fine, in_specs=placed, out_specs=P(EVERY, None), check_vma=False
    )
```

profile of v0, /device:TPU:0, one launch (start us, length us, event | category | flops | bytes accessed | tf_op | source)
XLA Modules:
  0.0 420.0 jit_solution(18270545394327127664)
XLA Ops:
  6.5 1.8 slice.119
  8.3 1.3 reshape.123
  9.6 6.0 %collective-permute-start = (bf16[48,12288]{1,0:T(8,128)(2,1)}, bf16[48,12288]{1,0:T(8,128)(2,1)}, u32[]{:S(2)}, u32[]{:S(2)}) collective-permute-start(bf16[48,12288]{1,0:T(8,128)(2,1)} %reshape.123), channel_id=1, source_target_pairs={{0,4},{1,5},{2,6},{3,7},{4,8},{5,9},{6,10},{7,11},{8,12},{9,13},{1... | collective-permute-start | bytes 3538952 | tf_op jit(solution)/shard_map/ppermute | solution.py:251
  16.4 3.8 all-to-all-start
  20.4 3.9 collective-permute-start.1
  25.2 2.3 constant_dynamic-slice_fusion.2
  27.5 1.1 constant_dynamic-slice_fusion.1
  28.6 0.8 broadcast_in_dim.24
  29.4 2.5 reshape.125.fq.fk.fv
  32.2 0.8 pad.6.taps
  33.0 7.1 %collective-permute-done = bf16[48,12288]{1,0:T(8,128)(2,1)} collective-permute-done((bf16[48,12288]{1,0:T(8,128)(2,1)}, bf16[48,12288]{1,0:T(8,128)(2,1)}, u32[]{:S(2)}, u32[]{:S(2)}) %collective-permute-start) | collective-permute-done | bytes 1179680 | tf_op jit(solution)/shard_map/ppermute | solution.py:251
  40.2 2.4 reshape.124.hq.hk.hv
  42.6 1.6 all-to-all-done
  45.5 7.8 %short_conv.4 = bf16[8,32,2048]{2,1,0:T(8,128)(2,1)} custom-call(s32[8]{0:T(128)} %copy-done.17, s32[8]{0:T(128)} %copy-done.18, bf16[8,32,12288]{2,1,0:T(8,128)(2,1)} %bitcast.56, bf16[8,32,12288]{2,1,0:T(8,128)(2,1)} %bitcast.57, bf16[8,32,12288]{2,1,0:T(8,128)(2,1)} %bitcast.58, bf16[8,6,12288]{2,1,0:T(8,128)(2,1)} %reshape.124.hq.hk.hv, ...), custom_call_target="tpu_custom_call" | custom-call | flops 1 | bytes 1 | tf_op jit(solution)/shard_map/short_conv/pallas_call | solution.py:64
  53.4 5.3 %all-to-all-start.1 = ((bf16[8,32,2048]{2,1,0:T(8,128)(2,1)}), bf16[8,32,2048]{2,1,0:T(8,128)(2,1)S(1)}, u32[]{:S(2)}, u32[]{:S(2)}) async-start(bf16[8,32,2048]{2,1,0:T(8,128)(2,1)} %short_conv.4), calls=%async_computation.1 | async-start | bytes 2097152 | tf_op jit(solution)/shard_map/all_to_all | solution.py:281
  59.4 7.9 %short_conv.5 = bf16[8,32,2048]{2,1,0:T(8,128)(2,1)} custom-call(s32[8]{0:T(128)} %copy-done.17, s32[8]{0:T(128)} %copy-done.18, bf16[8,32,12288]{2,1,0:T(8,128)(2,1)} %bitcast.59, bf16[8,32,12288]{2,1,0:T(8,128)(2,1)} %bitcast.60, bf16[8,32,12288]{2,1,0:T(8,128)(2,1)} %bitcast.61, bf16[8,6,12288]{2,1,0:T(8,128)(2,1)} %reshape.124.hq.hk.hv, ...), custom_call_target="tpu_custom_call" | custom-call | flops 1 | bytes 1 | tf_op jit(solution)/shard_map/short_conv/pallas_call | solution.py:64
  67.3 33.0 %all-to-all-done.1 = bf16[8,32,2048]{2,1,0:T(8,128)(2,1)S(1)} async-done(((bf16[8,32,2048]{2,1,0:T(8,128)(2,1)}), bf16[8,32,2048]{2,1,0:T(8,128)(2,1)S(1)}, u32[]{:S(2)}, u32[]{:S(2)}) %all-to-all-start.1) | async-done | bytes 1048608 | tf_op jit(solution)/shard_map/all_to_all | solution.py:281
  100.3 6.0 %all-to-all-start.2 = ((bf16[8,32,2048]{2,1,0:T(8,128)(2,1)}), bf16[8,32,2048]{2,1,0:T(8,128)(2,1)S(1)}, u32[]{:S(2)}, u32[]{:S(2)}) async-start(bf16[8,32,2048]{2,1,0:T(8,128)(2,1)} %short_conv.5), calls=%async_computation.2 | async-start | bytes 2097152 | tf_op jit(solution)/shard_map/all_to_all | solution.py:281
  106.4 2.0 collective-permute-start.2
  108.4 1.3 collective-permute-start.3
  109.7 7.8 %short_conv.6 = bf16[8,32,2048]{2,1,0:T(8,128)(2,1)} custom-call(s32[8]{0:T(128)} %copy-done.17, s32[8]{0:T(128)} %copy-done.18, bf16[8,32,12288]{2,1,0:T(8,128)(2,1)} %bitcast.62, bf16[8,32,12288]{2,1,0:T(8,128)(2,1)} %bitcast.63, bf16[8,32,12288]{2,1,0:T(8,128)(2,1)} %bitcast.64, bf16[8,6,12288]{2,1,0:T(8,128)(2,1)} %reshape.124.hq.hk.hv, ...), custom_call_target="tpu_custom_call" | custom-call | flops 1 | bytes 1 | tf_op jit(solution)/shard_map/short_conv/pallas_call | solution.py:64
  118.3 7.1 %medium_conv.4.refs_0_ = bf16[256,1024]{1,0:T(8,128)(2,1)} custom-call(bf16[256,2048]{1,0:T(8,128)(2,1)} %bitcast.78, bf16[256,2048]{1,0:T(8,128)(2,1)} %bitcast.79, bf16[128,1024]{1,0:T(8,128)(2,1)} %copy-done.12, f32[256,256]{1,0:T(8,128)} %pad.6.taps, bf16[2,128,256]{2,1,0:T(8,128)(2,1)} %add_convert_fusion.same), custom_call_target="tpu_custom_call" | custom-call | flops 1 | bytes 1 | tf_op jit(solution)/shard_map/medium_conv/pallas_call | solution.py:105
  125.3 17.4 %collective-permute-done.2 = bf16[512,1024]{1,0:T(8,128)(2,1)} collective-permute-done((bf16[512,1024]{1,0:T(8,128)(2,1)}, bf16[512,1024]{1,0:T(8,128)(2,1)}, u32[]{:S(2)}, u32[]{:S(2)}) %collective-permute-start.2) | collective-permute-done | bytes 1048608 | tf_op jit(solution)/shard_map/ppermute | solution.py:326
  142.8 4.6 %all-to-all-start.3 = ((bf16[8,32,2048]{2,1,0:T(8,128)(2,1)}), bf16[8,32,2048]{2,1,0:T(8,128)(2,1)S(1)}, u32[]{:S(2)}, u32[]{:S(2)}) async-start(bf16[8,32,2048]{2,1,0:T(8,128)(2,1)} %short_conv.6), calls=%async_computation.3 | async-start | bytes 2097152 | tf_op jit(solution)/shard_map/all_to_all | solution.py:281
  147.3 2.0 collective-permute-start.4
  149.4 1.3 collective-permute-start.6
  150.7 7.9 %short_conv.7 = bf16[8,32,2048]{2,1,0:T(8,128)(2,1)} custom-call(s32[8]{0:T(128)} %copy-done.17, s32[8]{0:T(128)} %copy-done.18, bf16[8,32,12288]{2,1,0:T(8,128)(2,1)} %bitcast.65, bf16[8,32,12288]{2,1,0:T(8,128)(2,1)} %bitcast.66, bf16[8,32,12288]{2,1,0:T(8,128)(2,1)} %bitcast.67, bf16[8,6,12288]{2,1,0:T(8,128)(2,1)} %reshape.124.hq.hk.hv, ...), custom_call_target="tpu_custom_call" | custom-call | flops 1 | bytes 1 | tf_op jit(solution)/shard_map/short_conv/pallas_call | solution.py:64
  158.6 2.3 fusion.12
  161.5 7.1 %medium_conv.5.refs_0_ = bf16[256,1024]{1,0:T(8,128)(2,1)} custom-call(bf16[256,2048]{1,0:T(8,128)(2,1)} %bitcast.72, bf16[256,2048]{1,0:T(8,128)(2,1)} %bitcast.73, bf16[128,1024]{1,0:T(8,128)(2,1)} %copy-done.10, f32[256,256]{1,0:T(8,128)} %pad.6.taps, bf16[2,128,256]{2,1,0:T(8,128)(2,1)} %add_convert_fusion.same), custom_call_target="tpu_custom_call" | custom-call | flops 1 | bytes 1 | tf_op jit(solution)/shard_map/medium_conv/pallas_call | solution.py:105
  169.3 29.4 %all-to-all-done.3 = bf16[8,32,2048]{2,1,0:T(8,128)(2,1)S(1)} async-done(((bf16[8,32,2048]{2,1,0:T(8,128)(2,1)}), bf16[8,32,2048]{2,1,0:T(8,128)(2,1)S(1)}, u32[]{:S(2)}, u32[]{:S(2)}) %all-to-all-start.3) | async-done | bytes 1048608 | tf_op jit(solution)/shard_map/all_to_all | solution.py:281
  198.7 4.5 %all-to-all-start.4 = ((bf16[8,32,2048]{2,1,0:T(8,128)(2,1)}), bf16[8,32,2048]{2,1,0:T(8,128)(2,1)S(1)}, u32[]{:S(2)}, u32[]{:S(2)}) async-start(bf16[8,32,2048]{2,1,0:T(8,128)(2,1)} %short_conv.7), calls=%async_computation.4 | async-start | bytes 2097152 | tf_op jit(solution)/shard_map/all_to_all | solution.py:281
  204.0 2.1 collective-permute-start.8
  206.1 1.9 collective-permute-start.9
  208.1 1.3 collective-permute-start.10
  209.4 1.1 collective-permute-done.10.halo
  211.2 7.0 %medium_conv.6.refs_0_ = bf16[256,1024]{1,0:T(8,128)(2,1)} custom-call(bf16[256,2048]{1,0:T(8,128)(2,1)} %bitcast.69, bf16[256,2048]{1,0:T(8,128)(2,1)} %bitcast.70, bf16[128,1024]{1,0:T(8,128)(2,1)} %copy-done.13, f32[256,256]{1,0:T(8,128)} %pad.6.taps, bf16[2,128,256]{2,1,0:T(8,128)(2,1)} %add_convert_fusion.same), custom_call_target="tpu_custom_call" | custom-call | flops 1 | bytes 1 | tf_op jit(solution)/shard_map/medium_conv/pallas_call | solution.py:105
  218.3 0.9 collective-permute-done.7.refs_3_
  219.2 9.0 %collective-permute-done.8.refs_2_ = bf16[256,1024]{1,0:T(8,128)(2,1)} collective-permute-done((bf16[256,1024]{1,0:T(8,128)(2,1)S(1)}, bf16[256,1024]{1,0:T(8,128)(2,1)}, u32[]{:S(2)}, u32[]{:S(2)}) %collective-permute-start.8) | collective-permute-done | bytes 524320 | tf_op jit(solution)/shard_map/ppermute | solution.py:339
  228.2 0.9 collective-permute-done.9.refs_1_
  229.0 9.3 %all-to-all-done.4 = bf16[8,32,2048]{2,1,0:T(8,128)(2,1)S(1)} async-done(((bf16[8,32,2048]{2,1,0:T(8,128)(2,1)}), bf16[8,32,2048]{2,1,0:T(8,128)(2,1)S(1)}, u32[]{:S(2)}, u32[]{:S(2)}) %all-to-all-start.4) | async-done | bytes 1048608 | tf_op jit(solution)/shard_map/all_to_all | solution.py:281
  238.4 1.5 collective-permute-start.15
  239.9 1.7 collective-permute-start.13
  241.6 0.7 copy-done.11
  242.3 7.1 %medium_conv.7.refs_0_ = bf16[256,1024]{1,0:T(8,128)(2,1)} custom-call(bf16[256,2048]{1,0:T(8,128)(2,1)} %bitcast.75, bf16[256,2048]{1,0:T(8,128)(2,1)} %bitcast.76, bf16[128,1024]{1,0:T(8,128)(2,1)} %copy-done.11, f32[256,256]{1,0:T(8,128)} %pad.6.taps, bf16[2,128,256]{2,1,0:T(8,128)(2,1)} %add_convert_fusion.same), custom_call_target="tpu_custom_call" | custom-call | flops 1 | bytes 1 | tf_op jit(solution)/shard_map/medium_conv/pallas_call | solution.py:105
  249.4 0.9 collective-permute-start.17
  250.3 7.0 %collective-permute-start.11 = (bf16[256,1024]{1,0:T(8,128)(2,1)}, bf16[256,1024]{1,0:T(8,128)(2,1)}, u32[]{:S(2)}, u32[]{:S(2)}) collective-permute-start(bf16[256,1024]{1,0:T(8,128)(2,1)} %collective-permute-done.8.refs_2_), channel_id=1, source_target_pairs={{0,2},{2,0},{1,3},{3,1},{4,6},{6,4},{5,7},{7,5},{8,10},{10,8},{9,1... | collective-permute-start | bytes 1572872 | tf_op jit(solution)/shard_map/ppermute | solution.py:336
  257.3 2.0 collective-permute-start.14
  259.4 5.3 %collective-permute-done.17.refs_2_ = bf16[256,1024]{1,0:T(8,128)(2,1)S(1)} collective-permute-done((bf16[256,1024]{1,0:T(8,128)(2,1)}, bf16[256,1024]{1,0:T(8,128)(2,1)S(1)}, u32[]{:S(2)}, u32[]{:S(2)}) %collective-permute-start.17) | collective-permute-done | bytes 524320 | tf_op jit(solution)/shard_map/ppermute | solution.py:339
  265.3 3.8 stack.79.refs_0_.refs_1_
  269.2 1.3 collective-permute-done.11.refs_3_
  270.5 3.9 stack.80.refs_2_.refs_3_
  274.4 7.2 %collective-permute-done.12.refs_1_ = bf16[256,1024]{1,0:T(8,128)(2,1)} collective-permute-done((bf16[256,1024]{1,0:T(8,128)(2,1)S(1)}, bf16[256,1024]{1,0:T(8,128)(2,1)}, u32[]{:S(2)}, u32[]{:S(2)}) %collective-permute-start.12) | collective-permute-done | bytes 524320 | tf_op jit(solution)/shard_map/ppermute | solution.py:340
  281.7 11.2 %collective-permute-done.14.refs_3_ = bf16[256,1024]{1,0:T(8,128)(2,1)} collective-permute-done((bf16[256,1024]{1,0:T(8,128)(2,1)}, bf16[256,1024]{1,0:T(8,128)(2,1)}, u32[]{:S(2)}, u32[]{:S(2)}) %collective-permute-start.14) | collective-permute-done | bytes 524320 | tf_op jit(solution)/shard_map/ppermute | solution.py:336
  292.9 3.9 stack.81.refs_4_.refs_5_
  296.8 7.3 %collective-permute-done.16.refs_1_ = bf16[256,1024]{1,0:T(8,128)(2,1)} collective-permute-done((bf16[256,1024]{1,0:T(8,128)(2,1)}, bf16[256,1024]{1,0:T(8,128)(2,1)}, u32[]{:S(2)}, u32[]{:S(2)}) %collective-permute-start.16) | collective-permute-done | bytes 524320 | tf_op jit(solution)/shard_map/ppermute | solution.py:340
  304.1 9.6 %collective-permute-done.18.refs_3_ = bf16[256,1024]{1,0:T(8,128)(2,1)} collective-permute-done((bf16[256,1024]{1,0:T(8,128)(2,1)S(1)}, bf16[256,1024]{1,0:T(8,128)(2,1)}, u32[]{:S(2)}, u32[]{:S(2)}) %collective-permute-start.18) | collective-permute-done | bytes 524320 | tf_op jit(solution)/shard_map/ppermute | solution.py:336
  313.7 4.0 stack.82.refs_6_.refs_7_
  318.3 3.9 collective-permute-done.22.refs_14_.refs_15_
  322.2 17.9 %project.2 = bf16[2048,512]{1,0:T(8,128)(2,1)} custom-call(s32[1]{0:T(128)} %bitcast.side, s32[8]{0:T(128)} %fusion.11.dest, bf16[1024,1024]{1,0:T(8,128)(2,1)} %stack.79.refs_0_.refs_1_, bf16[1024,1024]{1,0:T(8,128)(2,1)} %stack.79.refs_0_.refs_1_, bf16[1024,1024]{1,0:T(8,128)(2,1)} %stack.80.refs_2_.refs_3_, bf16[1024,1024]{1,0:T(8,128)(2,1)} %stack.80.refs_2_.refs_3_, ...), custom_call_target="tpu_custom_call" | custom-call | flops 1 | bytes 1 | tf_op jit(solution)/shard_map/project/pallas_call | solution.py:154
  340.0 3.6 all-to-all-start.5
  343.7 19.3 %all-gather.11.cloned.1.call-done.refs_17_ = bf16[2048,512]{1,0:T(8,128)(2,1)} async-done(((bf16[512,512]{1,0:T(8,128)(2,1)}), bf16[2048,512]{1,0:T(8,128)(2,1)}) %all-gather.11.cloned.1.call-update) | async-done | bytes 2097168 | tf_op jit(solution)/shard_map/all_gather | solution.py:306
  363.0 17.4 %project.3 = bf16[2048,512]{1,0:T(8,128)(2,1)} custom-call(s32[1]{0:T(128)} %bitcast.side, s32[8]{0:T(128)} %fusion.11.dest, bf16[1024,1024]{1,0:T(8,128)(2,1)} %stack.79.refs_0_.refs_1_, bf16[1024,1024]{1,0:T(8,128)(2,1)} %stack.79.refs_0_.refs_1_, bf16[1024,1024]{1,0:T(8,128)(2,1)} %stack.80.refs_2_.refs_3_, bf16[1024,1024]{1,0:T(8,128)(2,1)} %stack.80.refs_2_.refs_3_, ...), custom_call_target="tpu_custom_call" | custom-call | flops 1 | bytes 1 | tf_op jit(solution)/shard_map/project/pallas_call | solution.py:154
  380.3 29.7 %all_to_all.42.refs_1_ = bf16[8,256,512]{2,1,0:T(8,128)(2,1)S(1)} all-to-all(bf16[8,256,512]{2,1,0:T(8,128)(2,1)} %bitcast.81), channel_id=1, replica_groups=mesh['fh'=4,'fx'=2,'y'=2,'core'=2] {'fx','y','core'}, dimensions={0} | all-to-all | bytes 4194304 | tf_op jit(solution)/shard_map/all_to_all | solution.py:375
  410.0 3.5 place.1
  (96 shorter events, 9.3 us)
Async XLA Ops:
  8.3 7.3 %copy-start.16 = (s32[1,1024]{1,0:T(1,128)S(1)}, s32[1,1024]{1,0:T(1,128)}, u32[]{:S(2)}) copy-start(s32[1,1024]{1,0:T(1,128)} %param.8) | copy-start | bytes 12292
  8.3 12.0 %copy-start.19 = (s32[1,8]{1,0:T(1,128)S(1)}, s32[1,8]{1,0:T(1,128)}, u32[]{:S(2)}) copy-start(s32[1,8]{1,0:T(1,128)} %param.7) | copy-start | bytes 100
  9.6 17.9 %copy-start.5 = (bf16[512,2048]{1,0:T(8,128)(2,1)S(1)}, bf16[512,2048]{1,0:T(8,128)(2,1)}, u32[]{:S(2)}) copy-start(bf16[512,2048]{1,0:T(8,128)(2,1)} %param.11) | copy-start | bytes 6291460
  9.6 30.5 %collective-permute-start = (bf16[48,12288]{1,0:T(8,128)(2,1)}, bf16[48,12288]{1,0:T(8,128)(2,1)}, u32[]{:S(2)}, u32[]{:S(2)}) collective-permute-start(bf16[48,12288]{1,0:T(8,128)(2,1)} %reshape.123), channel_id=1, source_target_pairs={{0,4},{1,5},{2,6},{3,7},{4,8},{5,9},{6,10},{7,11},{8,12},{9,13},{1... | collective-permute-start | bytes 3538952 | tf_op jit(solution)/shard_map/ppermute | solution.py:251
  16.4 27.8 %all-to-all-start = ((s32[8,1,38]{2,1,0:T(1,128)}), s32[8,1,38]{2,1,0:T(1,128)S(1)}, u32[]{:S(2)}, u32[]{:S(2)}) async-start(s32[8,1,38]{2,1,0:T(1,128)} %bitcast.13), calls=%async_computation | async-start | bytes 8192 | tf_op jit(solution)/shard_map/all_to_all | solution.py:256
  20.4 8.2 %copy-start.17 = (s32[8]{0:T(128)}, s32[8]{0:T(128)S(1)}, u32[]{:S(2)}) copy-start(s32[8]{0:T(128)S(1)} %select_reduce_fusion.order) | copy-start | bytes 100
  20.4 22.2 %collective-permute-start.1 = (s32[8]{0:T(128)S(1)}, s32[8]{0:T(128)S(1)}, u32[]{:S(2)}, u32[]{:S(2)}) collective-permute-start(s32[8]{0:T(128)S(1)} %select_reduce_fusion.order), channel_id=1, source_target_pairs={{0,4},{1,5},{2,6},{3,7},{4,8},{5,9},{6,10},{7,11},{8,12},{9,13},{1... | collective-permute-start | bytes 104 | tf_op jit(solution)/shard_map/ppermute | solution.py:248
  25.2 3.4 copy-start.15
  29.4 2.5 copy-start.14
  42.6 2.9 copy-start.18
  53.4 46.9 %all-to-all-start.1 = ((bf16[8,32,2048]{2,1,0:T(8,128)(2,1)}), bf16[8,32,2048]{2,1,0:T(8,128)(2,1)S(1)}, u32[]{:S(2)}, u32[]{:S(2)}) async-start(bf16[8,32,2048]{2,1,0:T(8,128)(2,1)} %short_conv.4), calls=%async_computation.1 | async-start | bytes 2097152 | tf_op jit(solution)/shard_map/all_to_all | solution.py:281
  58.7 84.1 %all-gather.5.cloned.1.call-start = ((), (), s32[]{:S(2)}) async-start(), calls=%async_computation.7 | async-start | bytes 2621440 | tf_op jit(solution)/shard_map/all_gather | solution.py:306
  100.3 17.2 %copy-start.4 = (bf16[8,32,2048]{2,1,0:T(8,128)(2,1)}, bf16[8,32,2048]{2,1,0:T(8,128)(2,1)S(1)}, u32[]{:S(2)}) copy-start(bf16[8,32,2048]{2,1,0:T(8,128)(2,1)S(1)} %all-to-all-done.1) | copy-start | bytes 3145732
  100.3 42.4 %all-to-all-start.2 = ((bf16[8,32,2048]{2,1,0:T(8,128)(2,1)}), bf16[8,32,2048]{2,1,0:T(8,128)(2,1)S(1)}, u32[]{:S(2)}, u32[]{:S(2)}) async-start(bf16[8,32,2048]{2,1,0:T(8,128)(2,1)} %short_conv.5), calls=%async_computation.2 | async-start | bytes 2097152 | tf_op jit(solution)/shard_map/all_to_all | solution.py:281
  106.3 122.7 %all-gather.7.cloned.1.call-start = ((), (), s32[]{:S(2)}) async-start(), calls=%async_computation.8 | async-start | bytes 2621440 | tf_op jit(solution)/shard_map/all_gather | solution.py:306
  106.4 36.4 %collective-permute-start.2 = (bf16[512,1024]{1,0:T(8,128)(2,1)}, bf16[512,1024]{1,0:T(8,128)(2,1)}, u32[]{:S(2)}, u32[]{:S(2)}) collective-permute-start(bf16[512,1024]{1,0:T(8,128)(2,1)} %constant_dynamic-slice_fusion.1), channel_id=1, source_target_pairs={{0,4},{4,0},{1,5},{5,1},{2,6},{6,2},{3,7},{7,3},{8,12},{12,8},{9,1... | collective-permute-start | bytes 3145736 | tf_op jit(solution)/shard_map/ppermute | solution.py:326
  108.4 9.2 %collective-permute-start.3 = (bf16[128,1024]{1,0:T(8,128)(2,1)S(1)}, bf16[128,1024]{1,0:T(8,128)(2,1)S(1)}, u32[]{:S(2)}, u32[]{:S(2)}) collective-permute-start(bf16[128,1024]{1,0:T(8,128)(2,1)S(1)} %slice.113), channel_id=1, source_target_pairs={{0,1},{1,2},{2,3},{4,5},{5,6},{6,7},{8,9},{9,10},{10,11},{12,13},{... | collective-permute-start | bytes 786440 | tf_op jit(solution)/shard_map/ppermute | solution.py:344
  117.5 0.7 copy-start.12
  125.3 22.0 %copy-start.6 = (bf16[256,1024]{1,0:T(8,128)(2,1)S(1)}, bf16[256,1024]{1,0:T(8,128)(2,1)}, u32[]{:S(2)}) copy-start(bf16[256,1024]{1,0:T(8,128)(2,1)} %medium_conv.4.refs_0_) | copy-start | bytes 1572868
  142.7 15.8 %copy-start.2 = (bf16[8,32,2048]{2,1,0:T(8,128)(2,1)}, bf16[8,32,2048]{2,1,0:T(8,128)(2,1)S(1)}, u32[]{:S(2)}) copy-start(bf16[8,32,2048]{2,1,0:T(8,128)(2,1)S(1)} %all-to-all-done.2) | copy-start | bytes 3145732
  142.8 55.9 %all-to-all-start.3 = ((bf16[8,32,2048]{2,1,0:T(8,128)(2,1)}), bf16[8,32,2048]{2,1,0:T(8,128)(2,1)S(1)}, u32[]{:S(2)}, u32[]{:S(2)}) async-start(bf16[8,32,2048]{2,1,0:T(8,128)(2,1)} %short_conv.6), calls=%async_computation.3 | async-start | bytes 2097152 | tf_op jit(solution)/shard_map/all_to_all | solution.py:281
  147.3 21.9 %collective-permute-start.4 = (bf16[256,1024]{1,0:T(8,128)(2,1)S(1)}, bf16[256,1024]{1,0:T(8,128)(2,1)}, u32[]{:S(2)}, u32[]{:S(2)}) collective-permute-start(bf16[256,1024]{1,0:T(8,128)(2,1)S(1)} %copy-done.6), channel_id=1, source_target_pairs={{0,4},{4,0},{1,5},{5,1},{2,6},{6,2},{3,7},{7,3},{8,12},{12,8},{9,1... | collective-permute-start | bytes 1572872 | tf_op jit(solution)/shard_map/ppermute | solution.py:339
  149.4 19.9 %collective-permute-start.5 = (bf16[256,1024]{1,0:T(8,128)(2,1)S(1)}, bf16[256,1024]{1,0:T(8,128)(2,1)}, u32[]{:S(2)}, u32[]{:S(2)}) collective-permute-start(bf16[256,1024]{1,0:T(8,128)(2,1)S(1)} %copy-done.6), channel_id=1, source_target_pairs={{0,2},{2,0},{1,3},{3,1},{4,6},{6,4},{5,7},{7,5},{8,10},{10,8},{9,1... | collective-permute-start | bytes 1572872 | tf_op jit(solution)/shard_map/ppermute | solution.py:340
  149.4 11.4 %collective-permute-start.6 = (bf16[128,1024]{1,0:T(8,128)(2,1)S(1)}, bf16[128,1024]{1,0:T(8,128)(2,1)S(1)}, u32[]{:S(2)}, u32[]{:S(2)}) collective-permute-start(bf16[128,1024]{1,0:T(8,128)(2,1)S(1)} %slice.116), channel_id=1, source_target_pairs={{0,1},{1,2},{2,3},{4,5},{5,6},{6,7},{8,9},{9,10},{10,11},{12,13},{... | collective-permute-start | bytes 786440 | tf_op jit(solution)/shard_map/ppermute | solution.py:344
  160.8 0.7 copy-start.10
  168.6 35.4 %copy-start.7 = (bf16[256,1024]{1,0:T(8,128)(2,1)S(1)}, bf16[256,1024]{1,0:T(8,128)(2,1)}, u32[]{:S(2)}) copy-start(bf16[256,1024]{1,0:T(8,128)(2,1)} %medium_conv.5.refs_0_) | copy-start | bytes 1572868
  198.7 11.8 %copy-start.1 = (bf16[8,32,2048]{2,1,0:T(8,128)(2,1)}, bf16[8,32,2048]{2,1,0:T(8,128)(2,1)S(1)}, u32[]{:S(2)}) copy-start(bf16[8,32,2048]{2,1,0:T(8,128)(2,1)S(1)} %all-to-all-done.3) | copy-start | bytes 3145732
  198.7 39.6 %all-to-all-start.4 = ((bf16[8,32,2048]{2,1,0:T(8,128)(2,1)}), bf16[8,32,2048]{2,1,0:T(8,128)(2,1)S(1)}, u32[]{:S(2)}, u32[]{:S(2)}) async-start(bf16[8,32,2048]{2,1,0:T(8,128)(2,1)} %short_conv.7), calls=%async_computation.4 | async-start | bytes 2097152 | tf_op jit(solution)/shard_map/all_to_all | solution.py:281
  203.2 115.1 %all-gather.9.cloned.1.call-start = ((), (), s32[]{:S(2)}) async-start(), calls=%async_computation.9 | async-start | bytes 2621440 | tf_op jit(solution)/shard_map/all_gather | solution.py:306
  203.9 159.1 %all-gather.11.cloned.1.call-start = ((), (), s32[]{:S(2)}) async-start(), calls=%async_computation.10 | async-start | bytes 2621440 | tf_op jit(solution)/shard_map/all_gather | solution.py:306
  203.9 15.2 %collective-permute-start.7 = (bf16[256,1024]{1,0:T(8,128)(2,1)}, bf16[256,1024]{1,0:T(8,128)(2,1)}, u32[]{:S(2)}, u32[]{:S(2)}) collective-permute-start(bf16[256,1024]{1,0:T(8,128)(2,1)} %collective-permute-done.4.refs_2_), channel_id=1, source_target_pairs={{0,2},{2,0},{1,3},{3,1},{4,6},{6,4},{5,7},{7,5},{8,10},{10,8},{9,1... | collective-permute-start | bytes 1572872 | tf_op jit(solution)/shard_map/ppermute | solution.py:336
  204.0 24.2 %collective-permute-start.8 = (bf16[256,1024]{1,0:T(8,128)(2,1)S(1)}, bf16[256,1024]{1,0:T(8,128)(2,1)}, u32[]{:S(2)}, u32[]{:S(2)}) collective-permute-start(bf16[256,1024]{1,0:T(8,128)(2,1)S(1)} %copy-done.7), channel_id=1, source_target_pairs={{0,4},{4,0},{1,5},{5,1},{2,6},{6,2},{3,7},{7,3},{8,12},{12,8},{9,1... | collective-permute-start | bytes 1572872 | tf_op jit(solution)/shard_map/ppermute | solution.py:339
  206.1 22.9 %collective-permute-start.9 = (bf16[256,1024]{1,0:T(8,128)(2,1)S(1)}, bf16[256,1024]{1,0:T(8,128)(2,1)}, u32[]{:S(2)}, u32[]{:S(2)}) collective-permute-start(bf16[256,1024]{1,0:T(8,128)(2,1)S(1)} %copy-done.7), channel_id=1, source_target_pairs={{0,2},{2,0},{1,3},{3,1},{4,6},{6,4},{5,7},{7,5},{8,10},{10,8},{9,1... | collective-permute-start | bytes 1572872 | tf_op jit(solution)/shard_map/ppermute | solution.py:340
  208.1 2.4 collective-permute-start.10
  210.5 0.7 copy-start.13
  218.3 39.0 %copy-start.8 = (bf16[256,1024]{1,0:T(8,128)(2,1)S(1)}, bf16[256,1024]{1,0:T(8,128)(2,1)}, u32[]{:S(2)}) copy-start(bf16[256,1024]{1,0:T(8,128)(2,1)} %medium_conv.6.refs_0_) | copy-start | bytes 1572868
  238.3 3.2 copy-start.3
  238.4 3.2 collective-permute-start.15
  239.9 17.4 %collective-permute-start.13 = (bf16[256,1024]{1,0:T(8,128)(2,1)}, bf16[256,1024]{1,0:T(8,128)(2,1)}, u32[]{:S(2)}, u32[]{:S(2)}) collective-permute-start(bf16[256,1024]{1,0:T(8,128)(2,1)} %medium_conv.6.refs_0_), channel_id=1, source_target_pairs={{0,4},{4,0},{1,5},{5,1},{2,6},{6,2},{3,7},{7,3},{8,12},{12,8},{9,1... | collective-permute-start | bytes 1572872 | tf_op jit(solution)/shard_map/ppermute | solution.py:339
  241.6 0.7 copy-start.11
  249.4 15.3 %collective-permute-start.17 = (bf16[256,1024]{1,0:T(8,128)(2,1)}, bf16[256,1024]{1,0:T(8,128)(2,1)S(1)}, u32[]{:S(2)}, u32[]{:S(2)}) collective-permute-start(bf16[256,1024]{1,0:T(8,128)(2,1)} %medium_conv.7.refs_0_), channel_id=1, source_target_pairs={{0,4},{4,0},{1,5},{5,1},{2,6},{6,2},{3,7},{7,3},{8,12},{12,8},{9,1... | collective-permute-start | bytes 1572872 | tf_op jit(solution)/shard_map/ppermute | solution.py:339
  250.3 20.1 %collective-permute-start.11 = (bf16[256,1024]{1,0:T(8,128)(2,1)}, bf16[256,1024]{1,0:T(8,128)(2,1)}, u32[]{:S(2)}, u32[]{:S(2)}) collective-permute-start(bf16[256,1024]{1,0:T(8,128)(2,1)} %collective-permute-done.8.refs_2_), channel_id=1, source_target_pairs={{0,2},{2,0},{1,3},{3,1},{4,6},{6,4},{5,7},{7,5},{8,10},{10,8},{9,1... | collective-permute-start | bytes 1572872 | tf_op jit(solution)/shard_map/ppermute | solution.py:336
  257.3 24.4 %collective-permute-start.12 = (bf16[256,1024]{1,0:T(8,128)(2,1)S(1)}, bf16[256,1024]{1,0:T(8,128)(2,1)}, u32[]{:S(2)}, u32[]{:S(2)}) collective-permute-start(bf16[256,1024]{1,0:T(8,128)(2,1)S(1)} %copy-done.8), channel_id=1, source_target_pairs={{0,2},{2,0},{1,3},{3,1},{4,6},{6,4},{5,7},{7,5},{8,10},{10,8},{9,1... | collective-permute-start | bytes 1572872 | tf_op jit(solution)/shard_map/ppermute | solution.py:340
  257.3 35.6 %collective-permute-start.14 = (bf16[256,1024]{1,0:T(8,128)(2,1)}, bf16[256,1024]{1,0:T(8,128)(2,1)}, u32[]{:S(2)}, u32[]{:S(2)}) collective-permute-start(bf16[256,1024]{1,0:T(8,128)(2,1)} %collective-permute-done.13.refs_2_), channel_id=1, source_target_pairs={{0,2},{2,0},{1,3},{3,1},{4,6},{6,4},{5,7},{7,5},{8,10},{10,8},{9,1... | collective-permute-start | bytes 1572872 | tf_op jit(solution)/shard_map/ppermute | solution.py:336
  259.3 44.8 %collective-permute-start.16 = (bf16[256,1024]{1,0:T(8,128)(2,1)}, bf16[256,1024]{1,0:T(8,128)(2,1)}, u32[]{:S(2)}, u32[]{:S(2)}) collective-permute-start(bf16[256,1024]{1,0:T(8,128)(2,1)} %medium_conv.7.refs_0_), channel_id=1, source_target_pairs={{0,2},{2,0},{1,3},{3,1},{4,6},{6,4},{5,7},{7,5},{8,10},{10,8},{9,1... | collective-permute-start | bytes 1572872 | tf_op jit(solution)/shard_map/ppermute | solution.py:340
  264.7 4.5 %copy-start.9 = (bf16[256,1024]{1,0:T(8,128)(2,1)}, bf16[256,1024]{1,0:T(8,128)(2,1)S(1)}, u32[]{:S(2)}) copy-start(bf16[256,1024]{1,0:T(8,128)(2,1)S(1)} %collective-permute-done.17.refs_2_) | copy-start | bytes 1572868
  264.7 49.0 %collective-permute-start.18 = (bf16[256,1024]{1,0:T(8,128)(2,1)S(1)}, bf16[256,1024]{1,0:T(8,128)(2,1)}, u32[]{:S(2)}, u32[]{:S(2)}) collective-permute-start(bf16[256,1024]{1,0:T(8,128)(2,1)S(1)} %collective-permute-done.17.refs_2_), channel_id=1, source_target_pairs={{0,2},{2,0},{1,3},{3,1},{4,6},{6,4},{5,7},{7,5},{8,10},{10,8},{9,1... | collective-permute-start | bytes 1572872 | tf_op jit(solution)/shard_map/ppermute | solution.py:336
  270.4 47.8 %collective-permute-start.19 = (bf16[1024,1024]{1,0:T(8,128)(2,1)}, bf16[1024,1024]{1,0:T(8,128)(2,1)S(1)}, u32[]{:S(2)}, u32[]{:S(2)}) collective-permute-start(bf16[1024,1024]{1,0:T(8,128)(2,1)} %stack.79.refs_0_.refs_1_), channel_id=1, source_target_pairs={{0,1},{1,0},{2,3},{3,2},{4,5},{5,4},{6,7},{7,6},{8,9},{9,8},{10,11... | collective-permute-start | bytes 6291464 | tf_op jit(solution)/shard_map/ppermute | solution.py:333
  281.6 36.6 %collective-permute-start.20 = (bf16[1024,1024]{1,0:T(8,128)(2,1)}, bf16[1024,1024]{1,0:T(8,128)(2,1)}, u32[]{:S(2)}, u32[]{:S(2)}) collective-permute-start(bf16[1024,1024]{1,0:T(8,128)(2,1)} %stack.80.refs_2_.refs_3_), channel_id=1, source_target_pairs={{0,1},{1,0},{2,3},{3,2},{4,5},{5,4},{6,7},{7,6},{8,9},{9,8},{10,11... | collective-permute-start | bytes 6291464 | tf_op jit(solution)/shard_map/ppermute | solution.py:333
  296.8 21.4 %collective-permute-start.21 = (bf16[1024,1024]{1,0:T(8,128)(2,1)}, bf16[1024,1024]{1,0:T(8,128)(2,1)}, u32[]{:S(2)}, u32[]{:S(2)}) collective-permute-start(bf16[1024,1024]{1,0:T(8,128)(2,1)} %stack.81.refs_4_.refs_5_), channel_id=1, source_target_pairs={{0,1},{1,0},{2,3},{3,2},{4,5},{5,4},{6,7},{7,6},{8,9},{9,8},{10,11... | collective-permute-start | bytes 6291464 | tf_op jit(solution)/shard_map/ppermute | solution.py:333
  317.7 4.5 %collective-permute-start.22 = (bf16[1024,1024]{1,0:T(8,128)(2,1)}, bf16[1024,1024]{1,0:T(8,128)(2,1)}, u32[]{:S(2)}, u32[]{:S(2)}) collective-permute-start(bf16[1024,1024]{1,0:T(8,128)(2,1)} %stack.82.refs_6_.refs_7_), channel_id=1, source_target_pairs={{0,1},{1,0},{2,3},{3,2},{4,5},{5,4},{6,7},{7,6},{8,9},{9,8},{10,11... | collective-permute-start | bytes 6291464 | tf_op jit(solution)/shard_map/ppermute | solution.py:333
  318.3 3.9 copy-start
  340.0 40.3 %all-to-all-start.5 = ((bf16[8,256,512]{2,1,0:T(8,128)(2,1)}), bf16[8,256,512]{2,1,0:T(8,128)(2,1)S(1)}, u32[]{:S(2)}, u32[]{:S(2)}) async-start(bf16[8,256,512]{2,1,0:T(8,128)(2,1)} %bitcast.80), calls=%async_computation.5 | async-start | bytes 4194304 | tf_op jit(solution)/shard_map/all_to_all | solution.py:375
Sparse Core Ops, SparseCore 0:
  61.1 75.8 all-gather.4
  142.9 64.4 all-gather.6
  208.9 54.8 all-gather.8
  317.8 45.0 all-gather.10
where the time goes:
time: 424 us; the launch traced here: 420 us
  waiting for transfers between devices  177 us (42%)
  Pallas kernels  114 us (27%)
  starting transfers between devices  63.8 us (15%)
  blocking collectives  29.7 us (7%)
  local copies, waits for them, and re-layouts  19.5 us (5%)
  between operations  13.4 us (3%)
    all_to_all x4, waiting for transfers between devices, exchange(): routed = lax.all_to_all(sent, FSDP, split_axis=0, concat_axis=0, tiled=True)  71.8 us
    pallas_call x2, Pallas kernels, project_call(): pl.pallas_call(functools.partial(project_kernel, dest.shape[0]), grid_spe...  35.2 us
    pallas_call x4, Pallas kernels, short_call(): pl.pallas_call(short_kernel, grid_spec=pltpu.PrefetchScalarGridSpec(num_s...  31.4 us
    all_to_all x1, blocking collectives, on_device(): lax.all_to_all(given, PLANE, split_axis=0, concat_axis=0, tiled=True)  29.7 us
    pallas_call x4, Pallas kernels, medium_call(): pl.pallas_call(functools.partial(medium_kernel, group_size), grid=(steps,...  28.2 us
    ppermute x4, waiting for transfers between devices, on_device(): flying['by_both', j] = (step, lax.ppermute(live['by_x', j], 'y', SWAP))  23 us
    all_to_all x4, starting transfers between devices, exchange(): routed = lax.all_to_all(sent, FSDP, split_axis=0, concat_axis=0, tiled=True)  20.4 us
    all_gather x4, waiting for transfers between devices, start_panels(): lax.all_gather(source, 'fh', axis=0, tiled=True)  19.3 us
  transfers between devices with their start and end apart: 33, of which 19 were waited for; matrix products, arithmetic and copies ran while one was open for 4% of the time, Pallas kernels for 24%

commit v1 on v0

--- a/solution.py
+++ b/solution.py
@@ -15,8 +15,14 @@
 SWAP = [(0, 1), (1, 0)]
 CHUNKS = 4
 QUARTERS = 4
-PANEL_STEPS = (("keep", 0, 2, 1, 3), ("keep", 2, 2, 3, 5), ("got", 0, 2, 4, 6), ("got", 2, 2, 5, 9))
+PANEL_STEPS = (
+    ("keep", 0, 2, 0, 2),
+    ("got", 0, 2, 3, 5),
+    ("both", 2, 2, 5, 20),
+)
 FENCED = 5
+VIA_X = 3
+NEAR_EARLY = (0, 1, 2)
 PROJECTS = ((0, 2), (2, 2))
 ROWS = 128
 LANES = 128
@@ -55,7 +61,7 @@
         return pl.BlockSpec((1, rows, cols), lambda g, o, p: (o[g], 0, part * CHUNKS + chunk))
 
     def of_halo(part):
-        return pl.BlockSpec((1, halo.shape[1], cols), lambda g, o, p: (p[g], 0, part * CHUNKS + chunk))
+        return pl.BlockSpec((1, halo.shape[1], cols), lambda g, o, p: (p[g], 0, part * (CHUNKS // 2) + chunk % (CHUNKS // 2)))
 
     def of_taps(part):
         return pl.BlockSpec((taps_full.shape[0], cols), lambda g, o, p: (0, part * CHUNKS + chunk))
@@ -119,27 +125,31 @@
     )(routed, routed, halo, taps, same)
 
 
-def project_kernel(count, side, dest, *refs):
-    pieces, panels, out = refs[:-3], refs[-3:-1], refs[-1]
+def project_kernel(count, full, side, dest, *refs):
+    pieces, panels, sums, out = refs[:count], refs[count : count + 2], refs[count + 2 : -1], refs[-1]
     held, depth = pieces[0].shape
-    tile = out.shape[0] // count
+    tile = out.shape[0] // dest.shape[0]
     for half in range(2):
-        given = pieces[half * len(pieces) // 2 : (half + 1) * len(pieces) // 2]
-        total = None
-        for m, piece in enumerate(given):
+        rows = slice(half * held, (half + 1) * held)
+        total = sums[0][rows] if sums else None
+        for m, piece in enumerate(pieces[half * count // 2 : (half + 1) * count // 2]):
             i, other = m // 2, m % 2
-            rows = panels[other][i * depth : (i + 1) * depth]
-            term = jnp.dot(piece[...], rows, preferred_element_type=jnp.float32)
+            term = jnp.dot(piece[...], panels[other][i], preferred_element_type=jnp.float32)
             total = term if total is None else total + term
+        if not full:
+            out[rows] = total
+            continue
         total = total.astype(jnp.bfloat16)
         for m in range(held // tile):
             at = pl.multiple_of(dest[half * held // tile + m] * tile, tile)
             out[pl.ds(at, tile)] = total[m * tile : (m + 1) * tile]
 
 
-def project_call(side, dest, here, there, panels, cols, depth):
+def project_call(side, dest, here, there, panels, cols, depth, first, sums):
     held, wide = here[0].shape
     tile = min(256, cols)
+    rows = len(here) * wide // 2 // depth
+    full = first + len(here) == CHUNKS
 
     def specs():
         for i in range(wide // (2 * depth)):
@@ -150,24 +160,29 @@
                     pipeline_mode=pl.Buffered(1),
                 )
 
-    given = [x for x in list(here) + list(there) for _ in range(wide // depth)]
+    at_rows = first * wide // 2 // depth // rows
+    pieces = [x for x in list(here) + list(there) for _ in range(wide // depth)]
+    given = [] if sums is None else [sums]
     return pl.pallas_call(
-        functools.partial(project_kernel, dest.shape[0]),
+        functools.partial(project_kernel, len(pieces), full),
         grid_spec=pltpu.PrefetchScalarGridSpec(
             num_scalar_prefetch=2,
             grid=(cols // tile,),
             in_specs=[spec for _ in list(here) + list(there) for spec in specs()]
             + [
-                pl.BlockSpec((p.shape[0], tile), lambda n, s, d, at=at // tile: (0, at + n))
-                for p, at in panels
-            ],
+                pl.BlockSpec(
+                    (rows, depth, tile), lambda n, s, d, row=row, at=at // tile: (at_rows, row, at + n)
+                )
+                for _, row, at in panels
+            ]
+            + [pl.BlockSpec((2 * held, tile), lambda n, s, d: (0, n)) for _ in given],
             out_specs=pl.BlockSpec((2 * held, tile), lambda n, s, d: (0, n)),
         ),
-        out_shape=jax.ShapeDtypeStruct((2 * held, cols), jnp.bfloat16),
+        out_shape=jax.ShapeDtypeStruct((2 * held, cols), jnp.bfloat16 if full else jnp.float32),
         compiler_params=pltpu.CompilerParams(vmem_limit_bytes=56 * MIB),
         cost_estimate=LIGHT,
         name="project",
-    )(side, dest, *given, *(p for p, _ in panels))
+    )(side, dest, *pieces, *(p for p, _, _ in panels), *given)
 
 
 def stack_kernel(*refs):
@@ -243,23 +258,34 @@
             elif c + 1 < ctx_count:
                 shift.append((f * ctx_count + c, c + 1))
 
+    onward = [(i - ctx_count, o) for i, o in shift if i // ctx_count % 2 == 1]
+
+    live, flying = {}, {}
+
     seqs = jnp.arange(count, dtype=jnp.int32)
     order = jnp.sum(jnp.where(route[0][None, :] == seqs[:, None], seqs[None, :], 0), axis=1)
-    order_prev = lax.ppermute(order, EVERY, shift)
     blocks = loaded.reshape(count, blk, wide)
-    tail = blocks[:, blk - depth :].reshape(count * depth, wide)
-    halo = lax.ppermute(tail, EVERY, shift).reshape(count, depth, wide)
+    tails = []
+    for i in range(2):
+        parts = [
+            blocks[:, blk - depth :, at : at + channels // 2]
+            for at in range(i * channels // 2, wide, channels)
+        ]
+        tails.append(jnp.concatenate(parts, axis=2).reshape(count * depth, wide // 2))
+    direct = lax.ppermute(tails[0], EVERY, shift).reshape(count, depth, wide // 2)
+
     own_ids = jnp.concatenate([jnp.full((depth,), -1, jnp.int32), doc_ids[0]])
     own_ids = lax.dynamic_slice_in_dim(own_ids, ctx_at * tok_rows, depth + tok_rows, 0)
     near = jnp.stack([own_ids[f * blk : (f + 1) * blk + depth] for f in range(count)])
-    near = after(near, tail)
+    order_prev = lax.ppermute(after(order, tails[0]), EVERY, shift)
+    near = after(near, tails[0])
     near = lax.all_to_all(near, FSDP, split_axis=0, concat_axis=0, tiled=True)
 
 
     taps_full = jnp.repeat(short_filter, group_size, axis=1)
 
     half = out_weight.shape[1] // 2
-    keep = lax.dynamic_slice_in_dim(out_weight, x_at * half, half, 1)
+    keep = lax.dynamic_slice_in_dim(after(out_weight, tails[0]), x_at * half, half, 1)
     give = lax.dynamic_slice_in_dim(out_weight, (1 - x_at) * half, half, 1)
 
     reach = ROWS - medium_len
@@ -281,14 +307,9 @@
         routed = lax.all_to_all(sent, FSDP, split_axis=0, concat_axis=0, tiled=True)
         return routed.reshape(tok_rows, 2 * cols)
 
-    live, flying = {}, {}
-    def cut_panels(kind, value):
-        for k, first, wide, _, _ in PANEL_STEPS:
-            if k == kind:
-                at = half // QUARTERS * first
-                live["part", kind, first] = value[:, at : at + half // QUARTERS * wide]
-
-    cut_panels("keep", keep)
+    def cut(kind, first, wide):
+        at = half // QUARTERS * first
+        return live[kind][:, at : at + half // QUARTERS * wide]
 
     def fence(step):
         for key in [k for k, (due, _) in flying.items() if due <= step]:
@@ -302,40 +323,66 @@
     def start_panels(step):
         for kind, first, wide, begin, due in PANEL_STEPS:
             if begin == step:
-                source = live.pop(("part", kind, first))
-                flying[kind, first, wide] = (due, lax.all_gather(source, "fh", axis=0, tiled=True))
-
+                kinds = ("keep", "got") if kind == "both" else (kind,)
+                part = jnp.concatenate([cut(k, first, wide) for k in kinds], axis=0)
+                flying[kind, first, wide] = (due, lax.all_gather(part[None], "fh", axis=0, tiled=True))
+
+    live["keep"] = keep
     start_panels(0)
-    halo, near, order_prev = lax.optimization_barrier((halo, near, order_prev))
+    direct, near, order_prev = lax.optimization_barrier((direct, near, order_prev))
     mask = jnp.stack(
         [near[:, depth - i : depth - i + blk] == near[:, depth:] for i in range(short_len)], axis=-1
     ).astype(jnp.float32)
     live["give"] = give
-    live["sent", 0] = short_call(order, order_prev, blocks, halo, taps_full, mask, 0)
+    turned = lax.ppermute(after(tails[1], tails[0]), "fx", SWAP)
+    passed = lax.ppermute(turned, EVERY, onward)
+    flying["halo"] = (2, jnp.where(x_at == 1, turned, passed).reshape(count, depth, wide // 2))
+    live["sent", 0] = short_call(order, order_prev, blocks, direct, taps_full, mask, 0)
     live["mask"] = mask
     live["prior"] = order_prev
     live["medium"] = medium_rows
     live["same"] = same
+    place = jnp.arange(2 * ctx_count, dtype=jnp.int32)
+    dest = x_at * ctx_count + ctx_at
+    dest = dest ^ ((place & 4) // 4 + (place & 2) * 2 + (place & 1) * 2)
+    side = x_at.reshape(1)
+    unit = half // QUARTERS
+
+    def project(low, high, first, wide, sums=None):
+        held = {**live, **{k: v for k, (_, v) in flying.items()}}
+        panels = []
+        for other, kind in enumerate(("keep", "got")):
+            for key in [k for k in held if isinstance(k, tuple) and len(k) == 3 and k[0] in (kind, "both")]:
+                if key[1] <= first < key[1] + key[2]:
+                    row = other if key[0] == "both" else 0
+                    panels.append((held[key], row, (first - key[1]) * unit))
+        here, there = ([held[k, j] for j in range(low, high)] for k in ("here", "there"))
+        depth = out_weight.shape[0]
+        return project_call(side, dest, here, there, panels, unit * wide, depth, low, sums)
+
+    newest = []
+
+    def stack_steps(step, j):
+        if FENCED <= step and j < CHUNKS - 1:
+            live["gated", j] = after(live["gated", j], live["by_x", CHUNKS - 1])
+        here = stack_call([live.pop((k, j)) for k in ("gated", "by_y", "by_x", "by_both")])
+        flying["here", j] = (step, here)
+        flying["there", j] = (step + 1, lax.ppermute(here, "core", SWAP))
+
     last = CHUNKS + 4
     for step in range(1, last + 1):
-        if "got" in live:
-            cut_panels("got", live.pop("got"))
         fence(step)
         start_panels(step)
         if step == 1:
-            flying["got"] = (3, lax.ppermute(live.pop("give"), "fx", SWAP))
+            flying["got"] = (2, lax.ppermute(live.pop("give"), "fx", SWAP))
         if step <= CHUNKS:
             flying["routed", step - 1] = (step, exchange(live.pop(("sent", step - 1))))
-        j = step - 5
-        if 0 <= j < CHUNKS:
-            here = stack_call([live.pop((k, j)) for k in ("gated", "by_y", "by_x", "by_both")])
-            flying["here", j] = (step, here)
-            flying["there", j] = (step + 1, lax.ppermute(here, "core", SWAP))
-        j = step - 4
-        if 0 <= j < CHUNKS:
-            flying["by_both", j] = (step, lax.ppermute(live["by_x", j], "y", SWAP))
+        for j in [j for j in range(CHUNKS) if step == j + 4 - (j in NEAR_EARLY)]:
+            first, second = ("by_x", "y") if j < VIA_X else ("by_y", "fx")
+            flying["by_both", j] = (step, lax.ppermute(live[first, j], second, SWAP))
         j = step - 3
-        if 0 <= j < CHUNKS:
+        if 0 <= j < CHUNKS and j not in NEAR_EARLY:
+            live["gated", j] = after(live["gated", j], live["by_both", j - 1])
             flying["by_x", j] = (step, lax.ppermute(live["gated", j], "fx", SWAP))
             flying["by_y", j] = (step, lax.ppermute(live["gated", j], "y", SWAP))
         j = step - 2
@@ -344,31 +391,24 @@
             before = lax.ppermute(routed[tok_rows - ROWS :, cols:], CTX, next_ctx)
             gated = medium_call(routed, before, live["medium"], live["same"], j, group_size)
             flying["gated", j] = (step, gated)
+            newest.append(gated)
+            if j in NEAR_EARLY:
+                flying["by_x", j] = (step, lax.ppermute(gated, "fx", SWAP))
+                flying["by_y", j] = (step, lax.ppermute(gated, "y", SWAP))
+        for j in [j for j in range(CHUNKS) if step == (4, 7, 7, 8)[j]]:
+            stack_steps(step, j)
         if step < CHUNKS:
-            sent = short_call(
-                order, live["prior"], blocks, halo, taps_full, live["mask"], step
-            )
+            halo = direct if step < CHUNKS // 2 else live["halo"]
+            sent = short_call(order, live["prior"], blocks, halo, taps_full, live["mask"], step)
             flying["sent", step] = (step, sent)
     fence(last + 1)
     live.update({k: v for k, (_, v) in flying.items()})
 
-    place = jnp.arange(2 * ctx_count, dtype=jnp.int32)
-    dest = x_at * ctx_count + ctx_at
-    dest = dest ^ ((place & 4) // 4 + (place & 2) * 2 + (place & 1) * 2)
-    side = x_at.reshape(1)
-    here = [live["here", j] for j in range(CHUNKS)]
-    there = [live["there", j] for j in range(CHUNKS)]
-    parts = []
-    unit = half // QUARTERS
-    for first, wide in PROJECTS:
-        panels = []
-        for kind in ("keep", "got"):
-            for key in [k for k in live if isinstance(k, tuple) and len(k) == 3 and k[0] != "part"]:
-                if key[0] == kind and key[1] <= first < key[1] + key[2]:
-                    panels.append((live[key], (first - key[1]) * unit))
-        if parts:
-            here[0] = after(here[0], product)
-        product = project_call(side, dest, here, there, panels, unit * wide, out_weight.shape[0])
+    parts, product = [], None
+    for n, (first, wide) in enumerate(PROJECTS):
+        if n > 0:
+            live["here", 0] = after(live["here", 0], product)
+        product = project(0, CHUNKS, first, wide)
         given = product.reshape(-1, tok_rows, product.shape[1])
         if parts:
             given = after(given, parts[-1])

time: 424 us -> 382 us (0.901)
  waiting for transfers between devices: 177 us -> 99.8 us
  starting transfers between devices: 63.8 us -> 87.3 us
  local copies, waits for them, and re-layouts: 19.5 us -> 27.7 us
    all_to_all x4, waiting for transfers between devices: 71.8 us -> 20.6 us  [exchange(): routed = lax.all_to_all(sent, FSDP, split_axis=0, concat_axis=0, tiled=True)]
    ppermute x11 -> x19, starting transfers between devices: 21.7 us -> 41.5 us  [the longest x3 19.2 us: on_device(): flying['by_y', j] = (step, lax.ppermute(gated, 'y', SWAP))]
    all_gather x4 -> x3, waiting for transfers between devices: 19.3 us -> 0.02 us  [start_panels(): lax.all_gather(part[None], 'fh', axis=0, tiled=True)]
    ppermute x4 -> x1, waiting for transfers between devices: 15 us -> 0.07 us  [on_device(): flying['by_x', j] = (step, lax.ppermute(live['gated', j], 'fx', SWAP))]
    ppermute x4 -> x1, starting transfers between devices: 2.04 us -> 10.9 us  [on_device(): flying['by_y', j] = (step, lax.ppermute(live['gated', j], 'y', SWAP))]
    all_to_all x1, waiting for transfers between devices: 0.01 us -> 8.2 us  [on_device(): lax.all_to_all(given, PLANE, split_axis=0, concat_axis=0, tiled=True)]
    ppermute x4 -> x1, starting transfers between devices: 6.7 us -> 0.01 us  [on_device(): flying['by_x', j] = (step, lax.ppermute(live['gated', j], 'fx', SWAP))]
    ppermute x11 -> x19, waiting for transfers between devices: 51.4 us -> 55.7 us  [the longest x1 21 us: on_device(): flying['got'] = (2, lax.ppermute(live.pop('give'), 'fx', SWAP))]
  transfers between devices with their start and end apart: 33 -> 34, of which waited for: 19 -> 19; matrix products, arithmetic and copies ran while one was open for 4% -> 6% of each run, Pallas kernels for 24% -> 29%
where the time goes in v1:
time: 382 us; the launch traced here: 378 us
  Pallas kernels  114 us (30%)
  waiting for transfers between devices  99.8 us (26%)
  starting transfers between devices  87.3 us (23%)
  blocking collectives  29.6 us (8%)
  local copies, waits for them, and re-layouts  27.7 us (7%)
  between operations  13.5 us (4%)
  other arithmetic  6.12 us (2%)
    pallas_call x2, Pallas kernels, project_call(): pl.pallas_call(functools.partial(project_kernel, len(pieces), full), grid...  34.8 us
    pallas_call x4, Pallas kernels, short_call(): pl.pallas_call(short_kernel, grid_spec=pltpu.PrefetchScalarGridSpec(num_s...  31.3 us
    all_to_all x1, blocking collectives, on_device(): lax.all_to_all(given, PLANE, split_axis=0, concat_axis=0, tiled=True)  29.6 us
    pallas_call x4, Pallas kernels, medium_call(): pl.pallas_call(functools.partial(medium_kernel, group_size), grid=(steps,...  28.2 us
    ppermute x1, waiting for transfers between devices, on_device(): flying['got'] = (2, lax.ppermute(live.pop('give'), 'fx', SWAP))  21 us
    all_to_all x4, waiting for transfers between devices, exchange(): routed = lax.all_to_all(sent, FSDP, split_axis=0, concat_axis=0, tiled=True)  20.6 us
    ppermute x3, starting transfers between devices, on_device(): flying['by_y', j] = (step, lax.ppermute(gated, 'y', SWAP))  19.2 us
    all_to_all x4, starting transfers between devices, exchange(): routed = lax.all_to_all(sent, FSDP, split_axis=0, concat_axis=0, tiled=True)  18.8 us
  transfers between devices with their start and end apart: 34, of which 19 were waited for; matrix products, arithmetic and copies ran while one was open for 6% of the time, Pallas kernels for 29%

profile of v1, /device:TPU:0, one launch (start us, length us, event | category | flops | bytes accessed | tf_op | source)
XLA Modules:
  0.0 378.1 jit_solution(13107178079227507994)
XLA Ops:
  6.5 2.6 fusion.12
  10.3 5.7 %collective-permute-start = (bf16[48,6144]{1,0:T(8,128)(2,1)}, bf16[48,6144]{1,0:T(8,128)(2,1)}, u32[]{:S(2)}, u32[]{:S(2)}) collective-permute-start(bf16[48,6144]{1,0:T(8,128)(2,1)} %reshape.129), channel_id=1, source_target_pairs={{0,4},{1,5},{2,6},{3,7},{4,8},{5,9},{6,10},{7,11},{8,12},{9,13},{1... | collective-permute-start | bytes 1769480 | tf_op jit(solution)/shard_map/ppermute | solution.py:275
  16.7 4.1 %all-to-all-start = ((s32[8,1,38]{2,1,0:T(1,128)}), s32[8,1,38]{2,1,0:T(1,128)S(1)}, u32[]{:S(2)}, u32[]{:S(2)}) async-start(s32[8,1,38]{2,1,0:T(1,128)} %bitcast.13), calls=%async_computation | async-start | bytes 8192 | tf_op jit(solution)/shard_map/all_to_all | solution.py:282
  21.0 3.9 %collective-permute-start.1 = (s32[8]{0:T(128)S(1)}, s32[8]{0:T(128)S(1)}, u32[]{:S(2)}, u32[]{:S(2)}) collective-permute-start(s32[8]{0:T(128)S(1)} %select_reduce_fusion.order), channel_id=1, source_target_pairs={{0,4},{1,5},{2,6},{3,7},{4,8},{5,9},{6,10},{7,11},{8,12},{9,13},{1... | collective-permute-start | bytes 104 | tf_op jit(solution)/shard_map/ppermute | solution.py:280
  25.8 1.1 pad_maximum_fusion.2
  26.9 1.1 reshape.132
  28.0 1.5 collective-permute-start.2
  30.3 1.1 constant_dynamic-slice_fusion.2
  32.5 2.0 broadcast_in_dim.33
  34.4 4.4 %reshape.131.fq.fk.fv = f32[7,12288]{1,0:T(8,128)} reshape(f32[7,768,16]{2,1,0:T(8,128)} %broadcast_in_dim.33) | data formatting | bytes 688128 | tf_op jit(solution)/shard_map/reshape | solution.py:285
  39.9 2.2 reshape.130.hq.hk.hv
  42.1 3.2 collective-permute-done.2
  45.3 2.3 collective-permute-start.3
  49.0 7.8 %short_conv.4 = bf16[8,32,2048]{2,1,0:T(8,128)(2,1)} custom-call(s32[8]{0:T(128)} %copy-done.25, s32[8]{0:T(128)} %copy-done.26, bf16[8,32,12288]{2,1,0:T(8,128)(2,1)} %bitcast.59, bf16[8,32,12288]{2,1,0:T(8,128)(2,1)} %bitcast.60, bf16[8,32,12288]{2,1,0:T(8,128)(2,1)} %bitcast.61, bf16[8,6,6144]{2,1,0:T(8,128)(2,1)} %reshape.130.hq.hk.hv, ...), custom_call_target="tpu_custom_call" | custom-call | flops 1 | bytes 1 | tf_op jit(solution)/shard_map/short_conv/pallas_call | solution.py:70
  56.8 4.5 %all-to-all-start.1 = ((bf16[8,32,2048]{2,1,0:T(8,128)(2,1)}), bf16[8,32,2048]{2,1,0:T(8,128)(2,1)S(1)}, u32[]{:S(2)}, u32[]{:S(2)}) async-start(bf16[8,32,2048]{2,1,0:T(8,128)(2,1)} %short_conv.4), calls=%async_computation.1 | async-start | bytes 2097152 | tf_op jit(solution)/shard_map/all_to_all | solution.py:307
  61.3 2.0 collective-permute-start.4
  63.3 7.8 %short_conv.5 = bf16[8,32,2048]{2,1,0:T(8,128)(2,1)} custom-call(s32[8]{0:T(128)} %copy-done.25, s32[8]{0:T(128)} %copy-done.26, bf16[8,32,12288]{2,1,0:T(8,128)(2,1)} %bitcast.62, bf16[8,32,12288]{2,1,0:T(8,128)(2,1)} %bitcast.63, bf16[8,32,12288]{2,1,0:T(8,128)(2,1)} %bitcast.64, bf16[8,6,6144]{2,1,0:T(8,128)(2,1)} %reshape.130.hq.hk.hv, ...), custom_call_target="tpu_custom_call" | custom-call | flops 1 | bytes 1 | tf_op jit(solution)/shard_map/short_conv/pallas_call | solution.py:70
  71.1 2.3 collective-permute-done.3
  73.4 1.1 broadcast_select_fusion
  74.5 1.1 reshape.133.hq.hk.hv
  75.6 21.0 %collective-permute-done.4 = bf16[512,1024]{1,0:T(8,128)(2,1)S(1)} collective-permute-done((bf16[512,1024]{1,0:T(8,128)(2,1)}, bf16[512,1024]{1,0:T(8,128)(2,1)S(1)}, u32[]{:S(2)}, u32[]{:S(2)}) %collective-permute-start.4) | collective-permute-done | bytes 1048608 | tf_op jit(solution)/shard_map/ppermute | solution.py:377
  96.6 9.9 %all-to-all-done.1 = bf16[8,32,2048]{2,1,0:T(8,128)(2,1)S(1)} async-done(((bf16[8,32,2048]{2,1,0:T(8,128)(2,1)}), bf16[8,32,2048]{2,1,0:T(8,128)(2,1)S(1)}, u32[]{:S(2)}, u32[]{:S(2)}) %all-to-all-start.1) | async-done | bytes 1048608 | tf_op jit(solution)/shard_map/all_to_all | solution.py:307
  106.5 3.6 all-to-all-start.2
  110.1 1.8 collective-permute-start.5
  111.9 1.1 collective-permute-done.5.halo
  113.8 7.0 %medium_conv.4.refs_0_ = bf16[256,1024]{1,0:T(8,128)(2,1)} custom-call(bf16[256,2048]{1,0:T(8,128)(2,1)} %bitcast.80, bf16[256,2048]{1,0:T(8,128)(2,1)} %bitcast.81, bf16[128,1024]{1,0:T(8,128)(2,1)} %copy-done.21, f32[256,256]{1,0:T(8,128)} %pad.6.taps, bf16[2,128,256]{2,1,0:T(8,128)(2,1)} %add_convert_fusion.same), custom_call_target="tpu_custom_call" | custom-call | flops 1 | bytes 1 | tf_op jit(solution)/shard_map/medium_conv/pallas_call | solution.py:111
  120.8 1.6 collective-permute-start.6
  122.5 5.4 %collective-permute-start.7 = (bf16[256,1024]{1,0:T(8,128)(2,1)}, bf16[256,1024]{1,0:T(8,128)(2,1)S(1)}, u32[]{:S(2)}, u32[]{:S(2)}) collective-permute-start(bf16[256,1024]{1,0:T(8,128)(2,1)} %medium_conv.4.refs_0_), channel_id=1, source_target_pairs={{0,2},{2,0},{1,3},{3,1},{4,6},{6,4},{5,7},{7,5},{8,10},{10,8},{9,1... | collective-permute-start | bytes 1572872 | tf_op jit(solution)/shard_map/ppermute | solution.py:397
  127.8 7.8 %short_conv.6 = bf16[8,32,2048]{2,1,0:T(8,128)(2,1)} custom-call(s32[8]{0:T(128)} %copy-done.25, s32[8]{0:T(128)} %copy-done.26, bf16[8,32,12288]{2,1,0:T(8,128)(2,1)} %bitcast.65, bf16[8,32,12288]{2,1,0:T(8,128)(2,1)} %bitcast.66, bf16[8,32,12288]{2,1,0:T(8,128)(2,1)} %bitcast.67, bf16[8,6,6144]{2,1,0:T(8,128)(2,1)} %reshape.133.hq.hk.hv, ...), custom_call_target="tpu_custom_call" | custom-call | flops 1 | bytes 1 | tf_op jit(solution)/shard_map/short_conv/pallas_call | solution.py:70
  135.7 1.6 collective-permute-done.6.refs_2_
  137.3 1.9 collective-permute-done.7.refs_1_
  140.0 4.5 %all-to-all-start.3 = ((bf16[8,32,2048]{2,1,0:T(8,128)(2,1)}), bf16[8,32,2048]{2,1,0:T(8,128)(2,1)S(1)}, u32[]{:S(2)}, u32[]{:S(2)}) async-start(bf16[8,32,2048]{2,1,0:T(8,128)(2,1)} %short_conv.6), calls=%async_computation.3 | async-start | bytes 2097152 | tf_op jit(solution)/shard_map/all_to_all | solution.py:307
  145.6 1.9 collective-permute-start.9
  149.3 7.0 %medium_conv.5.refs_0_ = bf16[256,1024]{1,0:T(8,128)(2,1)} custom-call(bf16[256,2048]{1,0:T(8,128)(2,1)} %bitcast.77, bf16[256,2048]{1,0:T(8,128)(2,1)} %bitcast.78, bf16[128,1024]{1,0:T(8,128)(2,1)} %copy-done.18, f32[256,256]{1,0:T(8,128)} %pad.6.taps, bf16[2,128,256]{2,1,0:T(8,128)(2,1)} %add_convert_fusion.same), custom_call_target="tpu_custom_call" | custom-call | flops 1 | bytes 1 | tf_op jit(solution)/shard_map/medium_conv/pallas_call | solution.py:111
  156.3 1.7 collective-permute-start.10
  158.0 7.5 %collective-permute-start.11 = (bf16[256,1024]{1,0:T(8,128)(2,1)}, bf16[256,1024]{1,0:T(8,128)(2,1)S(1)}, u32[]{:S(2)}, u32[]{:S(2)}) collective-permute-start(bf16[256,1024]{1,0:T(8,128)(2,1)} %medium_conv.5.refs_0_), channel_id=1, source_target_pairs={{0,2},{2,0},{1,3},{3,1},{4,6},{6,4},{5,7},{7,5},{8,10},{10,8},{9,1... | collective-permute-start | bytes 1572872 | tf_op jit(solution)/shard_map/ppermute | solution.py:397
  165.5 7.8 %short_conv.7 = bf16[8,32,2048]{2,1,0:T(8,128)(2,1)} custom-call(s32[8]{0:T(128)} %copy-done.25, s32[8]{0:T(128)} %copy-done.26, bf16[8,32,12288]{2,1,0:T(8,128)(2,1)} %bitcast.68, bf16[8,32,12288]{2,1,0:T(8,128)(2,1)} %bitcast.69, bf16[8,32,12288]{2,1,0:T(8,128)(2,1)} %bitcast.70, bf16[8,6,6144]{2,1,0:T(8,128)(2,1)} %reshape.133.hq.hk.hv, ...), custom_call_target="tpu_custom_call" | custom-call | flops 1 | bytes 1 | tf_op jit(solution)/shard_map/short_conv/pallas_call | solution.py:70
  173.3 3.6 collective-permute-done.11.refs_1_
  176.9 10.7 %all-to-all-done.3 = bf16[8,32,2048]{2,1,0:T(8,128)(2,1)S(1)} async-done(((bf16[8,32,2048]{2,1,0:T(8,128)(2,1)}), bf16[8,32,2048]{2,1,0:T(8,128)(2,1)S(1)}, u32[]{:S(2)}, u32[]{:S(2)}) %all-to-all-start.3) | async-done | bytes 1048608 | tf_op jit(solution)/shard_map/all_to_all | solution.py:307
  187.7 4.2 %stack.79.refs_0_.refs_1_ = bf16[1024,1024]{1,0:T(8,128)(2,1)} custom-call(bf16[256,1024]{1,0:T(8,128)(2,1)} %medium_conv.4.refs_0_, bf16[256,1024]{1,0:T(8,128)(2,1)} %copy-done.13, bf16[256,1024]{1,0:T(8,128)(2,1)} %collective-permute-done.6.refs_2_, bf16[256,1024]{1,0:T(8,128)(2,1)} %copy-done.15), custom_call_target="tpu_custom_call" | custom-call | flops 1 | bytes 1 | tf_op jit(solution)/shard_map/stack/pallas_call | solution.py:198
  191.9 6.2 %all-to-all-start.4 = ((bf16[8,32,2048]{2,1,0:T(8,128)(2,1)}), bf16[8,32,2048]{2,1,0:T(8,128)(2,1)}, u32[]{:S(2)}, u32[]{:S(2)}) async-start(bf16[8,32,2048]{2,1,0:T(8,128)(2,1)} %short_conv.7), calls=%async_computation.4 | async-start | bytes 2097152 | tf_op jit(solution)/shard_map/all_to_all | solution.py:307
  198.2 2.3 collective-permute-start.13
  202.3 7.0 %medium_conv.6.refs_0_ = bf16[256,1024]{1,0:T(8,128)(2,1)} custom-call(bf16[256,2048]{1,0:T(8,128)(2,1)} %bitcast.74, bf16[256,2048]{1,0:T(8,128)(2,1)} %bitcast.75, bf16[128,1024]{1,0:T(8,128)(2,1)} %copy-done.19, f32[256,256]{1,0:T(8,128)} %pad.6.taps, bf16[2,128,256]{2,1,0:T(8,128)(2,1)} %add_convert_fusion.same), custom_call_target="tpu_custom_call" | custom-call | flops 1 | bytes 1 | tf_op jit(solution)/shard_map/medium_conv/pallas_call | solution.py:111
  209.4 2.3 collective-permute-start.14
  211.7 6.3 %collective-permute-start.15 = (bf16[256,1024]{1,0:T(8,128)(2,1)}, bf16[256,1024]{1,0:T(8,128)(2,1)}, u32[]{:S(2)}, u32[]{:S(2)}) collective-permute-start(bf16[256,1024]{1,0:T(8,128)(2,1)} %medium_conv.6.refs_0_), channel_id=1, source_target_pairs={{0,2},{2,0},{1,3},{3,1},{4,6},{6,4},{5,7},{7,5},{8,10},{10,8},{9,1... | collective-permute-start | bytes 1572872 | tf_op jit(solution)/shard_map/ppermute | solution.py:397
  218.0 12.6 %collective-permute-done.14.refs_2_ = bf16[256,1024]{1,0:T(8,128)(2,1)} collective-permute-done((bf16[256,1024]{1,0:T(8,128)(2,1)}, bf16[256,1024]{1,0:T(8,128)(2,1)}, u32[]{:S(2)}, u32[]{:S(2)}) %collective-permute-start.14) | collective-permute-done | bytes 524320 | tf_op jit(solution)/shard_map/ppermute | solution.py:396
  230.7 1.2 pad_maximum_fusion
  233.4 2.2 collective-permute-start.17
  237.3 7.1 %medium_conv.7.refs_0_ = bf16[256,1024]{1,0:T(8,128)(2,1)} custom-call(bf16[256,2048]{1,0:T(8,128)(2,1)} %bitcast.27.q.gate, bf16[256,2048]{1,0:T(8,128)(2,1)} %bitcast.27.q.gate, bf16[128,1024]{1,0:T(8,128)(2,1)} %copy-done.20, f32[256,256]{1,0:T(8,128)} %pad.6.taps, bf16[2,128,256]{2,1,0:T(8,128)(2,1)} %add_convert_fusion.same), custom_call_target="tpu_custom_call" | custom-call | flops 1 | bytes 1 | tf_op jit(solution)/shard_map/medium_conv/pallas_call | solution.py:111
  244.4 2.1 collective-permute-done.18.refs_3_
  246.6 10.9 %collective-permute-start.20 = (bf16[256,1024]{1,0:T(8,128)(2,1)}, bf16[256,1024]{1,0:T(8,128)(2,1)S(1)}, u32[]{:S(2)}, u32[]{:S(2)}) collective-permute-start(bf16[256,1024]{1,0:T(8,128)(2,1)} %medium_conv.7.refs_0_), channel_id=1, source_target_pairs={{0,2},{2,0},{1,3},{3,1},{4,6},{6,4},{5,7},{7,5},{8,10},{10,8},{9,1... | collective-permute-start | bytes 1572872 | tf_op jit(solution)/shard_map/ppermute | solution.py:387
  257.5 11.7 %collective-permute-done.20.refs_1_ = bf16[256,1024]{1,0:T(8,128)(2,1)S(1)} collective-permute-done((bf16[256,1024]{1,0:T(8,128)(2,1)}, bf16[256,1024]{1,0:T(8,128)(2,1)S(1)}, u32[]{:S(2)}, u32[]{:S(2)}) %collective-permute-start.20) | collective-permute-done | bytes 524320 | tf_op jit(solution)/shard_map/ppermute | solution.py:387
  270.1 3.9 %stack.80.refs_2_.refs_3_ = bf16[1024,1024]{1,0:T(8,128)(2,1)} custom-call(bf16[256,1024]{1,0:T(8,128)(2,1)} %medium_conv.5.refs_0_, bf16[256,1024]{1,0:T(8,128)(2,1)} %copy-done.12, bf16[256,1024]{1,0:T(8,128)(2,1)} %copy-done.11, bf16[256,1024]{1,0:T(8,128)(2,1)} %collective-permute-done.12.refs_3_), custom_call_target="tpu_custom_call" | custom-call | flops 1 | bytes 1 | tf_op jit(solution)/shard_map/stack/pallas_call | solution.py:198
  274.2 4.0 %stack.81.refs_4_.refs_5_ = bf16[1024,1024]{1,0:T(8,128)(2,1)} custom-call(bf16[256,1024]{1,0:T(8,128)(2,1)} %medium_conv.6.refs_0_, bf16[256,1024]{1,0:T(8,128)(2,1)} %collective-permute-done.15.refs_1_, bf16[256,1024]{1,0:T(8,128)(2,1)} %collective-permute-done.14.refs_2_, bf16[256,1024]{1,0:T(8,128)(2,1)} %copy-done.14), custom_call_target="tpu_custom_call" | custom-call | flops 1 | bytes 1 | tf_op jit(solution)/shard_map/stack/pallas_call | solution.py:198
  278.6 3.3 collective-permute-done.21.refs_3_
  282.0 4.0 %stack.82.refs_6_.refs_7_ = bf16[1024,1024]{1,0:T(8,128)(2,1)} custom-call(bf16[256,1024]{1,0:T(8,128)(2,1)} %medium_conv.7.refs_0_, bf16[256,1024]{1,0:T(8,128)(2,1)} %copy-done.16, bf16[256,1024]{1,0:T(8,128)(2,1)} %copy-done.17, bf16[256,1024]{1,0:T(8,128)(2,1)} %collective-permute-done.21.refs_3_), custom_call_target="tpu_custom_call" | custom-call | flops 1 | bytes 1 | tf_op jit(solution)/shard_map/stack/pallas_call | solution.py:198
  286.5 3.9 %collective-permute-done.24.refs_14_.refs_15_ = bf16[1024,1024]{1,0:T(8,128)(2,1)} collective-permute-done((bf16[1024,1024]{1,0:T(8,128)(2,1)}, bf16[1024,1024]{1,0:T(8,128)(2,1)}, u32[]{:S(2)}, u32[]{:S(2)}) %collective-permute-start.24) | collective-permute-done | bytes 2097184 | tf_op jit(solution)/shard_map/ppermute | solution.py:370
  290.4 17.4 %project.2 = bf16[2048,512]{1,0:T(8,128)(2,1)} custom-call(s32[1]{0:T(128)} %bitcast.side, s32[8]{0:T(128)} %fusion.11.dest, bf16[1024,1024]{1,0:T(8,128)(2,1)} %stack.79.refs_0_.refs_1_, bf16[1024,1024]{1,0:T(8,128)(2,1)} %stack.79.refs_0_.refs_1_, bf16[1024,1024]{1,0:T(8,128)(2,1)} %stack.80.refs_2_.refs_3_, bf16[1024,1024]{1,0:T(8,128)(2,1)} %stack.80.refs_2_.refs_3_, ...), custom_call_target="tpu_custom_call" | custom-call | flops 1 | bytes 1 | tf_op jit(solution)/shard_map/project/pallas_call | solution.py:166
  307.9 3.6 all-to-all-start.5
  311.5 17.4 %project.3 = bf16[2048,512]{1,0:T(8,128)(2,1)} custom-call(s32[1]{0:T(128)} %bitcast.side, s32[8]{0:T(128)} %fusion.11.dest, bf16[1024,1024]{1,0:T(8,128)(2,1)} %stack.79.refs_0_.refs_1_, bf16[1024,1024]{1,0:T(8,128)(2,1)} %stack.79.refs_0_.refs_1_, bf16[1024,1024]{1,0:T(8,128)(2,1)} %stack.80.refs_2_.refs_3_, bf16[1024,1024]{1,0:T(8,128)(2,1)} %stack.80.refs_2_.refs_3_, ...), custom_call_target="tpu_custom_call" | custom-call | flops 1 | bytes 1 | tf_op jit(solution)/shard_map/project/pallas_call | solution.py:166
  328.9 8.2 %all-to-all-done.5.refs_0_ = bf16[8,256,512]{2,1,0:T(8,128)(2,1)S(1)} async-done(((bf16[8,256,512]{2,1,0:T(8,128)(2,1)}), bf16[8,256,512]{2,1,0:T(8,128)(2,1)S(1)}, u32[]{:S(2)}, u32[]{:S(2)}) %all-to-all-start.5) | async-done | bytes 2097184 | tf_op jit(solution)/shard_map/all_to_all | solution.py:415
  337.1 1.3 copy-done.2
  338.4 29.6 %all_to_all.42.refs_1_ = bf16[8,256,512]{2,1,0:T(8,128)(2,1)S(1)} all-to-all(bf16[8,256,512]{2,1,0:T(8,128)(2,1)} %bitcast.83), channel_id=1, replica_groups=mesh['fh'=4,'fx'=2,'y'=2,'core'=2] {'fx','y','core'}, dimensions={0} | all-to-all | bytes 4194304 | tf_op jit(solution)/shard_map/all_to_all | solution.py:415
  368.1 3.5 place.1
  (124 shorter events, 19.0 us)
Async XLA Ops:
  6.5 18.3 %copy-start = (bf16[512,2048]{1,0:T(8,128)(2,1)S(1)}, bf16[512,2048]{1,0:T(8,128)(2,1)}, u32[]{:S(2)}) copy-start(bf16[512,2048]{1,0:T(8,128)(2,1)} %param.11) | copy-start | bytes 6291460
  9.1 6.8 %copy-start.24 = (s32[1,1024]{1,0:T(1,128)S(1)}, s32[1,1024]{1,0:T(1,128)}, u32[]{:S(2)}) copy-start(s32[1,1024]{1,0:T(1,128)} %param.8) | copy-start | bytes 12292
  9.1 11.7 %copy-start.27 = (s32[1,8]{1,0:T(1,128)S(1)}, s32[1,8]{1,0:T(1,128)}, u32[]{:S(2)}) copy-start(s32[1,8]{1,0:T(1,128)} %param.7) | copy-start | bytes 100
  10.3 29.7 %collective-permute-start = (bf16[48,6144]{1,0:T(8,128)(2,1)}, bf16[48,6144]{1,0:T(8,128)(2,1)}, u32[]{:S(2)}, u32[]{:S(2)}) collective-permute-start(bf16[48,6144]{1,0:T(8,128)(2,1)} %reshape.129), channel_id=1, source_target_pairs={{0,4},{1,5},{2,6},{3,7},{4,8},{5,9},{6,10},{7,11},{8,12},{9,13},{1... | collective-permute-start | bytes 1769480 | tf_op jit(solution)/shard_map/ppermute | solution.py:275
  16.7 25.4 %all-to-all-start = ((s32[8,1,38]{2,1,0:T(1,128)}), s32[8,1,38]{2,1,0:T(1,128)S(1)}, u32[]{:S(2)}, u32[]{:S(2)}) async-start(s32[8,1,38]{2,1,0:T(1,128)} %bitcast.13), calls=%async_computation | async-start | bytes 8192 | tf_op jit(solution)/shard_map/all_to_all | solution.py:282
  20.8 85.7 %all-gather.7.cloned.1.call-start = ((), (), s32[]{:S(2)}) async-start(), calls=%async_computation.7 | async-start | bytes 2621440 | tf_op jit(solution)/shard_map/all_gather | solution.py:328
  21.0 7.0 %copy-start.25 = (s32[8]{0:T(128)}, s32[8]{0:T(128)S(1)}, u32[]{:S(2)}) copy-start(s32[8]{0:T(128)S(1)} %select_reduce_fusion.order) | copy-start | bytes 100
  21.0 21.1 %collective-permute-start.1 = (s32[8]{0:T(128)S(1)}, s32[8]{0:T(128)S(1)}, u32[]{:S(2)}, u32[]{:S(2)}) collective-permute-start(s32[8]{0:T(128)S(1)} %select_reduce_fusion.order), channel_id=1, source_target_pairs={{0,4},{1,5},{2,6},{3,7},{4,8},{5,9},{6,10},{7,11},{8,12},{9,13},{1... | collective-permute-start | bytes 104 | tf_op jit(solution)/shard_map/ppermute | solution.py:280
  28.0 17.4 %collective-permute-start.2 = (bf16[48,6144]{1,0:T(8,128)(2,1)}, bf16[48,6144]{1,0:T(8,128)(2,1)}, u32[]{:S(2)}, u32[]{:S(2)}) collective-permute-start(bf16[48,6144]{1,0:T(8,128)(2,1)} %reshape.132), channel_id=1, source_target_pairs={{0,4},{4,0},{1,5},{5,1},{2,6},{6,2},{3,7},{7,3},{8,12},{12,8},{9,1... | collective-permute-start | bytes 1769480 | tf_op jit(solution)/shard_map/ppermute | solution.py:337
  30.3 2.2 copy-start.23
  34.4 4.4 %copy-start.22 = (bf16[128,256]{1,0:T(8,128)(2,1)S(1)}, bf16[128,256]{1,0:T(8,128)(2,1)}, u32[]{:S(2)}) copy-start(bf16[128,256]{1,0:T(8,128)(2,1)} %param.10) | copy-start | bytes 196612
  42.1 6.9 %copy-start.26 = (s32[8]{0:T(128)}, s32[8]{0:T(128)S(1)}, u32[]{:S(2)}) copy-start(s32[8]{0:T(128)S(1)} %collective-permute-done.1.order_prev) | copy-start | bytes 100
  45.3 28.0 %collective-permute-start.3 = (bf16[48,6144]{1,0:T(8,128)(2,1)}, bf16[48,6144]{1,0:T(8,128)(2,1)}, u32[]{:S(2)}, u32[]{:S(2)}) collective-permute-start(bf16[48,6144]{1,0:T(8,128)(2,1)} %collective-permute-done.2), channel_id=1, source_target_pairs={{0,8},{1,9},{2,10},{3,11},{8,16},{9,17},{10,18},{11,19},{16,24},{1... | collective-permute-start | bytes 1769480 | tf_op jit(solution)/shard_map/ppermute | solution.py:338
  56.8 49.7 %all-to-all-start.1 = ((bf16[8,32,2048]{2,1,0:T(8,128)(2,1)}), bf16[8,32,2048]{2,1,0:T(8,128)(2,1)S(1)}, u32[]{:S(2)}, u32[]{:S(2)}) async-start(bf16[8,32,2048]{2,1,0:T(8,128)(2,1)} %short_conv.4), calls=%async_computation.1 | async-start | bytes 2097152 | tf_op jit(solution)/shard_map/all_to_all | solution.py:307
  61.3 35.3 %collective-permute-start.4 = (bf16[512,1024]{1,0:T(8,128)(2,1)}, bf16[512,1024]{1,0:T(8,128)(2,1)S(1)}, u32[]{:S(2)}, u32[]{:S(2)}) collective-permute-start(bf16[512,1024]{1,0:T(8,128)(2,1)} %constant_dynamic-slice_fusion.1), channel_id=1, source_target_pairs={{0,4},{4,0},{1,5},{5,1},{2,6},{6,2},{3,7},{7,3},{8,12},{12,8},{9,1... | collective-permute-start | bytes 3145736 | tf_op jit(solution)/shard_map/ppermute | solution.py:377
  96.6 24.2 %copy-start.9 = (bf16[512,1024]{1,0:T(8,128)(2,1)}, bf16[512,1024]{1,0:T(8,128)(2,1)S(1)}, u32[]{:S(2)}) copy-start(bf16[512,1024]{1,0:T(8,128)(2,1)S(1)} %collective-permute-done.4) | copy-start | bytes 3145732
  106.5 6.6 %copy-start.8 = (bf16[8,32,2048]{2,1,0:T(8,128)(2,1)}, bf16[8,32,2048]{2,1,0:T(8,128)(2,1)S(1)}, u32[]{:S(2)}) copy-start(bf16[8,32,2048]{2,1,0:T(8,128)(2,1)S(1)} %all-to-all-done.1) | copy-start | bytes 3145732
  106.5 32.7 %all-to-all-start.2 = ((bf16[8,32,2048]{2,1,0:T(8,128)(2,1)}), bf16[8,32,2048]{2,1,0:T(8,128)(2,1)S(1)}, u32[]{:S(2)}, u32[]{:S(2)}) async-start(bf16[8,32,2048]{2,1,0:T(8,128)(2,1)} %short_conv.5), calls=%async_computation.2 | async-start | bytes 2097152 | tf_op jit(solution)/shard_map/all_to_all | solution.py:307
  110.1 3.0 collective-permute-start.5
  113.1 0.7 copy-start.21
  120.8 16.5 %collective-permute-start.6 = (bf16[256,1024]{1,0:T(8,128)(2,1)}, bf16[256,1024]{1,0:T(8,128)(2,1)}, u32[]{:S(2)}, u32[]{:S(2)}) collective-permute-start(bf16[256,1024]{1,0:T(8,128)(2,1)} %medium_conv.4.refs_0_), channel_id=1, source_target_pairs={{0,4},{4,0},{1,5},{5,1},{2,6},{6,2},{3,7},{7,3},{8,12},{12,8},{9,1... | collective-permute-start | bytes 1572872 | tf_op jit(solution)/shard_map/ppermute | solution.py:396
  122.5 16.8 %collective-permute-start.7 = (bf16[256,1024]{1,0:T(8,128)(2,1)}, bf16[256,1024]{1,0:T(8,128)(2,1)S(1)}, u32[]{:S(2)}, u32[]{:S(2)}) collective-permute-start(bf16[256,1024]{1,0:T(8,128)(2,1)} %medium_conv.4.refs_0_), channel_id=1, source_target_pairs={{0,2},{2,0},{1,3},{3,1},{4,6},{6,4},{5,7},{7,5},{8,10},{10,8},{9,1... | collective-permute-start | bytes 1572872 | tf_op jit(solution)/shard_map/ppermute | solution.py:397
  135.7 9.0 %copy-start.10 = (bf16[512,1024]{1,0:T(8,128)(2,1)S(1)}, bf16[512,1024]{1,0:T(8,128)(2,1)}, u32[]{:S(2)}) copy-start(bf16[512,1024]{1,0:T(8,128)(2,1)} %copy-done.9) | copy-start | bytes 3145732
  139.2 0.8 copy-start.13
  139.2 6.3 %copy-start.7 = (bf16[8,32,2048]{2,1,0:T(8,128)(2,1)}, bf16[8,32,2048]{2,1,0:T(8,128)(2,1)S(1)}, u32[]{:S(2)}) copy-start(bf16[8,32,2048]{2,1,0:T(8,128)(2,1)S(1)} %all-to-all-done.2) | copy-start | bytes 3145732
  140.0 47.6 %all-to-all-start.3 = ((bf16[8,32,2048]{2,1,0:T(8,128)(2,1)}), bf16[8,32,2048]{2,1,0:T(8,128)(2,1)S(1)}, u32[]{:S(2)}, u32[]{:S(2)}) async-start(bf16[8,32,2048]{2,1,0:T(8,128)(2,1)} %short_conv.6), calls=%async_computation.3 | async-start | bytes 2097152 | tf_op jit(solution)/shard_map/all_to_all | solution.py:307
  144.6 86.1 %all-gather.9.cloned.1.call-start = ((), (), s32[]{:S(2)}) async-start(), calls=%async_computation.8 | async-start | bytes 2621440 | tf_op jit(solution)/shard_map/all_gather | solution.py:328
  145.6 3.0 collective-permute-start.9
  147.5 25.9 %collective-permute-start.8 = (bf16[256,1024]{1,0:T(8,128)(2,1)}, bf16[256,1024]{1,0:T(8,128)(2,1)S(1)}, u32[]{:S(2)}, u32[]{:S(2)}) collective-permute-start(bf16[256,1024]{1,0:T(8,128)(2,1)} %collective-permute-done.6.refs_2_), channel_id=1, source_target_pairs={{0,2},{2,0},{1,3},{3,1},{4,6},{6,4},{5,7},{7,5},{8,10},{10,8},{9,1... | collective-permute-start | bytes 1572872 | tf_op jit(solution)/shard_map/ppermute | solution.py:382
  148.6 0.7 copy-start.18
  156.3 17.0 %collective-permute-start.10 = (bf16[256,1024]{1,0:T(8,128)(2,1)}, bf16[256,1024]{1,0:T(8,128)(2,1)S(1)}, u32[]{:S(2)}, u32[]{:S(2)}) collective-permute-start(bf16[256,1024]{1,0:T(8,128)(2,1)} %medium_conv.5.refs_0_), channel_id=1, source_target_pairs={{0,4},{4,0},{1,5},{5,1},{2,6},{6,2},{3,7},{7,3},{8,12},{12,8},{9,1... | collective-permute-start | bytes 1572872 | tf_op jit(solution)/shard_map/ppermute | solution.py:396
  158.0 18.9 %collective-permute-start.11 = (bf16[256,1024]{1,0:T(8,128)(2,1)}, bf16[256,1024]{1,0:T(8,128)(2,1)S(1)}, u32[]{:S(2)}, u32[]{:S(2)}) collective-permute-start(bf16[256,1024]{1,0:T(8,128)(2,1)} %medium_conv.5.refs_0_), channel_id=1, source_target_pairs={{0,2},{2,0},{1,3},{3,1},{4,6},{6,4},{5,7},{7,5},{8,10},{10,8},{9,1... | collective-permute-start | bytes 1572872 | tf_op jit(solution)/shard_map/ppermute | solution.py:397
  173.3 14.3 %copy-start.15 = (bf16[256,1024]{1,0:T(8,128)(2,1)}, bf16[256,1024]{1,0:T(8,128)(2,1)S(1)}, u32[]{:S(2)}) copy-start(bf16[256,1024]{1,0:T(8,128)(2,1)S(1)} %collective-permute-done.8.refs_3_) | copy-start | bytes 1572868
  173.3 14.3 %copy-start.11 = (bf16[256,1024]{1,0:T(8,128)(2,1)}, bf16[256,1024]{1,0:T(8,128)(2,1)S(1)}, u32[]{:S(2)}) copy-start(bf16[256,1024]{1,0:T(8,128)(2,1)S(1)} %collective-permute-done.10.refs_2_) | copy-start | bytes 1572868
  176.9 10.7 %copy-start.12 = (bf16[256,1024]{1,0:T(8,128)(2,1)}, bf16[256,1024]{1,0:T(8,128)(2,1)S(1)}, u32[]{:S(2)}) copy-start(bf16[256,1024]{1,0:T(8,128)(2,1)S(1)} %collective-permute-done.11.refs_1_) | copy-start | bytes 1572868
  187.7 10.5 %copy-start.6 = (bf16[8,32,2048]{2,1,0:T(8,128)(2,1)}, bf16[8,32,2048]{2,1,0:T(8,128)(2,1)S(1)}, u32[]{:S(2)}) copy-start(bf16[8,32,2048]{2,1,0:T(8,128)(2,1)S(1)} %all-to-all-done.3) | copy-start | bytes 3145732
  191.9 38.8 %collective-permute-start.16 = (bf16[1024,1024]{1,0:T(8,128)(2,1)}, bf16[1024,1024]{1,0:T(8,128)(2,1)S(1)}, u32[]{:S(2)}, u32[]{:S(2)}) collective-permute-start(bf16[1024,1024]{1,0:T(8,128)(2,1)} %stack.79.refs_0_.refs_1_), channel_id=1, source_target_pairs={{0,1},{1,0},{2,3},{3,2},{4,5},{5,4},{6,7},{7,6},{8,9},{9,8},{10,11... | collective-permute-start | bytes 6291464 | tf_op jit(solution)/shard_map/ppermute | solution.py:370
  191.9 38.8 %all-to-all-start.4 = ((bf16[8,32,2048]{2,1,0:T(8,128)(2,1)}), bf16[8,32,2048]{2,1,0:T(8,128)(2,1)}, u32[]{:S(2)}, u32[]{:S(2)}) async-start(bf16[8,32,2048]{2,1,0:T(8,128)(2,1)} %short_conv.7), calls=%async_computation.4 | async-start | bytes 2097152 | tf_op jit(solution)/shard_map/all_to_all | solution.py:307
  198.1 113.4 %all-gather.11.cloned.1.call-start = ((), (), s32[]{:S(2)}) async-start(), calls=%async_computation.9 | async-start | bytes 5242880 | tf_op jit(solution)/shard_map/all_gather | solution.py:328
  198.2 32.5 %slice-start = ((bf16[512,1024]{1,0:T(8,128)(2,1)}), bf16[512,512]{1,0:T(8,128)(2,1)S(1)}, s32[]{:S(2)}) async-start(bf16[512,1024]{1,0:T(8,128)(2,1)} %constant_dynamic-slice_fusion.2), calls=%async_computation.10 | async-start | bytes 1048576 | tf_op jit(solution)/shard_map/slice | solution.py:312
  198.2 32.5 %slice-start.1 = ((bf16[512,1024]{1,0:T(8,128)(2,1)}), bf16[512,512]{1,0:T(8,128)(2,1)S(1)}, s32[]{:S(2)}) async-start(bf16[512,1024]{1,0:T(8,128)(2,1)} %copy-done.9), calls=%async_computation.11 | async-start | bytes 1048576 | tf_op jit(solution)/shard_map/slice | solution.py:312
  198.2 3.4 collective-permute-start.13
  200.5 17.5 %collective-permute-start.12 = (bf16[256,1024]{1,0:T(8,128)(2,1)}, bf16[256,1024]{1,0:T(8,128)(2,1)}, u32[]{:S(2)}, u32[]{:S(2)}) collective-permute-start(bf16[256,1024]{1,0:T(8,128)(2,1)} %copy-done.11), channel_id=1, source_target_pairs={{0,2},{2,0},{1,3},{3,1},{4,6},{6,4},{5,7},{7,5},{8,10},{10,8},{9,1... | collective-permute-start | bytes 1572872 | tf_op jit(solution)/shard_map/ppermute | solution.py:382
  201.6 0.7 copy-start.19
  209.4 21.3 %collective-permute-start.14 = (bf16[256,1024]{1,0:T(8,128)(2,1)}, bf16[256,1024]{1,0:T(8,128)(2,1)}, u32[]{:S(2)}, u32[]{:S(2)}) collective-permute-start(bf16[256,1024]{1,0:T(8,128)(2,1)} %medium_conv.6.refs_0_), channel_id=1, source_target_pairs={{0,4},{4,0},{1,5},{5,1},{2,6},{6,2},{3,7},{7,3},{8,12},{12,8},{9,1... | collective-permute-start | bytes 1572872 | tf_op jit(solution)/shard_map/ppermute | solution.py:396
  211.7 19.0 %collective-permute-start.15 = (bf16[256,1024]{1,0:T(8,128)(2,1)}, bf16[256,1024]{1,0:T(8,128)(2,1)}, u32[]{:S(2)}, u32[]{:S(2)}) collective-permute-start(bf16[256,1024]{1,0:T(8,128)(2,1)} %medium_conv.6.refs_0_), channel_id=1, source_target_pairs={{0,2},{2,0},{1,3},{3,1},{4,6},{6,4},{5,7},{7,5},{8,10},{10,8},{9,1... | collective-permute-start | bytes 1572872 | tf_op jit(solution)/shard_map/ppermute | solution.py:397
  230.7 1.7 copy-start.4
  232.4 14.2 %collective-permute-start.18 = (bf16[256,1024]{1,0:T(8,128)(2,1)}, bf16[256,1024]{1,0:T(8,128)(2,1)S(1)}, u32[]{:S(2)}, u32[]{:S(2)}) collective-permute-start(bf16[256,1024]{1,0:T(8,128)(2,1)} %collective-permute-done.14.refs_2_), channel_id=1, source_target_pairs={{0,2},{2,0},{1,3},{3,1},{4,6},{6,4},{5,7},{7,5},{8,10},{10,8},{9,1... | collective-permute-start | bytes 1572872 | tf_op jit(solution)/shard_map/ppermute | solution.py:382
  233.4 3.2 collective-permute-start.17
  236.6 0.7 copy-start.20
  246.6 27.5 %copy-start.14 = (bf16[256,1024]{1,0:T(8,128)(2,1)}, bf16[256,1024]{1,0:T(8,128)(2,1)S(1)}, u32[]{:S(2)}) copy-start(bf16[256,1024]{1,0:T(8,128)(2,1)S(1)} %collective-permute-done.18.refs_3_) | copy-start | bytes 1572868
  246.6 22.6 %collective-permute-start.20 = (bf16[256,1024]{1,0:T(8,128)(2,1)}, bf16[256,1024]{1,0:T(8,128)(2,1)S(1)}, u32[]{:S(2)}, u32[]{:S(2)}) collective-permute-start(bf16[256,1024]{1,0:T(8,128)(2,1)} %medium_conv.7.refs_0_), channel_id=1, source_target_pairs={{0,2},{2,0},{1,3},{3,1},{4,6},{6,4},{5,7},{7,5},{8,10},{10,8},{9,1... | collective-permute-start | bytes 1572872 | tf_op jit(solution)/shard_map/ppermute | solution.py:387
  257.5 11.7 %collective-permute-start.19 = (bf16[256,1024]{1,0:T(8,128)(2,1)}, bf16[256,1024]{1,0:T(8,128)(2,1)S(1)}, u32[]{:S(2)}, u32[]{:S(2)}) collective-permute-start(bf16[256,1024]{1,0:T(8,128)(2,1)} %medium_conv.7.refs_0_), channel_id=1, source_target_pairs={{0,4},{4,0},{1,5},{5,1},{2,6},{6,2},{3,7},{7,3},{8,12},{12,8},{9,1... | collective-permute-start | bytes 1572872 | tf_op jit(solution)/shard_map/ppermute | solution.py:386
  269.2 4.9 %copy-start.16 = (bf16[256,1024]{1,0:T(8,128)(2,1)}, bf16[256,1024]{1,0:T(8,128)(2,1)S(1)}, u32[]{:S(2)}) copy-start(bf16[256,1024]{1,0:T(8,128)(2,1)S(1)} %collective-permute-done.20.refs_1_) | copy-start | bytes 1572868
  269.2 12.8 %collective-permute-start.21 = (bf16[256,1024]{1,0:T(8,128)(2,1)S(1)}, bf16[256,1024]{1,0:T(8,128)(2,1)}, u32[]{:S(2)}, u32[]{:S(2)}) collective-permute-start(bf16[256,1024]{1,0:T(8,128)(2,1)S(1)} %collective-permute-done.20.refs_1_), channel_id=1, source_target_pairs={{0,4},{4,0},{1,5},{5,1},{2,6},{6,2},{3,7},{7,3},{8,12},{12,8},{9,1... | collective-permute-start | bytes 1572872 | tf_op jit(solution)/shard_map/ppermute | solution.py:382
  269.3 0.9 copy-start.17
  274.1 12.4 %collective-permute-start.22 = (bf16[1024,1024]{1,0:T(8,128)(2,1)}, bf16[1024,1024]{1,0:T(8,128)(2,1)S(1)}, u32[]{:S(2)}, u32[]{:S(2)}) collective-permute-start(bf16[1024,1024]{1,0:T(8,128)(2,1)} %stack.80.refs_2_.refs_3_), channel_id=1, source_target_pairs={{0,1},{1,0},{2,3},{3,2},{4,5},{5,4},{6,7},{7,6},{8,9},{9,8},{10,11... | collective-permute-start | bytes 6291464 | tf_op jit(solution)/shard_map/ppermute | solution.py:370
  278.2 8.4 %collective-permute-start.23 = (bf16[1024,1024]{1,0:T(8,128)(2,1)}, bf16[1024,1024]{1,0:T(8,128)(2,1)}, u32[]{:S(2)}, u32[]{:S(2)}) collective-permute-start(bf16[1024,1024]{1,0:T(8,128)(2,1)} %stack.81.refs_4_.refs_5_), channel_id=1, source_target_pairs={{0,1},{1,0},{2,3},{3,2},{4,5},{5,4},{6,7},{7,6},{8,9},{9,8},{10,11... | collective-permute-start | bytes 6291464 | tf_op jit(solution)/shard_map/ppermute | solution.py:370
  285.9 4.5 %collective-permute-start.24 = (bf16[1024,1024]{1,0:T(8,128)(2,1)}, bf16[1024,1024]{1,0:T(8,128)(2,1)}, u32[]{:S(2)}, u32[]{:S(2)}) collective-permute-start(bf16[1024,1024]{1,0:T(8,128)(2,1)} %stack.82.refs_6_.refs_7_), channel_id=1, source_target_pairs={{0,1},{1,0},{2,3},{3,2},{4,5},{5,4},{6,7},{7,6},{8,9},{9,8},{10,11... | collective-permute-start | bytes 6291464 | tf_op jit(solution)/shard_map/ppermute | solution.py:370
  286.5 3.9 %copy-start.5 = (bf16[1024,1024]{1,0:T(8,128)(2,1)}, bf16[1024,1024]{1,0:T(8,128)(2,1)S(1)}, u32[]{:S(2)}) copy-start(bf16[1024,1024]{1,0:T(8,128)(2,1)S(1)} %collective-permute-done.22.refs_10_.refs_11_) | copy-start | bytes 6291460
  307.9 29.2 %all-to-all-start.5 = ((bf16[8,256,512]{2,1,0:T(8,128)(2,1)}), bf16[8,256,512]{2,1,0:T(8,128)(2,1)S(1)}, u32[]{:S(2)}, u32[]{:S(2)}) async-start(bf16[8,256,512]{2,1,0:T(8,128)(2,1)} %bitcast.82), calls=%async_computation.5 | async-start | bytes 4194304 | tf_op jit(solution)/shard_map/all_to_all | solution.py:415
  337.1 1.3 copy-start.2
  338.4 29.6 %copy-start.3 = (bf16[8,256,512]{2,1,0:T(8,128)(2,1)S(1)}, bf16[8,256,512]{2,1,0:T(8,128)(2,1)}, u32[]{:S(2)}) copy-start(bf16[8,256,512]{2,1,0:T(8,128)(2,1)} %copy-done.2) | copy-start | bytes 6291460
  368.1 3.5 copy-start.1
Sparse Core Ops, SparseCore 0:
  25.9 76.7 all-gather.6
  147.0 63.2 all-gather.8
  232.5 78.4 all-gather.10

commit v2 on v1

--- a/solution.py
+++ b/solution.py
@@ -258,8 +258,6 @@
             elif c + 1 < ctx_count:
                 shift.append((f * ctx_count + c, c + 1))
 
-    onward = [(i - ctx_count, o) for i, o in shift if i // ctx_count % 2 == 1]
-
     live, flying = {}, {}
 
     seqs = jnp.arange(count, dtype=jnp.int32)
@@ -334,9 +332,8 @@
         [near[:, depth - i : depth - i + blk] == near[:, depth:] for i in range(short_len)], axis=-1
     ).astype(jnp.float32)
     live["give"] = give
-    turned = lax.ppermute(after(tails[1], tails[0]), "fx", SWAP)
-    passed = lax.ppermute(turned, EVERY, onward)
-    flying["halo"] = (2, jnp.where(x_at == 1, turned, passed).reshape(count, depth, wide // 2))
+    rest = lax.ppermute(after(tails[1], tails[0]), EVERY, shift).reshape(count, depth, wide // 2)
+    flying["halo"] = (2, rest)
     live["sent", 0] = short_call(order, order_prev, blocks, direct, taps_full, mask, 0)
     live["mask"] = mask
     live["prior"] = order_prev
@@ -360,7 +357,6 @@
         depth = out_weight.shape[0]
         return project_call(side, dest, here, there, panels, unit * wide, depth, low, sums)
 
-    newest = []
 
     def stack_steps(step, j):
         if FENCED <= step and j < CHUNKS - 1:
@@ -378,20 +374,21 @@
         if step <= CHUNKS:
             flying["routed", step - 1] = (step, exchange(live.pop(("sent", step - 1))))
         for j in [j for j in range(CHUNKS) if step == j + 4 - (j in NEAR_EARLY)]:
-            first, second = ("by_x", "y") if j < VIA_X else ("by_y", "fx")
-            flying["by_both", j] = (step, lax.ppermute(live[first, j], second, SWAP))
+            if j < VIA_X:
+                flying["by_both", j] = (step, lax.ppermute(live["by_x", j], "y", SWAP))
         j = step - 3
         if 0 <= j < CHUNKS and j not in NEAR_EARLY:
             live["gated", j] = after(live["gated", j], live["by_both", j - 1])
             flying["by_x", j] = (step, lax.ppermute(live["gated", j], "fx", SWAP))
             flying["by_y", j] = (step, lax.ppermute(live["gated", j], "y", SWAP))
+            across = [(0, 3), (1, 2), (2, 1), (3, 0)]
+            flying["by_both", j] = (step, lax.ppermute(live["gated", j], ("fx", "y"), across))
         j = step - 2
         if 0 <= j < CHUNKS:
             routed = live.pop(("routed", j))
             before = lax.ppermute(routed[tok_rows - ROWS :, cols:], CTX, next_ctx)
             gated = medium_call(routed, before, live["medium"], live["same"], j, group_size)
             flying["gated", j] = (step, gated)
-            newest.append(gated)
             if j in NEAR_EARLY:
                 flying["by_x", j] = (step, lax.ppermute(gated, "fx", SWAP))
                 flying["by_y", j] = (step, lax.ppermute(gated, "y", SWAP))

time: 382 us -> 380 us (level)
  starting transfers between devices: 87.3 us -> 100 us
  waiting for transfers between devices: 99.8 us -> 87.9 us
    ppermute x6 -> x5, waiting for transfers between devices: 11 us -> 35.5 us  [the longest x1 33.4 us: on_device(): lax.ppermute(after(tails[1], tails[0]), EVERY, shift)]
    ppermute x1, waiting for transfers between devices: 21 us -> 0.01 us  [on_device(): flying['got'] = (2, lax.ppermute(live.pop('give'), 'fx', SWAP))]
    all_to_all x4, waiting for transfers between devices: 20.6 us -> 11 us  [exchange(): routed = lax.all_to_all(sent, FSDP, split_axis=0, concat_axis=0, tiled=True)]
    ppermute x4, starting transfers between devices: 0.55 us -> 7.09 us  [stack_steps(): flying['there', j] = (step + 1, lax.ppermute(here, 'core', SWAP))]
    ppermute x1, waiting for transfers between devices: 11.7 us -> 6.42 us  [on_device(): flying['by_y', j] = (step, lax.ppermute(live['gated', j], 'y', SWAP))]
    all_to_all x4, starting transfers between devices: 18.8 us -> 23.7 us  [exchange(): routed = lax.all_to_all(sent, FSDP, split_axis=0, concat_axis=0, tiled=True)]
  transfers between devices with their start and end apart: 34 -> 33, of which waited for: 19 -> 13; matrix products, arithmetic and copies ran while one was open for 6% -> 5% of each run, Pallas kernels for 29% -> 29%
where the time goes in v2:
time: 380 us; the launch traced here: 376 us
  Pallas kernels  114 us (30%)
  starting transfers between devices  100 us (26%)
  waiting for transfers between devices  87.9 us (23%)
  blocking collectives  29.6 us (8%)
  local copies, waits for them, and re-layouts  25.9 us (7%)
  between operations  13.5 us (4%)
  other arithmetic  4.96 us (1%)
    pallas_call x2, Pallas kernels, project_call(): pl.pallas_call(functools.partial(project_kernel, len(pieces), full), grid...  34.8 us
    ppermute x1, waiting for transfers between devices, on_device(): lax.ppermute(after(tails[1], tails[0]), EVERY, shift)  33.4 us
    pallas_call x4, Pallas kernels, short_call(): pl.pallas_call(short_kernel, grid_spec=pltpu.PrefetchScalarGridSpec(num_s...  31.3 us
    all_to_all x1, blocking collectives, on_device(): lax.all_to_all(given, PLANE, split_axis=0, concat_axis=0, tiled=True)  29.6 us
    pallas_call x4, Pallas kernels, medium_call(): pl.pallas_call(functools.partial(medium_kernel, group_size), grid=(steps,...  28.3 us
    all_to_all x4, starting transfers between devices, exchange(): routed = lax.all_to_all(sent, FSDP, split_axis=0, concat_axis=0, tiled=True)  23.7 us
    ppermute x3, starting transfers between devices, on_device(): flying['by_y', j] = (step, lax.ppermute(gated, 'y', SWAP))  20.6 us
    pallas_call x4, Pallas kernels, stack_call(): pl.pallas_call(stack_kernel, grid=(cols // tile,), in_specs=[pl.BlockSpec...  16.3 us
  transfers between devices with their start and end apart: 33, of which 13 were waited for; matrix products, arithmetic and copies ran while one was open for 5% of the time, Pallas kernels for 29%

profile of v2, /device:TPU:0, one launch (start us, length us, event | category | flops | bytes accessed | tf_op | source)
XLA Modules:
  0.0 376.1 jit_solution(14161424117122200607)
XLA Ops:
  6.5 2.7 fusion.12
  9.4 1.0 reshape.129
  10.4 4.9 %collective-permute-start = (bf16[48,6144]{1,0:T(8,128)(2,1)}, bf16[48,6144]{1,0:T(8,128)(2,1)S(1)}, u32[]{:S(2)}, u32[]{:S(2)}) collective-permute-start(bf16[48,6144]{1,0:T(8,128)(2,1)} %reshape.129), channel_id=1, source_target_pairs={{0,4},{1,5},{2,6},{3,7},{4,8},{5,9},{6,10},{7,11},{8,12},{9,13},{1... | collective-permute-start | bytes 1769480 | tf_op jit(solution)/shard_map/ppermute | solution.py:273
  16.0 4.8 %all-to-all-start = ((s32[8,1,38]{2,1,0:T(1,128)}), s32[8,1,38]{2,1,0:T(1,128)S(1)}, u32[]{:S(2)}, u32[]{:S(2)}) async-start(s32[8,1,38]{2,1,0:T(1,128)} %bitcast.13), calls=%async_computation | async-start | bytes 8192 | tf_op jit(solution)/shard_map/all_to_all | solution.py:280
  21.1 3.9 %collective-permute-start.1 = (s32[8]{0:T(128)S(1)}, s32[8]{0:T(128)S(1)}, u32[]{:S(2)}, u32[]{:S(2)}) collective-permute-start(s32[8]{0:T(128)S(1)} %select_reduce_fusion.order), channel_id=1, source_target_pairs={{0,4},{1,5},{2,6},{3,7},{4,8},{5,9},{6,10},{7,11},{8,12},{9,13},{1... | collective-permute-start | bytes 104 | tf_op jit(solution)/shard_map/ppermute | solution.py:278
  26.8 1.1 constant_dynamic-slice_fusion.2
  27.8 1.1 constant_dynamic-slice_fusion.1
  28.9 2.0 broadcast_in_dim.33
  30.9 4.4 %reshape.131.fq.fk.fv = f32[7,12288]{1,0:T(8,128)} reshape(f32[7,768,16]{2,1,0:T(8,128)} %broadcast_in_dim.33) | data formatting | bytes 688128 | tf_op jit(solution)/shard_map/reshape | solution.py:283
  36.5 1.1 reshape.130.hq.hk.hv
  38.9 7.8 %short_conv.4 = bf16[8,32,2048]{2,1,0:T(8,128)(2,1)} custom-call(s32[8]{0:T(128)} %copy-done.25, s32[8]{0:T(128)} %copy-done.26, bf16[8,32,12288]{2,1,0:T(8,128)(2,1)} %bitcast.59, bf16[8,32,12288]{2,1,0:T(8,128)(2,1)} %bitcast.60, bf16[8,32,12288]{2,1,0:T(8,128)(2,1)} %bitcast.61, bf16[8,6,6144]{2,1,0:T(8,128)(2,1)} %reshape.130.hq.hk.hv, ...), custom_call_target="tpu_custom_call" | custom-call | flops 1 | bytes 1 | tf_op jit(solution)/shard_map/short_conv/pallas_call | solution.py:70
  46.7 4.8 %all-to-all-start.1 = ((bf16[8,32,2048]{2,1,0:T(8,128)(2,1)}), bf16[8,32,2048]{2,1,0:T(8,128)(2,1)S(1)}, u32[]{:S(2)}, u32[]{:S(2)}) async-start(bf16[8,32,2048]{2,1,0:T(8,128)(2,1)} %short_conv.4), calls=%async_computation.1 | async-start | bytes 2097152 | tf_op jit(solution)/shard_map/all_to_all | solution.py:305
  51.5 2.0 collective-permute-start.3
  53.5 1.1 pad_maximum_fusion.2
  54.6 1.0 reshape.132
  55.7 2.0 collective-permute-start.2
  57.6 7.8 %short_conv.5 = bf16[8,32,2048]{2,1,0:T(8,128)(2,1)} custom-call(s32[8]{0:T(128)} %copy-done.25, s32[8]{0:T(128)} %copy-done.26, bf16[8,32,12288]{2,1,0:T(8,128)(2,1)} %bitcast.62, bf16[8,32,12288]{2,1,0:T(8,128)(2,1)} %bitcast.63, bf16[8,32,12288]{2,1,0:T(8,128)(2,1)} %bitcast.64, bf16[8,6,6144]{2,1,0:T(8,128)(2,1)} %reshape.130.hq.hk.hv, ...), custom_call_target="tpu_custom_call" | custom-call | flops 1 | bytes 1 | tf_op jit(solution)/shard_map/short_conv/pallas_call | solution.py:70
  65.4 33.4 %collective-permute-done.2 = bf16[48,6144]{1,0:T(8,128)(2,1)S(1)} collective-permute-done((bf16[48,6144]{1,0:T(8,128)(2,1)}, bf16[48,6144]{1,0:T(8,128)(2,1)S(1)}, u32[]{:S(2)}, u32[]{:S(2)}) %collective-permute-start.2) | collective-permute-done | bytes 589856 | tf_op jit(solution)/shard_map/ppermute | solution.py:335
  98.8 1.1 reshape.133.hq.hk.hv
  100.0 10.2 %all-to-all-start.2 = ((bf16[8,32,2048]{2,1,0:T(8,128)(2,1)}), bf16[8,32,2048]{2,1,0:T(8,128)(2,1)S(1)}, u32[]{:S(2)}, u32[]{:S(2)}) async-start(bf16[8,32,2048]{2,1,0:T(8,128)(2,1)} %short_conv.5), calls=%async_computation.2 | async-start | bytes 2097152 | tf_op jit(solution)/shard_map/all_to_all | solution.py:305
  110.2 1.7 collective-permute-start.4
  111.9 1.1 collective-permute-done.4.halo
  113.7 7.1 %medium_conv.4.refs_0_ = bf16[256,1024]{1,0:T(8,128)(2,1)} custom-call(bf16[256,2048]{1,0:T(8,128)(2,1)} %bitcast.80, bf16[256,2048]{1,0:T(8,128)(2,1)} %bitcast.81, bf16[128,1024]{1,0:T(8,128)(2,1)} %copy-done.21, f32[256,256]{1,0:T(8,128)} %pad.6.taps, bf16[2,128,256]{2,1,0:T(8,128)(2,1)} %add_convert_fusion.same), custom_call_target="tpu_custom_call" | custom-call | flops 1 | bytes 1 | tf_op jit(solution)/shard_map/medium_conv/pallas_call | solution.py:111
  120.8 1.8 collective-permute-start.5
  122.5 6.6 %collective-permute-start.6 = (bf16[256,1024]{1,0:T(8,128)(2,1)}, bf16[256,1024]{1,0:T(8,128)(2,1)S(1)}, u32[]{:S(2)}, u32[]{:S(2)}) collective-permute-start(bf16[256,1024]{1,0:T(8,128)(2,1)} %medium_conv.4.refs_0_), channel_id=1, source_target_pairs={{0,2},{2,0},{1,3},{3,1},{4,6},{6,4},{5,7},{7,5},{8,10},{10,8},{9,1... | collective-permute-start | bytes 1572872 | tf_op jit(solution)/shard_map/ppermute | solution.py:394
  129.1 7.8 %short_conv.6 = bf16[8,32,2048]{2,1,0:T(8,128)(2,1)} custom-call(s32[8]{0:T(128)} %copy-done.25, s32[8]{0:T(128)} %copy-done.26, bf16[8,32,12288]{2,1,0:T(8,128)(2,1)} %bitcast.65, bf16[8,32,12288]{2,1,0:T(8,128)(2,1)} %bitcast.66, bf16[8,32,12288]{2,1,0:T(8,128)(2,1)} %bitcast.67, bf16[8,6,6144]{2,1,0:T(8,128)(2,1)} %reshape.133.hq.hk.hv, ...), custom_call_target="tpu_custom_call" | custom-call | flops 1 | bytes 1 | tf_op jit(solution)/shard_map/short_conv/pallas_call | solution.py:70
  137.0 3.5 collective-permute-done.6.refs_1_
  141.3 4.5 %all-to-all-start.3 = ((bf16[8,32,2048]{2,1,0:T(8,128)(2,1)}), bf16[8,32,2048]{2,1,0:T(8,128)(2,1)S(1)}, u32[]{:S(2)}, u32[]{:S(2)}) async-start(bf16[8,32,2048]{2,1,0:T(8,128)(2,1)} %short_conv.6), calls=%async_computation.3 | async-start | bytes 2097152 | tf_op jit(solution)/shard_map/all_to_all | solution.py:305
  146.8 1.3 collective-permute-start.8
  148.2 1.3 collective-permute-start.7
  150.1 7.0 %medium_conv.5.refs_0_ = bf16[256,1024]{1,0:T(8,128)(2,1)} custom-call(bf16[256,2048]{1,0:T(8,128)(2,1)} %bitcast.77, bf16[256,2048]{1,0:T(8,128)(2,1)} %bitcast.78, bf16[128,1024]{1,0:T(8,128)(2,1)} %copy-done.18, f32[256,256]{1,0:T(8,128)} %pad.6.taps, bf16[2,128,256]{2,1,0:T(8,128)(2,1)} %add_convert_fusion.same), custom_call_target="tpu_custom_call" | custom-call | flops 1 | bytes 1 | tf_op jit(solution)/shard_map/medium_conv/pallas_call | solution.py:111
  157.2 2.0 collective-permute-start.9
  159.2 7.6 %collective-permute-start.10 = (bf16[256,1024]{1,0:T(8,128)(2,1)}, bf16[256,1024]{1,0:T(8,128)(2,1)S(1)}, u32[]{:S(2)}, u32[]{:S(2)}) collective-permute-start(bf16[256,1024]{1,0:T(8,128)(2,1)} %medium_conv.5.refs_0_), channel_id=1, source_target_pairs={{0,2},{2,0},{1,3},{3,1},{4,6},{6,4},{5,7},{7,5},{8,10},{10,8},{9,1... | collective-permute-start | bytes 1572872 | tf_op jit(solution)/shard_map/ppermute | solution.py:394
  166.8 7.8 %short_conv.7 = bf16[8,32,2048]{2,1,0:T(8,128)(2,1)} custom-call(s32[8]{0:T(128)} %copy-done.25, s32[8]{0:T(128)} %copy-done.26, bf16[8,32,12288]{2,1,0:T(8,128)(2,1)} %bitcast.68, bf16[8,32,12288]{2,1,0:T(8,128)(2,1)} %bitcast.69, bf16[8,32,12288]{2,1,0:T(8,128)(2,1)} %bitcast.70, bf16[8,6,6144]{2,1,0:T(8,128)(2,1)} %reshape.133.hq.hk.hv, ...), custom_call_target="tpu_custom_call" | custom-call | flops 1 | bytes 1 | tf_op jit(solution)/shard_map/short_conv/pallas_call | solution.py:70
  174.6 3.6 collective-permute-done.10.refs_1_
  178.2 11.0 %all-to-all-done.3 = bf16[8,32,2048]{2,1,0:T(8,128)(2,1)S(1)} async-done(((bf16[8,32,2048]{2,1,0:T(8,128)(2,1)}), bf16[8,32,2048]{2,1,0:T(8,128)(2,1)S(1)}, u32[]{:S(2)}, u32[]{:S(2)}) %all-to-all-start.3) | async-done | bytes 1048608 | tf_op jit(solution)/shard_map/all_to_all | solution.py:305
  189.2 4.2 %stack.79.refs_0_.refs_1_ = bf16[1024,1024]{1,0:T(8,128)(2,1)} custom-call(bf16[256,1024]{1,0:T(8,128)(2,1)} %medium_conv.4.refs_0_, bf16[256,1024]{1,0:T(8,128)(2,1)} %copy-done.14, bf16[256,1024]{1,0:T(8,128)(2,1)} %collective-permute-done.5.refs_2_, bf16[256,1024]{1,0:T(8,128)(2,1)} %copy-done.16), custom_call_target="tpu_custom_call" | custom-call | flops 1 | bytes 1 | tf_op jit(solution)/shard_map/stack/pallas_call | solution.py:198
  193.4 4.2 %all-to-all-start.4 = ((bf16[8,32,2048]{2,1,0:T(8,128)(2,1)}), bf16[8,32,2048]{2,1,0:T(8,128)(2,1)}, u32[]{:S(2)}, u32[]{:S(2)}) async-start(bf16[8,32,2048]{2,1,0:T(8,128)(2,1)} %short_conv.7), calls=%async_computation.4 | async-start | bytes 2097152 | tf_op jit(solution)/shard_map/all_to_all | solution.py:305
  197.8 2.6 collective-permute-start.12
  200.4 1.0 collective-permute-done.12.halo
  202.2 7.1 %medium_conv.6.refs_0_ = bf16[256,1024]{1,0:T(8,128)(2,1)} custom-call(bf16[256,2048]{1,0:T(8,128)(2,1)} %bitcast.74, bf16[256,2048]{1,0:T(8,128)(2,1)} %bitcast.75, bf16[128,1024]{1,0:T(8,128)(2,1)} %copy-done.19, f32[256,256]{1,0:T(8,128)} %pad.6.taps, bf16[2,128,256]{2,1,0:T(8,128)(2,1)} %add_convert_fusion.same), custom_call_target="tpu_custom_call" | custom-call | flops 1 | bytes 1 | tf_op jit(solution)/shard_map/medium_conv/pallas_call | solution.py:111
  209.2 1.5 collective-permute-start.13
  210.8 6.3 %collective-permute-start.14 = (bf16[256,1024]{1,0:T(8,128)(2,1)}, bf16[256,1024]{1,0:T(8,128)(2,1)}, u32[]{:S(2)}, u32[]{:S(2)}) collective-permute-start(bf16[256,1024]{1,0:T(8,128)(2,1)} %medium_conv.6.refs_0_), channel_id=1, source_target_pairs={{0,2},{2,0},{1,3},{3,1},{4,6},{6,4},{5,7},{7,5},{8,10},{10,8},{9,1... | collective-permute-start | bytes 1572872 | tf_op jit(solution)/shard_map/ppermute | solution.py:394
  217.1 12.4 %collective-permute-done.13.refs_2_ = bf16[256,1024]{1,0:T(8,128)(2,1)} collective-permute-done((bf16[256,1024]{1,0:T(8,128)(2,1)}, bf16[256,1024]{1,0:T(8,128)(2,1)}, u32[]{:S(2)}, u32[]{:S(2)}) %collective-permute-start.13) | collective-permute-done | bytes 524320 | tf_op jit(solution)/shard_map/ppermute | solution.py:393
  229.5 1.2 pad_maximum_fusion
  232.7 2.3 collective-permute-start.16
  236.7 7.1 %medium_conv.7.refs_0_ = bf16[256,1024]{1,0:T(8,128)(2,1)} custom-call(bf16[256,2048]{1,0:T(8,128)(2,1)} %bitcast.27.q.gate, bf16[256,2048]{1,0:T(8,128)(2,1)} %bitcast.27.q.gate, bf16[128,1024]{1,0:T(8,128)(2,1)} %copy-done.20, f32[256,256]{1,0:T(8,128)} %pad.6.taps, bf16[2,128,256]{2,1,0:T(8,128)(2,1)} %add_convert_fusion.same), custom_call_target="tpu_custom_call" | custom-call | flops 1 | bytes 1 | tf_op jit(solution)/shard_map/medium_conv/pallas_call | solution.py:111
  243.8 2.2 collective-permute-done.17.refs_3_
  246.0 11.0 %collective-permute-start.19 = (bf16[256,1024]{1,0:T(8,128)(2,1)}, bf16[256,1024]{1,0:T(8,128)(2,1)}, u32[]{:S(2)}, u32[]{:S(2)}) collective-permute-start(bf16[256,1024]{1,0:T(8,128)(2,1)} %medium_conv.7.refs_0_), channel_id=1, source_target_pairs={{0,2},{2,0},{1,3},{3,1},{4,6},{6,4},{5,7},{7,5},{8,10},{10,8},{9,1... | collective-permute-start | bytes 1572872 | tf_op jit(solution)/shard_map/ppermute | solution.py:383
  257.0 1.4 collective-permute-start.20
  258.4 4.1 %stack.80.refs_2_.refs_3_ = bf16[1024,1024]{1,0:T(8,128)(2,1)} custom-call(bf16[256,1024]{1,0:T(8,128)(2,1)} %medium_conv.5.refs_0_, bf16[256,1024]{1,0:T(8,128)(2,1)} %copy-done.13, bf16[256,1024]{1,0:T(8,128)(2,1)} %copy-done.12, bf16[256,1024]{1,0:T(8,128)(2,1)} %collective-permute-done.11.refs_3_), custom_call_target="tpu_custom_call" | custom-call | flops 1 | bytes 1 | tf_op jit(solution)/shard_map/stack/pallas_call | solution.py:198
  262.5 7.1 %collective-permute-start.21 = (bf16[1024,1024]{1,0:T(8,128)(2,1)}, bf16[1024,1024]{1,0:T(8,128)(2,1)S(1)}, u32[]{:S(2)}, u32[]{:S(2)}) collective-permute-start(bf16[1024,1024]{1,0:T(8,128)(2,1)} %stack.80.refs_2_.refs_3_), channel_id=1, source_target_pairs={{0,1},{1,0},{2,3},{3,2},{4,5},{5,4},{6,7},{7,6},{8,9},{9,8},{10,11... | collective-permute-start | bytes 6291464 | tf_op jit(solution)/shard_map/ppermute | solution.py:366
  269.5 4.0 %stack.81.refs_4_.refs_5_ = bf16[1024,1024]{1,0:T(8,128)(2,1)} custom-call(bf16[256,1024]{1,0:T(8,128)(2,1)} %medium_conv.6.refs_0_, bf16[256,1024]{1,0:T(8,128)(2,1)} %collective-permute-done.14.refs_1_, bf16[256,1024]{1,0:T(8,128)(2,1)} %collective-permute-done.13.refs_2_, bf16[256,1024]{1,0:T(8,128)(2,1)} %copy-done.15), custom_call_target="tpu_custom_call" | custom-call | flops 1 | bytes 1 | tf_op jit(solution)/shard_map/stack/pallas_call | solution.py:198
  273.6 6.4 %collective-permute-done.19.refs_1_ = bf16[256,1024]{1,0:T(8,128)(2,1)} collective-permute-done((bf16[256,1024]{1,0:T(8,128)(2,1)}, bf16[256,1024]{1,0:T(8,128)(2,1)}, u32[]{:S(2)}, u32[]{:S(2)}) %collective-permute-start.19) | collective-permute-done | bytes 524320 | tf_op jit(solution)/shard_map/ppermute | solution.py:383
  280.0 4.0 %stack.82.refs_6_.refs_7_ = bf16[1024,1024]{1,0:T(8,128)(2,1)} custom-call(bf16[256,1024]{1,0:T(8,128)(2,1)} %medium_conv.7.refs_0_, bf16[256,1024]{1,0:T(8,128)(2,1)} %collective-permute-done.19.refs_1_, bf16[256,1024]{1,0:T(8,128)(2,1)} %copy-done.17, bf16[256,1024]{1,0:T(8,128)(2,1)} %collective-permute-done.20.refs_3_), custom_call_target="tpu_custom_call" | custom-call | flops 1 | bytes 1 | tf_op jit(solution)/shard_map/stack/pallas_call | solution.py:198
  284.5 3.9 %collective-permute-done.23.refs_14_.refs_15_ = bf16[1024,1024]{1,0:T(8,128)(2,1)} collective-permute-done((bf16[1024,1024]{1,0:T(8,128)(2,1)}, bf16[1024,1024]{1,0:T(8,128)(2,1)}, u32[]{:S(2)}, u32[]{:S(2)}) %collective-permute-start.23) | collective-permute-done | bytes 2097184 | tf_op jit(solution)/shard_map/ppermute | solution.py:366
  288.4 17.5 %project.2 = bf16[2048,512]{1,0:T(8,128)(2,1)} custom-call(s32[1]{0:T(128)} %bitcast.side, s32[8]{0:T(128)} %fusion.11.dest, bf16[1024,1024]{1,0:T(8,128)(2,1)} %stack.79.refs_0_.refs_1_, bf16[1024,1024]{1,0:T(8,128)(2,1)} %stack.79.refs_0_.refs_1_, bf16[1024,1024]{1,0:T(8,128)(2,1)} %stack.80.refs_2_.refs_3_, bf16[1024,1024]{1,0:T(8,128)(2,1)} %stack.80.refs_2_.refs_3_, ...), custom_call_target="tpu_custom_call" | custom-call | flops 1 | bytes 1 | tf_op jit(solution)/shard_map/project/pallas_call | solution.py:166
  305.9 3.6 all-to-all-start.5
  309.5 1.2 all-gather.11.cloned.1.call-done
  310.7 17.4 %project.3 = bf16[2048,512]{1,0:T(8,128)(2,1)} custom-call(s32[1]{0:T(128)} %bitcast.side, s32[8]{0:T(128)} %fusion.11.dest, bf16[1024,1024]{1,0:T(8,128)(2,1)} %stack.79.refs_0_.refs_1_, bf16[1024,1024]{1,0:T(8,128)(2,1)} %stack.79.refs_0_.refs_1_, bf16[1024,1024]{1,0:T(8,128)(2,1)} %stack.80.refs_2_.refs_3_, bf16[1024,1024]{1,0:T(8,128)(2,1)} %stack.80.refs_2_.refs_3_, ...), custom_call_target="tpu_custom_call" | custom-call | flops 1 | bytes 1 | tf_op jit(solution)/shard_map/project/pallas_call | solution.py:166
  328.1 7.1 %all-to-all-done.5.refs_0_ = bf16[8,256,512]{2,1,0:T(8,128)(2,1)S(1)} async-done(((bf16[8,256,512]{2,1,0:T(8,128)(2,1)}), bf16[8,256,512]{2,1,0:T(8,128)(2,1)S(1)}, u32[]{:S(2)}, u32[]{:S(2)}) %all-to-all-start.5) | async-done | bytes 2097184 | tf_op jit(solution)/shard_map/all_to_all | solution.py:412
  335.1 1.3 copy-done.2
  336.5 29.6 %all_to_all.42.refs_1_ = bf16[8,256,512]{2,1,0:T(8,128)(2,1)S(1)} all-to-all(bf16[8,256,512]{2,1,0:T(8,128)(2,1)} %bitcast.83), channel_id=1, replica_groups=mesh['fh'=4,'fx'=2,'y'=2,'core'=2] {'fx','y','core'}, dimensions={0} | all-to-all | bytes 4194304 | tf_op jit(solution)/shard_map/all_to_all | solution.py:412
  366.1 3.5 place.1
  (121 shorter events, 13.7 us)
Async XLA Ops:
  6.5 18.4 %copy-start = (bf16[512,2048]{1,0:T(8,128)(2,1)S(1)}, bf16[512,2048]{1,0:T(8,128)(2,1)}, u32[]{:S(2)}) copy-start(bf16[512,2048]{1,0:T(8,128)(2,1)} %param.11) | copy-start | bytes 6291460
  9.2 6.1 %copy-start.24 = (s32[1,1024]{1,0:T(1,128)S(1)}, s32[1,1024]{1,0:T(1,128)}, u32[]{:S(2)}) copy-start(s32[1,1024]{1,0:T(1,128)} %param.8) | copy-start | bytes 12292
  9.2 11.7 %copy-start.27 = (s32[1,8]{1,0:T(1,128)S(1)}, s32[1,8]{1,0:T(1,128)}, u32[]{:S(2)}) copy-start(s32[1,8]{1,0:T(1,128)} %param.7) | copy-start | bytes 100
  10.4 26.1 %collective-permute-start = (bf16[48,6144]{1,0:T(8,128)(2,1)}, bf16[48,6144]{1,0:T(8,128)(2,1)S(1)}, u32[]{:S(2)}, u32[]{:S(2)}) collective-permute-start(bf16[48,6144]{1,0:T(8,128)(2,1)} %reshape.129), channel_id=1, source_target_pairs={{0,4},{1,5},{2,6},{3,7},{4,8},{5,9},{6,10},{7,11},{8,12},{9,13},{1... | collective-permute-start | bytes 1769480 | tf_op jit(solution)/shard_map/ppermute | solution.py:273
  16.0 21.5 %all-to-all-start = ((s32[8,1,38]{2,1,0:T(1,128)}), s32[8,1,38]{2,1,0:T(1,128)S(1)}, u32[]{:S(2)}, u32[]{:S(2)}) async-start(s32[8,1,38]{2,1,0:T(1,128)} %bitcast.13), calls=%async_computation | async-start | bytes 8192 | tf_op jit(solution)/shard_map/all_to_all | solution.py:280
  20.9 79.1 %all-gather.7.cloned.1.call-start = ((), (), s32[]{:S(2)}) async-start(), calls=%async_computation.7 | async-start | bytes 2621440 | tf_op jit(solution)/shard_map/all_gather | solution.py:326
  21.1 7.9 %copy-start.25 = (s32[8]{0:T(128)}, s32[8]{0:T(128)S(1)}, u32[]{:S(2)}) copy-start(s32[8]{0:T(128)S(1)} %select_reduce_fusion.order) | copy-start | bytes 100
  21.1 16.5 %collective-permute-start.1 = (s32[8]{0:T(128)S(1)}, s32[8]{0:T(128)S(1)}, u32[]{:S(2)}, u32[]{:S(2)}) collective-permute-start(s32[8]{0:T(128)S(1)} %select_reduce_fusion.order), channel_id=1, source_target_pairs={{0,4},{1,5},{2,6},{3,7},{4,8},{5,9},{6,10},{7,11},{8,12},{9,13},{1... | collective-permute-start | bytes 104 | tf_op jit(solution)/shard_map/ppermute | solution.py:278
  26.8 2.2 copy-start.23
  30.9 4.4 %copy-start.22 = (bf16[128,256]{1,0:T(8,128)(2,1)S(1)}, bf16[128,256]{1,0:T(8,128)(2,1)}, u32[]{:S(2)}) copy-start(bf16[128,256]{1,0:T(8,128)(2,1)} %param.10) | copy-start | bytes 196612
  37.6 1.3 copy-start.26
  46.7 6.8 %copy-start.11 = (bf16[8,6,2048]{2,1,0:T(8,128)(2,1)S(1)}, bf16[8,6,2048]{2,1,0:T(8,128)(2,1)}, u32[]{:S(2)}) copy-start(bf16[8,6,2048]{2,1,0:T(8,128)(2,1)} %get-tuple-element.150) | copy-start | bytes 589828
  46.7 53.2 %all-to-all-start.1 = ((bf16[8,32,2048]{2,1,0:T(8,128)(2,1)}), bf16[8,32,2048]{2,1,0:T(8,128)(2,1)S(1)}, u32[]{:S(2)}, u32[]{:S(2)}) async-start(bf16[8,32,2048]{2,1,0:T(8,128)(2,1)} %short_conv.4), calls=%async_computation.1 | async-start | bytes 2097152 | tf_op jit(solution)/shard_map/all_to_all | solution.py:305
  51.5 48.4 %collective-permute-start.3 = (bf16[512,1024]{1,0:T(8,128)(2,1)}, bf16[512,1024]{1,0:T(8,128)(2,1)S(1)}, u32[]{:S(2)}, u32[]{:S(2)}) collective-permute-start(bf16[512,1024]{1,0:T(8,128)(2,1)} %constant_dynamic-slice_fusion.1), channel_id=1, source_target_pairs={{0,4},{4,0},{1,5},{5,1},{2,6},{6,2},{3,7},{7,3},{8,12},{12,8},{9,1... | collective-permute-start | bytes 3145736 | tf_op jit(solution)/shard_map/ppermute | solution.py:373
  55.7 43.2 %collective-permute-start.2 = (bf16[48,6144]{1,0:T(8,128)(2,1)}, bf16[48,6144]{1,0:T(8,128)(2,1)S(1)}, u32[]{:S(2)}, u32[]{:S(2)}) collective-permute-start(bf16[48,6144]{1,0:T(8,128)(2,1)} %reshape.132), channel_id=1, source_target_pairs={{0,4},{1,5},{2,6},{3,7},{4,8},{5,9},{6,10},{7,11},{8,12},{9,13},{1... | collective-permute-start | bytes 1769480 | tf_op jit(solution)/shard_map/ppermute | solution.py:335
  99.9 20.8 %copy-start.9 = (bf16[512,1024]{1,0:T(8,128)(2,1)}, bf16[512,1024]{1,0:T(8,128)(2,1)S(1)}, u32[]{:S(2)}) copy-start(bf16[512,1024]{1,0:T(8,128)(2,1)S(1)} %collective-permute-done.3) | copy-start | bytes 3145732
  99.9 13.0 %copy-start.8 = (bf16[8,32,2048]{2,1,0:T(8,128)(2,1)}, bf16[8,32,2048]{2,1,0:T(8,128)(2,1)S(1)}, u32[]{:S(2)}) copy-start(bf16[8,32,2048]{2,1,0:T(8,128)(2,1)S(1)} %all-to-all-done.1) | copy-start | bytes 3145732
  100.0 40.5 %all-to-all-start.2 = ((bf16[8,32,2048]{2,1,0:T(8,128)(2,1)}), bf16[8,32,2048]{2,1,0:T(8,128)(2,1)S(1)}, u32[]{:S(2)}, u32[]{:S(2)}) async-start(bf16[8,32,2048]{2,1,0:T(8,128)(2,1)} %short_conv.5), calls=%async_computation.2 | async-start | bytes 2097152 | tf_op jit(solution)/shard_map/all_to_all | solution.py:305
  110.2 2.8 collective-permute-start.4
  113.0 0.7 copy-start.21
  120.8 16.2 %collective-permute-start.5 = (bf16[256,1024]{1,0:T(8,128)(2,1)}, bf16[256,1024]{1,0:T(8,128)(2,1)}, u32[]{:S(2)}, u32[]{:S(2)}) collective-permute-start(bf16[256,1024]{1,0:T(8,128)(2,1)} %medium_conv.4.refs_0_), channel_id=1, source_target_pairs={{0,4},{4,0},{1,5},{5,1},{2,6},{6,2},{3,7},{7,3},{8,12},{12,8},{9,1... | collective-permute-start | bytes 1572872 | tf_op jit(solution)/shard_map/ppermute | solution.py:393
  122.5 18.0 %collective-permute-start.6 = (bf16[256,1024]{1,0:T(8,128)(2,1)}, bf16[256,1024]{1,0:T(8,128)(2,1)S(1)}, u32[]{:S(2)}, u32[]{:S(2)}) collective-permute-start(bf16[256,1024]{1,0:T(8,128)(2,1)} %medium_conv.4.refs_0_), channel_id=1, source_target_pairs={{0,2},{2,0},{1,3},{3,1},{4,6},{6,4},{5,7},{7,5},{8,10},{10,8},{9,1... | collective-permute-start | bytes 1572872 | tf_op jit(solution)/shard_map/ppermute | solution.py:394
  137.0 9.0 %copy-start.10 = (bf16[512,1024]{1,0:T(8,128)(2,1)S(1)}, bf16[512,1024]{1,0:T(8,128)(2,1)}, u32[]{:S(2)}) copy-start(bf16[512,1024]{1,0:T(8,128)(2,1)} %copy-done.9) | copy-start | bytes 3145732
  140.5 0.8 copy-start.14
  140.5 6.3 %copy-start.7 = (bf16[8,32,2048]{2,1,0:T(8,128)(2,1)}, bf16[8,32,2048]{2,1,0:T(8,128)(2,1)S(1)}, u32[]{:S(2)}) copy-start(bf16[8,32,2048]{2,1,0:T(8,128)(2,1)S(1)} %all-to-all-done.2) | copy-start | bytes 3145732
  141.3 47.9 %all-to-all-start.3 = ((bf16[8,32,2048]{2,1,0:T(8,128)(2,1)}), bf16[8,32,2048]{2,1,0:T(8,128)(2,1)S(1)}, u32[]{:S(2)}, u32[]{:S(2)}) async-start(bf16[8,32,2048]{2,1,0:T(8,128)(2,1)} %short_conv.6), calls=%async_computation.3 | async-start | bytes 2097152 | tf_op jit(solution)/shard_map/all_to_all | solution.py:305
  145.9 83.6 %all-gather.9.cloned.1.call-start = ((), (), s32[]{:S(2)}) async-start(), calls=%async_computation.8 | async-start | bytes 2621440 | tf_op jit(solution)/shard_map/all_gather | solution.py:326
  146.8 2.6 collective-permute-start.8
  148.2 26.4 %collective-permute-start.7 = (bf16[256,1024]{1,0:T(8,128)(2,1)}, bf16[256,1024]{1,0:T(8,128)(2,1)S(1)}, u32[]{:S(2)}, u32[]{:S(2)}) collective-permute-start(bf16[256,1024]{1,0:T(8,128)(2,1)} %collective-permute-done.5.refs_2_), channel_id=1, source_target_pairs={{0,2},{2,0},{1,3},{3,1},{4,6},{6,4},{5,7},{7,5},{8,10},{10,8},{9,1... | collective-permute-start | bytes 1572872 | tf_op jit(solution)/shard_map/ppermute | solution.py:378
  149.5 0.7 copy-start.18
  157.2 17.4 %collective-permute-start.9 = (bf16[256,1024]{1,0:T(8,128)(2,1)}, bf16[256,1024]{1,0:T(8,128)(2,1)S(1)}, u32[]{:S(2)}, u32[]{:S(2)}) collective-permute-start(bf16[256,1024]{1,0:T(8,128)(2,1)} %medium_conv.5.refs_0_), channel_id=1, source_target_pairs={{0,4},{4,0},{1,5},{5,1},{2,6},{6,2},{3,7},{7,3},{8,12},{12,8},{9,1... | collective-permute-start | bytes 1572872 | tf_op jit(solution)/shard_map/ppermute | solution.py:393
  159.2 19.1 %collective-permute-start.10 = (bf16[256,1024]{1,0:T(8,128)(2,1)}, bf16[256,1024]{1,0:T(8,128)(2,1)S(1)}, u32[]{:S(2)}, u32[]{:S(2)}) collective-permute-start(bf16[256,1024]{1,0:T(8,128)(2,1)} %medium_conv.5.refs_0_), channel_id=1, source_target_pairs={{0,2},{2,0},{1,3},{3,1},{4,6},{6,4},{5,7},{7,5},{8,10},{10,8},{9,1... | collective-permute-start | bytes 1572872 | tf_op jit(solution)/shard_map/ppermute | solution.py:394
  174.6 14.6 %copy-start.16 = (bf16[256,1024]{1,0:T(8,128)(2,1)}, bf16[256,1024]{1,0:T(8,128)(2,1)S(1)}, u32[]{:S(2)}) copy-start(bf16[256,1024]{1,0:T(8,128)(2,1)S(1)} %collective-permute-done.7.refs_3_) | copy-start | bytes 1572868
  174.6 14.6 %copy-start.12 = (bf16[256,1024]{1,0:T(8,128)(2,1)}, bf16[256,1024]{1,0:T(8,128)(2,1)S(1)}, u32[]{:S(2)}) copy-start(bf16[256,1024]{1,0:T(8,128)(2,1)S(1)} %collective-permute-done.9.refs_2_) | copy-start | bytes 1572868
  178.2 11.0 %copy-start.13 = (bf16[256,1024]{1,0:T(8,128)(2,1)}, bf16[256,1024]{1,0:T(8,128)(2,1)S(1)}, u32[]{:S(2)}) copy-start(bf16[256,1024]{1,0:T(8,128)(2,1)S(1)} %collective-permute-done.10.refs_1_) | copy-start | bytes 1572868
  189.2 8.5 %copy-start.6 = (bf16[8,32,2048]{2,1,0:T(8,128)(2,1)}, bf16[8,32,2048]{2,1,0:T(8,128)(2,1)S(1)}, u32[]{:S(2)}) copy-start(bf16[8,32,2048]{2,1,0:T(8,128)(2,1)S(1)} %all-to-all-done.3) | copy-start | bytes 3145732
  193.4 36.1 %collective-permute-start.15 = (bf16[1024,1024]{1,0:T(8,128)(2,1)}, bf16[1024,1024]{1,0:T(8,128)(2,1)S(1)}, u32[]{:S(2)}, u32[]{:S(2)}) collective-permute-start(bf16[1024,1024]{1,0:T(8,128)(2,1)} %stack.79.refs_0_.refs_1_), channel_id=1, source_target_pairs={{0,1},{1,0},{2,3},{3,2},{4,5},{5,4},{6,7},{7,6},{8,9},{9,8},{10,11... | collective-permute-start | bytes 6291464 | tf_op jit(solution)/shard_map/ppermute | solution.py:366
  193.4 36.1 %all-to-all-start.4 = ((bf16[8,32,2048]{2,1,0:T(8,128)(2,1)}), bf16[8,32,2048]{2,1,0:T(8,128)(2,1)}, u32[]{:S(2)}, u32[]{:S(2)}) async-start(bf16[8,32,2048]{2,1,0:T(8,128)(2,1)} %short_conv.7), calls=%async_computation.4 | async-start | bytes 2097152 | tf_op jit(solution)/shard_map/all_to_all | solution.py:305
  197.7 113.0 %all-gather.11.cloned.1.call-start = ((), (), s32[]{:S(2)}) async-start(), calls=%async_computation.9 | async-start | bytes 5242880 | tf_op jit(solution)/shard_map/all_gather | solution.py:326
  197.7 31.8 %slice-start = ((bf16[512,1024]{1,0:T(8,128)(2,1)}), bf16[512,512]{1,0:T(8,128)(2,1)S(1)}, s32[]{:S(2)}) async-start(bf16[512,1024]{1,0:T(8,128)(2,1)} %constant_dynamic-slice_fusion.2), calls=%async_computation.10 | async-start | bytes 1048576 | tf_op jit(solution)/shard_map/slice | solution.py:310
  197.8 31.8 %slice-start.1 = ((bf16[512,1024]{1,0:T(8,128)(2,1)}), bf16[512,512]{1,0:T(8,128)(2,1)S(1)}, s32[]{:S(2)}) async-start(bf16[512,1024]{1,0:T(8,128)(2,1)} %copy-done.9), calls=%async_computation.11 | async-start | bytes 1048576 | tf_op jit(solution)/shard_map/slice | solution.py:310
  197.8 3.7 collective-permute-start.12
  200.3 16.8 %collective-permute-start.11 = (bf16[256,1024]{1,0:T(8,128)(2,1)}, bf16[256,1024]{1,0:T(8,128)(2,1)}, u32[]{:S(2)}, u32[]{:S(2)}) collective-permute-start(bf16[256,1024]{1,0:T(8,128)(2,1)} %copy-done.12), channel_id=1, source_target_pairs={{0,2},{2,0},{1,3},{3,1},{4,6},{6,4},{5,7},{7,5},{8,10},{10,8},{9,1... | collective-permute-start | bytes 1572872 | tf_op jit(solution)/shard_map/ppermute | solution.py:378
  201.5 0.7 copy-start.19
  209.2 20.3 %collective-permute-start.13 = (bf16[256,1024]{1,0:T(8,128)(2,1)}, bf16[256,1024]{1,0:T(8,128)(2,1)}, u32[]{:S(2)}, u32[]{:S(2)}) collective-permute-start(bf16[256,1024]{1,0:T(8,128)(2,1)} %medium_conv.6.refs_0_), channel_id=1, source_target_pairs={{0,4},{4,0},{1,5},{5,1},{2,6},{6,2},{3,7},{7,3},{8,12},{12,8},{9,1... | collective-permute-start | bytes 1572872 | tf_op jit(solution)/shard_map/ppermute | solution.py:393
  210.8 18.7 %collective-permute-start.14 = (bf16[256,1024]{1,0:T(8,128)(2,1)}, bf16[256,1024]{1,0:T(8,128)(2,1)}, u32[]{:S(2)}, u32[]{:S(2)}) collective-permute-start(bf16[256,1024]{1,0:T(8,128)(2,1)} %medium_conv.6.refs_0_), channel_id=1, source_target_pairs={{0,2},{2,0},{1,3},{3,1},{4,6},{6,4},{5,7},{7,5},{8,10},{10,8},{9,1... | collective-permute-start | bytes 1572872 | tf_op jit(solution)/shard_map/ppermute | solution.py:394
  229.5 1.7 copy-start.4
  231.2 14.8 %collective-permute-start.17 = (bf16[256,1024]{1,0:T(8,128)(2,1)}, bf16[256,1024]{1,0:T(8,128)(2,1)S(1)}, u32[]{:S(2)}, u32[]{:S(2)}) collective-permute-start(bf16[256,1024]{1,0:T(8,128)(2,1)} %collective-permute-done.13.refs_2_), channel_id=1, source_target_pairs={{0,2},{2,0},{1,3},{3,1},{4,6},{6,4},{5,7},{7,5},{8,10},{10,8},{9,1... | collective-permute-start | bytes 1572872 | tf_op jit(solution)/shard_map/ppermute | solution.py:378
  232.7 3.3 collective-permute-start.16
  236.0 0.7 copy-start.20
  246.0 16.5 %copy-start.15 = (bf16[256,1024]{1,0:T(8,128)(2,1)}, bf16[256,1024]{1,0:T(8,128)(2,1)S(1)}, u32[]{:S(2)}) copy-start(bf16[256,1024]{1,0:T(8,128)(2,1)S(1)} %collective-permute-done.17.refs_3_) | copy-start | bytes 1572868
  246.0 12.4 %collective-permute-start.18 = (bf16[256,1024]{1,0:T(8,128)(2,1)}, bf16[256,1024]{1,0:T(8,128)(2,1)S(1)}, u32[]{:S(2)}, u32[]{:S(2)}) collective-permute-start(bf16[256,1024]{1,0:T(8,128)(2,1)} %medium_conv.7.refs_0_), channel_id=1, source_target_pairs={{0,4},{4,0},{1,5},{5,1},{2,6},{6,2},{3,7},{7,3},{8,12},{12,8},{9,1... | collective-permute-start | bytes 1572872 | tf_op jit(solution)/shard_map/ppermute | solution.py:382
  246.0 34.0 %collective-permute-start.19 = (bf16[256,1024]{1,0:T(8,128)(2,1)}, bf16[256,1024]{1,0:T(8,128)(2,1)}, u32[]{:S(2)}, u32[]{:S(2)}) collective-permute-start(bf16[256,1024]{1,0:T(8,128)(2,1)} %medium_conv.7.refs_0_), channel_id=1, source_target_pairs={{0,2},{2,0},{1,3},{3,1},{4,6},{6,4},{5,7},{7,5},{8,10},{10,8},{9,1... | collective-permute-start | bytes 1572872 | tf_op jit(solution)/shard_map/ppermute | solution.py:383
  257.0 23.0 %collective-permute-start.20 = (bf16[256,1024]{1,0:T(8,128)(2,1)}, bf16[256,1024]{1,0:T(8,128)(2,1)}, u32[]{:S(2)}, u32[]{:S(2)}) collective-permute-start(bf16[256,1024]{1,0:T(8,128)(2,1)} %medium_conv.7.refs_0_), channel_id=1, source_target_pairs={{0,6},{2,4},{4,2},{6,0},{1,7},{3,5},{5,3},{7,1},{8,14},{10,12},{12... | collective-permute-start | bytes 1572872 | tf_op jit(solution)/shard_map/ppermute | solution.py:385
  258.3 4.1 %copy-start.17 = (bf16[256,1024]{1,0:T(8,128)(2,1)}, bf16[256,1024]{1,0:T(8,128)(2,1)S(1)}, u32[]{:S(2)}) copy-start(bf16[256,1024]{1,0:T(8,128)(2,1)S(1)} %collective-permute-done.18.refs_2_) | copy-start | bytes 1572868
  262.5 22.0 %collective-permute-start.21 = (bf16[1024,1024]{1,0:T(8,128)(2,1)}, bf16[1024,1024]{1,0:T(8,128)(2,1)S(1)}, u32[]{:S(2)}, u32[]{:S(2)}) collective-permute-start(bf16[1024,1024]{1,0:T(8,128)(2,1)} %stack.80.refs_2_.refs_3_), channel_id=1, source_target_pairs={{0,1},{1,0},{2,3},{3,2},{4,5},{5,4},{6,7},{7,6},{8,9},{9,8},{10,11... | collective-permute-start | bytes 6291464 | tf_op jit(solution)/shard_map/ppermute | solution.py:366
  273.5 11.0 %collective-permute-start.22 = (bf16[1024,1024]{1,0:T(8,128)(2,1)}, bf16[1024,1024]{1,0:T(8,128)(2,1)}, u32[]{:S(2)}, u32[]{:S(2)}) collective-permute-start(bf16[1024,1024]{1,0:T(8,128)(2,1)} %stack.81.refs_4_.refs_5_), channel_id=1, source_target_pairs={{0,1},{1,0},{2,3},{3,2},{4,5},{5,4},{6,7},{7,6},{8,9},{9,8},{10,11... | collective-permute-start | bytes 6291464 | tf_op jit(solution)/shard_map/ppermute | solution.py:366
  283.9 4.5 %collective-permute-start.23 = (bf16[1024,1024]{1,0:T(8,128)(2,1)}, bf16[1024,1024]{1,0:T(8,128)(2,1)}, u32[]{:S(2)}, u32[]{:S(2)}) collective-permute-start(bf16[1024,1024]{1,0:T(8,128)(2,1)} %stack.82.refs_6_.refs_7_), channel_id=1, source_target_pairs={{0,1},{1,0},{2,3},{3,2},{4,5},{5,4},{6,7},{7,6},{8,9},{9,8},{10,11... | collective-permute-start | bytes 6291464 | tf_op jit(solution)/shard_map/ppermute | solution.py:366
  284.5 3.9 %copy-start.5 = (bf16[1024,1024]{1,0:T(8,128)(2,1)}, bf16[1024,1024]{1,0:T(8,128)(2,1)S(1)}, u32[]{:S(2)}) copy-start(bf16[1024,1024]{1,0:T(8,128)(2,1)S(1)} %collective-permute-done.21.refs_10_.refs_11_) | copy-start | bytes 6291460
  305.9 29.2 %all-to-all-start.5 = ((bf16[8,256,512]{2,1,0:T(8,128)(2,1)}), bf16[8,256,512]{2,1,0:T(8,128)(2,1)S(1)}, u32[]{:S(2)}, u32[]{:S(2)}) async-start(bf16[8,256,512]{2,1,0:T(8,128)(2,1)} %bitcast.82), calls=%async_computation.5 | async-start | bytes 4194304 | tf_op jit(solution)/shard_map/all_to_all | solution.py:412
  335.1 1.3 copy-start.2
  336.5 29.6 %copy-start.3 = (bf16[8,256,512]{2,1,0:T(8,128)(2,1)S(1)}, bf16[8,256,512]{2,1,0:T(8,128)(2,1)}, u32[]{:S(2)}) copy-start(bf16[8,256,512]{2,1,0:T(8,128)(2,1)} %copy-done.2) | copy-start | bytes 6291460
  366.1 3.5 copy-start.1
Sparse Core Ops, SparseCore 0:
  26.0 65.1 all-gather.6
  148.3 63.2 all-gather.8
  231.3 79.3 all-gather.10

commit v3 on v2

--- a/solution.py
+++ b/solution.py
@@ -125,64 +125,65 @@
     )(routed, routed, halo, taps, same)
 
 
-def project_kernel(count, full, side, dest, *refs):
-    pieces, panels, sums, out = refs[:count], refs[count : count + 2], refs[count + 2 : -1], refs[-1]
-    held, depth = pieces[0].shape
+def project_kernel(count, depth, side, dest, *refs):
+    pieces, panels, (out, held, sems) = refs[:count], refs[count : count + 2], refs[count + 2 :]
+    rows, wide = pieces[0].shape
     tile = out.shape[0] // dest.shape[0]
+    pairs = wide // (2 * depth)
+    first = pl.program_id(0) == 0
+    copies = [pltpu.make_async_copy(p, held.at[j], sems.at[j]) for j, p in enumerate(pieces)]
+
+    @pl.when(first)
+    def _():
+        for copy in copies:
+            copy.start()
+
     for half in range(2):
-        rows = slice(half * held, (half + 1) * held)
-        total = sums[0][rows] if sums else None
-        for m, piece in enumerate(pieces[half * count // 2 : (half + 1) * count // 2]):
-            i, other = m // 2, m % 2
-            term = jnp.dot(piece[...], panels[other][i], preferred_element_type=jnp.float32)
-            total = term if total is None else total + term
-        if not full:
-            out[rows] = total
-            continue
+        total = None
+        for j in range(count // 2):
+            m = half * (count // 2) + j
+            pl.when(first)(copies[m].wait)
+            for i in range(pairs):
+                for other in range(2):
+                    at = pl.multiple_of((2 * i + (side[0] + other) % 2) * depth, depth)
+                    term = jnp.dot(
+                        held[m, :, pl.ds(at, depth)],
+                        panels[other][j * pairs + i],
+                        preferred_element_type=jnp.float32,
+                    )
+                    total = term if total is None else total + term
         total = total.astype(jnp.bfloat16)
-        for m in range(held // tile):
-            at = pl.multiple_of(dest[half * held // tile + m] * tile, tile)
+        for m in range(rows // tile):
+            at = pl.multiple_of(dest[half * rows // tile + m] * tile, tile)
             out[pl.ds(at, tile)] = total[m * tile : (m + 1) * tile]
 
 
-def project_call(side, dest, here, there, panels, cols, depth, first, sums):
-    held, wide = here[0].shape
+def project_call(side, dest, here, there, panels, cols, depth):
+    rows, wide = here[0].shape
     tile = min(256, cols)
-    rows = len(here) * wide // 2 // depth
-    full = first + len(here) == CHUNKS
-
-    def specs():
-        for i in range(wide // (2 * depth)):
-            for other in range(2):
-                yield pl.BlockSpec(
-                    (held, depth),
-                    lambda n, s, d, i=i, other=other: (0, 2 * i + (s[0] + other) % 2),
-                    pipeline_mode=pl.Buffered(1),
-                )
-
-    at_rows = first * wide // 2 // depth // rows
-    pieces = [x for x in list(here) + list(there) for _ in range(wide // depth)]
-    given = [] if sums is None else [sums]
+    pieces = list(here) + list(there)
+    held = len(here) * wide // 2 // depth
     return pl.pallas_call(
-        functools.partial(project_kernel, len(pieces), full),
+        functools.partial(project_kernel, len(pieces), depth),
         grid_spec=pltpu.PrefetchScalarGridSpec(
             num_scalar_prefetch=2,
             grid=(cols // tile,),
-            in_specs=[spec for _ in list(here) + list(there) for spec in specs()]
+            in_specs=[pl.BlockSpec(memory_space=pl.ANY) for _ in pieces]
             + [
-                pl.BlockSpec(
-                    (rows, depth, tile), lambda n, s, d, row=row, at=at // tile: (at_rows, row, at + n)
-                )
+                pl.BlockSpec((held, depth, tile), lambda n, s, d, row=row, at=at // tile: (0, row, at + n))
                 for _, row, at in panels
-            ]
-            + [pl.BlockSpec((2 * held, tile), lambda n, s, d: (0, n)) for _ in given],
-            out_specs=pl.BlockSpec((2 * held, tile), lambda n, s, d: (0, n)),
+            ],
+            out_specs=pl.BlockSpec((2 * rows, tile), lambda n, s, d: (0, n)),
+            scratch_shapes=[
+                pltpu.VMEM((len(pieces), rows, wide), jnp.bfloat16),
+                pltpu.SemaphoreType.DMA((len(pieces),)),
+            ],
         ),
-        out_shape=jax.ShapeDtypeStruct((2 * held, cols), jnp.bfloat16 if full else jnp.float32),
+        out_shape=jax.ShapeDtypeStruct((2 * rows, cols), jnp.bfloat16),
         compiler_params=pltpu.CompilerParams(vmem_limit_bytes=56 * MIB),
         cost_estimate=LIGHT,
         name="project",
-    )(side, dest, *pieces, *(p for p, _, _ in panels), *given)
+    )(side, dest, *pieces, *(p for p, _, _ in panels))
 
 
 def stack_kernel(*refs):
@@ -355,7 +356,7 @@
                     panels.append((held[key], row, (first - key[1]) * unit))
         here, there = ([held[k, j] for j in range(low, high)] for k in ("here", "there"))
         depth = out_weight.shape[0]
-        return project_call(side, dest, here, there, panels, unit * wide, depth, low, sums)
+        return project_call(side, dest, here, there, panels, unit * wide, depth)
 
 
     def stack_steps(step, j):

time: 380 us -> 387 us (1.018)
  Pallas kernels: 114 us -> 126 us
  waiting for transfers between devices: 87.9 us -> 80.7 us
    pallas_call x2, Pallas kernels: 34.8 us -> 46.8 us  [project_call(): pl.pallas_call(functools.partial(project_kernel, len(pieces), depth), gri...]
    all_to_all x1, waiting for transfers between devices: 7.09 us -> 2.19 us  [on_device(): lax.all_to_all(given, PLANE, split_axis=0, concat_axis=0, tiled=True)]
  transfers between devices with their start and end apart: 33 -> 33, of which waited for: 13 -> 12; matrix products, arithmetic and copies ran while one was open for 5% -> 5% of each run, Pallas kernels for 29% -> 32%
where the time goes in v3:
time: 387 us; the launch traced here: 383 us
  Pallas kernels  126 us (33%)
  starting transfers between devices  100 us (26%)
  waiting for transfers between devices  80.7 us (21%)
  blocking collectives  29.6 us (8%)
  local copies, waits for them, and re-layouts  27.6 us (7%)
  between operations  13.5 us (3%)
  other arithmetic  4.81 us (1%)
    pallas_call x2, Pallas kernels, project_call(): pl.pallas_call(functools.partial(project_kernel, len(pieces), depth), gri...  46.8 us
    ppermute x1, waiting for transfers between devices, on_device(): lax.ppermute(after(tails[1], tails[0]), EVERY, shift)  33.4 us
    pallas_call x4, Pallas kernels, short_call(): pl.pallas_call(short_kernel, grid_spec=pltpu.PrefetchScalarGridSpec(num_s...  31.3 us
    all_to_all x1, blocking collectives, on_device(): lax.all_to_all(given, PLANE, split_axis=0, concat_axis=0, tiled=True)  29.6 us
    pallas_call x4, Pallas kernels, medium_call(): pl.pallas_call(functools.partial(medium_kernel, group_size), grid=(steps,...  28.2 us
    all_to_all x4, starting transfers between devices, exchange(): routed = lax.all_to_all(sent, FSDP, split_axis=0, concat_axis=0, tiled=True)  23.4 us
    ppermute x3, starting transfers between devices, on_device(): flying['by_y', j] = (step, lax.ppermute(gated, 'y', SWAP))  20.4 us
    pallas_call x4, Pallas kernels, stack_call(): pl.pallas_call(stack_kernel, grid=(cols // tile,), in_specs=[pl.BlockSpec...  16.3 us
  transfers between devices with their start and end apart: 33, of which 12 were waited for; matrix products, arithmetic and copies ran while one was open for 5% of the time, Pallas kernels for 32%

profile of v3, /device:TPU:0, one launch (start us, length us, event | category | flops | bytes accessed | tf_op | source)
XLA Modules:
  0.0 382.5 jit_solution(2086137221142400917)
XLA Ops:
  6.5 2.6 fusion.12
  9.3 1.0 reshape.129
  10.4 5.7 %collective-permute-start = (bf16[48,6144]{1,0:T(8,128)(2,1)}, bf16[48,6144]{1,0:T(8,128)(2,1)}, u32[]{:S(2)}, u32[]{:S(2)}) collective-permute-start(bf16[48,6144]{1,0:T(8,128)(2,1)} %reshape.129), channel_id=1, source_target_pairs={{0,4},{1,5},{2,6},{3,7},{4,8},{5,9},{6,10},{7,11},{8,12},{9,13},{1... | collective-permute-start | bytes 1769480 | tf_op jit(solution)/shard_map/ppermute | solution.py:274
  16.8 4.1 %all-to-all-start = ((s32[8,1,38]{2,1,0:T(1,128)}), s32[8,1,38]{2,1,0:T(1,128)S(1)}, u32[]{:S(2)}, u32[]{:S(2)}) async-start(s32[8,1,38]{2,1,0:T(1,128)} %bitcast.13), calls=%async_computation | async-start | bytes 8192 | tf_op jit(solution)/shard_map/all_to_all | solution.py:281
  21.1 3.9 %collective-permute-start.1 = (s32[8]{0:T(128)S(1)}, s32[8]{0:T(128)S(1)}, u32[]{:S(2)}, u32[]{:S(2)}) collective-permute-start(s32[8]{0:T(128)S(1)} %select_reduce_fusion.order), channel_id=1, source_target_pairs={{0,4},{1,5},{2,6},{3,7},{4,8},{5,9},{6,10},{7,11},{8,12},{9,13},{1... | collective-permute-start | bytes 104 | tf_op jit(solution)/shard_map/ppermute | solution.py:279
  26.9 1.1 constant_dynamic-slice_fusion.1
  27.9 2.0 broadcast_in_dim.33
  29.9 4.3 %reshape.131.fq.fk.fv = f32[7,12288]{1,0:T(8,128)} reshape(f32[7,768,16]{2,1,0:T(8,128)} %broadcast_in_dim.33) | data formatting | bytes 688128 | tf_op jit(solution)/shard_map/reshape | solution.py:284
  35.4 2.2 reshape.130.hq.hk.hv
  38.9 7.8 %short_conv.4 = bf16[8,32,2048]{2,1,0:T(8,128)(2,1)} custom-call(s32[8]{0:T(128)} %copy-done.26, s32[8]{0:T(128)} %copy-done.27, bf16[8,32,12288]{2,1,0:T(8,128)(2,1)} %bitcast.59, bf16[8,32,12288]{2,1,0:T(8,128)(2,1)} %bitcast.60, bf16[8,32,12288]{2,1,0:T(8,128)(2,1)} %bitcast.61, bf16[8,6,6144]{2,1,0:T(8,128)(2,1)} %reshape.130.hq.hk.hv, ...), custom_call_target="tpu_custom_call" | custom-call | flops 1 | bytes 1 | tf_op jit(solution)/shard_map/short_conv/pallas_call | solution.py:70
  46.8 4.8 %all-to-all-start.1 = ((bf16[8,32,2048]{2,1,0:T(8,128)(2,1)}), bf16[8,32,2048]{2,1,0:T(8,128)(2,1)S(1)}, u32[]{:S(2)}, u32[]{:S(2)}) async-start(bf16[8,32,2048]{2,1,0:T(8,128)(2,1)} %short_conv.4), calls=%async_computation.1 | async-start | bytes 2097152 | tf_op jit(solution)/shard_map/all_to_all | solution.py:306
  51.6 2.0 collective-permute-start.3
  53.6 1.1 pad_maximum_fusion.2
  54.7 1.0 reshape.132
  55.7 2.0 collective-permute-start.2
  57.7 7.8 %short_conv.5 = bf16[8,32,2048]{2,1,0:T(8,128)(2,1)} custom-call(s32[8]{0:T(128)} %copy-done.26, s32[8]{0:T(128)} %copy-done.27, bf16[8,32,12288]{2,1,0:T(8,128)(2,1)} %bitcast.62, bf16[8,32,12288]{2,1,0:T(8,128)(2,1)} %bitcast.63, bf16[8,32,12288]{2,1,0:T(8,128)(2,1)} %bitcast.64, bf16[8,6,6144]{2,1,0:T(8,128)(2,1)} %reshape.130.hq.hk.hv, ...), custom_call_target="tpu_custom_call" | custom-call | flops 1 | bytes 1 | tf_op jit(solution)/shard_map/short_conv/pallas_call | solution.py:70
  65.5 33.4 %collective-permute-done.2 = bf16[48,6144]{1,0:T(8,128)(2,1)S(1)} collective-permute-done((bf16[48,6144]{1,0:T(8,128)(2,1)}, bf16[48,6144]{1,0:T(8,128)(2,1)S(1)}, u32[]{:S(2)}, u32[]{:S(2)}) %collective-permute-start.2) | collective-permute-done | bytes 589856 | tf_op jit(solution)/shard_map/ppermute | solution.py:336
  99.0 1.1 reshape.133.hq.hk.hv
  100.1 10.1 %all-to-all-start.2 = ((bf16[8,32,2048]{2,1,0:T(8,128)(2,1)}), bf16[8,32,2048]{2,1,0:T(8,128)(2,1)S(1)}, u32[]{:S(2)}, u32[]{:S(2)}) async-start(bf16[8,32,2048]{2,1,0:T(8,128)(2,1)} %short_conv.5), calls=%async_computation.2 | async-start | bytes 2097152 | tf_op jit(solution)/shard_map/all_to_all | solution.py:306
  110.2 1.6 collective-permute-start.4
  111.8 1.1 collective-permute-done.4.halo
  113.7 7.0 %medium_conv.4.refs_0_ = bf16[256,1024]{1,0:T(8,128)(2,1)} custom-call(bf16[256,2048]{1,0:T(8,128)(2,1)} %bitcast.83, bf16[256,2048]{1,0:T(8,128)(2,1)} %bitcast.84, bf16[128,1024]{1,0:T(8,128)(2,1)} %copy-done.22, f32[256,256]{1,0:T(8,128)} %pad.6.taps, bf16[2,128,256]{2,1,0:T(8,128)(2,1)} %add_convert_fusion.same), custom_call_target="tpu_custom_call" | custom-call | flops 1 | bytes 1 | tf_op jit(solution)/shard_map/medium_conv/pallas_call | solution.py:111
  120.7 1.9 collective-permute-start.5
  122.6 6.4 %collective-permute-start.6 = (bf16[256,1024]{1,0:T(8,128)(2,1)}, bf16[256,1024]{1,0:T(8,128)(2,1)S(1)}, u32[]{:S(2)}, u32[]{:S(2)}) collective-permute-start(bf16[256,1024]{1,0:T(8,128)(2,1)} %medium_conv.4.refs_0_), channel_id=1, source_target_pairs={{0,2},{2,0},{1,3},{3,1},{4,6},{6,4},{5,7},{7,5},{8,10},{10,8},{9,1... | collective-permute-start | bytes 1572872 | tf_op jit(solution)/shard_map/ppermute | solution.py:395
  129.1 7.8 %short_conv.6 = bf16[8,32,2048]{2,1,0:T(8,128)(2,1)} custom-call(s32[8]{0:T(128)} %copy-done.26, s32[8]{0:T(128)} %copy-done.27, bf16[8,32,12288]{2,1,0:T(8,128)(2,1)} %bitcast.65, bf16[8,32,12288]{2,1,0:T(8,128)(2,1)} %bitcast.66, bf16[8,32,12288]{2,1,0:T(8,128)(2,1)} %bitcast.67, bf16[8,6,6144]{2,1,0:T(8,128)(2,1)} %reshape.133.hq.hk.hv, ...), custom_call_target="tpu_custom_call" | custom-call | flops 1 | bytes 1 | tf_op jit(solution)/shard_map/short_conv/pallas_call | solution.py:70
  136.9 3.6 collective-permute-done.6.refs_1_
  141.3 4.6 %all-to-all-start.3 = ((bf16[8,32,2048]{2,1,0:T(8,128)(2,1)}), bf16[8,32,2048]{2,1,0:T(8,128)(2,1)S(1)}, u32[]{:S(2)}, u32[]{:S(2)}) async-start(bf16[8,32,2048]{2,1,0:T(8,128)(2,1)} %short_conv.6), calls=%async_computation.3 | async-start | bytes 2097152 | tf_op jit(solution)/shard_map/all_to_all | solution.py:306
  145.9 1.9 slice.134
  147.8 1.3 collective-permute-start.8
  149.1 1.3 collective-permute-start.7
  151.2 7.1 %medium_conv.5.refs_0_ = bf16[256,1024]{1,0:T(8,128)(2,1)} custom-call(bf16[256,2048]{1,0:T(8,128)(2,1)} %bitcast.80, bf16[256,2048]{1,0:T(8,128)(2,1)} %bitcast.81, bf16[128,1024]{1,0:T(8,128)(2,1)} %copy-done.19, f32[256,256]{1,0:T(8,128)} %pad.6.taps, bf16[2,128,256]{2,1,0:T(8,128)(2,1)} %add_convert_fusion.same), custom_call_target="tpu_custom_call" | custom-call | flops 1 | bytes 1 | tf_op jit(solution)/shard_map/medium_conv/pallas_call | solution.py:111
  158.3 2.0 collective-permute-start.9
  160.2 7.6 %collective-permute-start.10 = (bf16[256,1024]{1,0:T(8,128)(2,1)}, bf16[256,1024]{1,0:T(8,128)(2,1)S(1)}, u32[]{:S(2)}, u32[]{:S(2)}) collective-permute-start(bf16[256,1024]{1,0:T(8,128)(2,1)} %medium_conv.5.refs_0_), channel_id=1, source_target_pairs={{0,2},{2,0},{1,3},{3,1},{4,6},{6,4},{5,7},{7,5},{8,10},{10,8},{9,1... | collective-permute-start | bytes 1572872 | tf_op jit(solution)/shard_map/ppermute | solution.py:395
  167.8 7.8 %short_conv.7 = bf16[8,32,2048]{2,1,0:T(8,128)(2,1)} custom-call(s32[8]{0:T(128)} %copy-done.26, s32[8]{0:T(128)} %copy-done.27, bf16[8,32,12288]{2,1,0:T(8,128)(2,1)} %bitcast.68, bf16[8,32,12288]{2,1,0:T(8,128)(2,1)} %bitcast.69, bf16[8,32,12288]{2,1,0:T(8,128)(2,1)} %bitcast.70, bf16[8,6,6144]{2,1,0:T(8,128)(2,1)} %reshape.133.hq.hk.hv, ...), custom_call_target="tpu_custom_call" | custom-call | flops 1 | bytes 1 | tf_op jit(solution)/shard_map/short_conv/pallas_call | solution.py:70
  175.7 3.5 collective-permute-done.10.refs_1_
  179.2 10.0 %all-to-all-done.3 = bf16[8,32,2048]{2,1,0:T(8,128)(2,1)S(1)} async-done(((bf16[8,32,2048]{2,1,0:T(8,128)(2,1)}), bf16[8,32,2048]{2,1,0:T(8,128)(2,1)S(1)}, u32[]{:S(2)}, u32[]{:S(2)}) %all-to-all-start.3) | async-done | bytes 1048608 | tf_op jit(solution)/shard_map/all_to_all | solution.py:306
  189.3 4.2 %stack.79.refs_0_ = bf16[1024,1024]{1,0:T(8,128)(2,1)} custom-call(bf16[256,1024]{1,0:T(8,128)(2,1)} %medium_conv.4.refs_0_, bf16[256,1024]{1,0:T(8,128)(2,1)} %copy-done.16, bf16[256,1024]{1,0:T(8,128)(2,1)} %copy-done.15, bf16[256,1024]{1,0:T(8,128)(2,1)} %collective-permute-done.7.refs_3_), custom_call_target="tpu_custom_call" | custom-call | flops 1 | bytes 1 | tf_op jit(solution)/shard_map/stack/pallas_call | solution.py:199
  193.6 4.0 %all-to-all-start.4 = ((bf16[8,32,2048]{2,1,0:T(8,128)(2,1)}), bf16[8,32,2048]{2,1,0:T(8,128)(2,1)S(1)}, u32[]{:S(2)}, u32[]{:S(2)}) async-start(bf16[8,32,2048]{2,1,0:T(8,128)(2,1)} %short_conv.7), calls=%async_computation.4 | async-start | bytes 2097152 | tf_op jit(solution)/shard_map/all_to_all | solution.py:306
  197.6 2.1 collective-permute-start.12
  199.8 1.1 collective-permute-done.12.halo
  201.6 7.0 %medium_conv.6.refs_0_ = bf16[256,1024]{1,0:T(8,128)(2,1)} custom-call(bf16[256,2048]{1,0:T(8,128)(2,1)} %bitcast.74, bf16[256,2048]{1,0:T(8,128)(2,1)} %bitcast.75, bf16[128,1024]{1,0:T(8,128)(2,1)} %copy-done.20, f32[256,256]{1,0:T(8,128)} %pad.6.taps, bf16[2,128,256]{2,1,0:T(8,128)(2,1)} %add_convert_fusion.same), custom_call_target="tpu_custom_call" | custom-call | flops 1 | bytes 1 | tf_op jit(solution)/shard_map/medium_conv/pallas_call | solution.py:111
  208.6 1.7 collective-permute-start.13
  210.3 6.4 %collective-permute-start.14 = (bf16[256,1024]{1,0:T(8,128)(2,1)}, bf16[256,1024]{1,0:T(8,128)(2,1)}, u32[]{:S(2)}, u32[]{:S(2)}) collective-permute-start(bf16[256,1024]{1,0:T(8,128)(2,1)} %medium_conv.6.refs_0_), channel_id=1, source_target_pairs={{0,2},{2,0},{1,3},{3,1},{4,6},{6,4},{5,7},{7,5},{8,10},{10,8},{9,1... | collective-permute-start | bytes 1572872 | tf_op jit(solution)/shard_map/ppermute | solution.py:395
  216.7 11.6 %collective-permute-done.13.refs_2_ = bf16[256,1024]{1,0:T(8,128)(2,1)S(1)} collective-permute-done((bf16[256,1024]{1,0:T(8,128)(2,1)}, bf16[256,1024]{1,0:T(8,128)(2,1)S(1)}, u32[]{:S(2)}, u32[]{:S(2)}) %collective-permute-start.13) | collective-permute-done | bytes 524320 | tf_op jit(solution)/shard_map/ppermute | solution.py:394
  229.1 1.1 slice.138
  230.3 1.0 pad_maximum_fusion
  232.4 2.3 collective-permute-start.16
  236.3 7.1 %medium_conv.7.refs_0_ = bf16[256,1024]{1,0:T(8,128)(2,1)} custom-call(bf16[256,2048]{1,0:T(8,128)(2,1)} %bitcast.77, bf16[256,2048]{1,0:T(8,128)(2,1)} %bitcast.78, bf16[128,1024]{1,0:T(8,128)(2,1)} %copy-done.21, f32[256,256]{1,0:T(8,128)} %pad.6.taps, bf16[2,128,256]{2,1,0:T(8,128)(2,1)} %add_convert_fusion.same), custom_call_target="tpu_custom_call" | custom-call | flops 1 | bytes 1 | tf_op jit(solution)/shard_map/medium_conv/pallas_call | solution.py:111
  243.5 2.7 collective-permute-done.17.refs_3_
  246.3 11.1 %collective-permute-start.19 = (bf16[256,1024]{1,0:T(8,128)(2,1)}, bf16[256,1024]{1,0:T(8,128)(2,1)}, u32[]{:S(2)}, u32[]{:S(2)}) collective-permute-start(bf16[256,1024]{1,0:T(8,128)(2,1)} %medium_conv.7.refs_0_), channel_id=1, source_target_pairs={{0,2},{2,0},{1,3},{3,1},{4,6},{6,4},{5,7},{7,5},{8,10},{10,8},{9,1... | collective-permute-start | bytes 1572872 | tf_op jit(solution)/shard_map/ppermute | solution.py:384
  257.4 1.4 collective-permute-start.20
  258.8 4.1 %stack.80.refs_1_ = bf16[1024,1024]{1,0:T(8,128)(2,1)} custom-call(bf16[256,1024]{1,0:T(8,128)(2,1)} %medium_conv.5.refs_0_, bf16[256,1024]{1,0:T(8,128)(2,1)} %copy-done.11, bf16[256,1024]{1,0:T(8,128)(2,1)} %copy-done.10, bf16[256,1024]{1,0:T(8,128)(2,1)} %copy-done.12), custom_call_target="tpu_custom_call" | custom-call | flops 1 | bytes 1 | tf_op jit(solution)/shard_map/stack/pallas_call | solution.py:199
  262.9 7.0 %collective-permute-start.21 = (bf16[1024,1024]{1,0:T(8,128)(2,1)}, bf16[1024,1024]{1,0:T(8,128)(2,1)S(1)}, u32[]{:S(2)}, u32[]{:S(2)}) collective-permute-start(bf16[1024,1024]{1,0:T(8,128)(2,1)} %stack.80.refs_1_), channel_id=1, source_target_pairs={{0,1},{1,0},{2,3},{3,2},{4,5},{5,4},{6,7},{7,6},{8,9},{9,8},{10,11... | collective-permute-start | bytes 6291464 | tf_op jit(solution)/shard_map/ppermute | solution.py:367
  269.9 4.0 %stack.81.refs_2_ = bf16[1024,1024]{1,0:T(8,128)(2,1)} custom-call(bf16[256,1024]{1,0:T(8,128)(2,1)} %medium_conv.6.refs_0_, bf16[256,1024]{1,0:T(8,128)(2,1)} %collective-permute-done.14.refs_1_, bf16[256,1024]{1,0:T(8,128)(2,1)} %copy-done.13, bf16[256,1024]{1,0:T(8,128)(2,1)} %copy-done.17), custom_call_target="tpu_custom_call" | custom-call | flops 1 | bytes 1 | tf_op jit(solution)/shard_map/stack/pallas_call | solution.py:199
  273.9 6.4 %collective-permute-done.19.refs_1_ = bf16[256,1024]{1,0:T(8,128)(2,1)} collective-permute-done((bf16[256,1024]{1,0:T(8,128)(2,1)}, bf16[256,1024]{1,0:T(8,128)(2,1)}, u32[]{:S(2)}, u32[]{:S(2)}) %collective-permute-start.19) | collective-permute-done | bytes 524320 | tf_op jit(solution)/shard_map/ppermute | solution.py:384
  280.4 4.0 %stack.82.refs_3_ = bf16[1024,1024]{1,0:T(8,128)(2,1)} custom-call(bf16[256,1024]{1,0:T(8,128)(2,1)} %medium_conv.7.refs_0_, bf16[256,1024]{1,0:T(8,128)(2,1)} %collective-permute-done.19.refs_1_, bf16[256,1024]{1,0:T(8,128)(2,1)} %copy-done.18, bf16[256,1024]{1,0:T(8,128)(2,1)} %collective-permute-done.20.refs_3_), custom_call_target="tpu_custom_call" | custom-call | flops 1 | bytes 1 | tf_op jit(solution)/shard_map/stack/pallas_call | solution.py:199
  284.9 4.0 %collective-permute-done.23.refs_7_ = bf16[1024,1024]{1,0:T(8,128)(2,1)} collective-permute-done((bf16[1024,1024]{1,0:T(8,128)(2,1)}, bf16[1024,1024]{1,0:T(8,128)(2,1)}, u32[]{:S(2)}, u32[]{:S(2)}) %collective-permute-start.23) | collective-permute-done | bytes 2097184 | tf_op jit(solution)/shard_map/ppermute | solution.py:367
  288.8 23.4 %project.2 = bf16[2048,512]{1,0:T(8,128)(2,1)} custom-call(s32[1]{0:T(128)} %bitcast.side, s32[8]{0:T(128)} %fusion.11.dest, bf16[1024,1024]{1,0:T(8,128)(2,1)} %stack.79.refs_0_, bf16[1024,1024]{1,0:T(8,128)(2,1)} %stack.80.refs_1_, bf16[1024,1024]{1,0:T(8,128)(2,1)} %stack.81.refs_2_, bf16[1024,1024]{1,0:T(8,128)(2,1)} %stack.82.refs_3_, ...), custom_call_target="tpu_custom_call" | custom-call | flops 1 | bytes 1 | tf_op jit(solution)/shard_map/project/pallas_call | solution.py:166
  312.3 3.6 all-to-all-start.5
  315.9 23.4 %project.3 = bf16[2048,512]{1,0:T(8,128)(2,1)} custom-call(s32[1]{0:T(128)} %bitcast.side, s32[8]{0:T(128)} %fusion.11.dest, bf16[1024,1024]{1,0:T(8,128)(2,1)} %stack.79.refs_0_, bf16[1024,1024]{1,0:T(8,128)(2,1)} %stack.80.refs_1_, bf16[1024,1024]{1,0:T(8,128)(2,1)} %stack.81.refs_2_, bf16[1024,1024]{1,0:T(8,128)(2,1)} %stack.82.refs_3_, ...), custom_call_target="tpu_custom_call" | custom-call | flops 1 | bytes 1 | tf_op jit(solution)/shard_map/project/pallas_call | solution.py:166
  339.3 2.2 all-to-all-done.5.refs_0_
  341.5 1.3 copy-done.2
  342.8 29.6 %all_to_all.42.refs_1_ = bf16[8,256,512]{2,1,0:T(8,128)(2,1)S(1)} all-to-all(bf16[8,256,512]{2,1,0:T(8,128)(2,1)} %bitcast.86), channel_id=1, replica_groups=mesh['fh'=4,'fx'=2,'y'=2,'core'=2] {'fx','y','core'}, dimensions={0} | all-to-all | bytes 4194304 | tf_op jit(solution)/shard_map/all_to_all | solution.py:413
  372.5 3.5 place.1
  (121 shorter events, 13.0 us)
Async XLA Ops:
  6.5 18.4 %copy-start = (bf16[512,2048]{1,0:T(8,128)(2,1)S(1)}, bf16[512,2048]{1,0:T(8,128)(2,1)}, u32[]{:S(2)}) copy-start(bf16[512,2048]{1,0:T(8,128)(2,1)} %param.11) | copy-start | bytes 6291460
  9.2 6.9 %copy-start.25 = (s32[1,1024]{1,0:T(1,128)S(1)}, s32[1,1024]{1,0:T(1,128)}, u32[]{:S(2)}) copy-start(s32[1,1024]{1,0:T(1,128)} %param.8) | copy-start | bytes 12292
  9.2 11.7 %copy-start.28 = (s32[1,8]{1,0:T(1,128)S(1)}, s32[1,8]{1,0:T(1,128)}, u32[]{:S(2)}) copy-start(s32[1,8]{1,0:T(1,128)} %param.7) | copy-start | bytes 100
  10.4 25.1 %collective-permute-start = (bf16[48,6144]{1,0:T(8,128)(2,1)}, bf16[48,6144]{1,0:T(8,128)(2,1)}, u32[]{:S(2)}, u32[]{:S(2)}) collective-permute-start(bf16[48,6144]{1,0:T(8,128)(2,1)} %reshape.129), channel_id=1, source_target_pairs={{0,4},{1,5},{2,6},{3,7},{4,8},{5,9},{6,10},{7,11},{8,12},{9,13},{1... | collective-permute-start | bytes 1769480 | tf_op jit(solution)/shard_map/ppermute | solution.py:274
  16.8 20.8 %all-to-all-start = ((s32[8,1,38]{2,1,0:T(1,128)}), s32[8,1,38]{2,1,0:T(1,128)S(1)}, u32[]{:S(2)}, u32[]{:S(2)}) async-start(s32[8,1,38]{2,1,0:T(1,128)} %bitcast.13), calls=%async_computation | async-start | bytes 8192 | tf_op jit(solution)/shard_map/all_to_all | solution.py:281
  20.9 79.2 %all-gather.7.cloned.1.call-start = ((), (), s32[]{:S(2)}) async-start(), calls=%async_computation.7 | async-start | bytes 2621440 | tf_op jit(solution)/shard_map/all_gather | solution.py:327
  21.0 6.9 %copy-start.26 = (s32[8]{0:T(128)}, s32[8]{0:T(128)S(1)}, u32[]{:S(2)}) copy-start(s32[8]{0:T(128)S(1)} %select_reduce_fusion.order) | copy-start | bytes 100
  21.1 16.5 %collective-permute-start.1 = (s32[8]{0:T(128)S(1)}, s32[8]{0:T(128)S(1)}, u32[]{:S(2)}, u32[]{:S(2)}) collective-permute-start(s32[8]{0:T(128)S(1)} %select_reduce_fusion.order), channel_id=1, source_target_pairs={{0,4},{1,5},{2,6},{3,7},{4,8},{5,9},{6,10},{7,11},{8,12},{9,13},{1... | collective-permute-start | bytes 104 | tf_op jit(solution)/shard_map/ppermute | solution.py:279
  26.8 1.2 copy-start.24
  29.9 4.3 %copy-start.23 = (bf16[128,256]{1,0:T(8,128)(2,1)S(1)}, bf16[128,256]{1,0:T(8,128)(2,1)}, u32[]{:S(2)}) copy-start(bf16[128,256]{1,0:T(8,128)(2,1)} %param.10) | copy-start | bytes 196612
  37.6 1.3 copy-start.27
  46.8 6.9 %copy-start.9 = (bf16[8,6,2048]{2,1,0:T(8,128)(2,1)S(1)}, bf16[8,6,2048]{2,1,0:T(8,128)(2,1)}, u32[]{:S(2)}) copy-start(bf16[8,6,2048]{2,1,0:T(8,128)(2,1)} %get-tuple-element.150) | copy-start | bytes 589828
  46.8 53.3 %all-to-all-start.1 = ((bf16[8,32,2048]{2,1,0:T(8,128)(2,1)}), bf16[8,32,2048]{2,1,0:T(8,128)(2,1)S(1)}, u32[]{:S(2)}, u32[]{:S(2)}) async-start(bf16[8,32,2048]{2,1,0:T(8,128)(2,1)} %short_conv.4), calls=%async_computation.1 | async-start | bytes 2097152 | tf_op jit(solution)/shard_map/all_to_all | solution.py:306
  51.6 48.4 %collective-permute-start.3 = (bf16[512,1024]{1,0:T(8,128)(2,1)}, bf16[512,1024]{1,0:T(8,128)(2,1)}, u32[]{:S(2)}, u32[]{:S(2)}) collective-permute-start(bf16[512,1024]{1,0:T(8,128)(2,1)} %constant_dynamic-slice_fusion.1), channel_id=1, source_target_pairs={{0,4},{4,0},{1,5},{5,1},{2,6},{6,2},{3,7},{7,3},{8,12},{12,8},{9,1... | collective-permute-start | bytes 3145736 | tf_op jit(solution)/shard_map/ppermute | solution.py:374
  55.7 43.2 %collective-permute-start.2 = (bf16[48,6144]{1,0:T(8,128)(2,1)}, bf16[48,6144]{1,0:T(8,128)(2,1)S(1)}, u32[]{:S(2)}, u32[]{:S(2)}) collective-permute-start(bf16[48,6144]{1,0:T(8,128)(2,1)} %reshape.132), channel_id=1, source_target_pairs={{0,4},{1,5},{2,6},{3,7},{4,8},{5,9},{6,10},{7,11},{8,12},{9,13},{1... | collective-permute-start | bytes 1769480 | tf_op jit(solution)/shard_map/ppermute | solution.py:336
  100.0 12.9 %copy-start.7 = (bf16[8,32,2048]{2,1,0:T(8,128)(2,1)}, bf16[8,32,2048]{2,1,0:T(8,128)(2,1)S(1)}, u32[]{:S(2)}) copy-start(bf16[8,32,2048]{2,1,0:T(8,128)(2,1)S(1)} %all-to-all-done.1) | copy-start | bytes 3145732
  100.1 40.4 %all-to-all-start.2 = ((bf16[8,32,2048]{2,1,0:T(8,128)(2,1)}), bf16[8,32,2048]{2,1,0:T(8,128)(2,1)S(1)}, u32[]{:S(2)}, u32[]{:S(2)}) async-start(bf16[8,32,2048]{2,1,0:T(8,128)(2,1)} %short_conv.5), calls=%async_computation.2 | async-start | bytes 2097152 | tf_op jit(solution)/shard_map/all_to_all | solution.py:306
  110.2 2.8 collective-permute-start.4
  112.9 0.7 copy-start.22
  120.7 16.2 %collective-permute-start.5 = (bf16[256,1024]{1,0:T(8,128)(2,1)}, bf16[256,1024]{1,0:T(8,128)(2,1)S(1)}, u32[]{:S(2)}, u32[]{:S(2)}) collective-permute-start(bf16[256,1024]{1,0:T(8,128)(2,1)} %medium_conv.4.refs_0_), channel_id=1, source_target_pairs={{0,4},{4,0},{1,5},{5,1},{2,6},{6,2},{3,7},{7,3},{8,12},{12,8},{9,1... | collective-permute-start | bytes 1572872 | tf_op jit(solution)/shard_map/ppermute | solution.py:394
  122.6 17.8 %collective-permute-start.6 = (bf16[256,1024]{1,0:T(8,128)(2,1)}, bf16[256,1024]{1,0:T(8,128)(2,1)S(1)}, u32[]{:S(2)}, u32[]{:S(2)}) collective-permute-start(bf16[256,1024]{1,0:T(8,128)(2,1)} %medium_conv.4.refs_0_), channel_id=1, source_target_pairs={{0,2},{2,0},{1,3},{3,1},{4,6},{6,4},{5,7},{7,5},{8,10},{10,8},{9,1... | collective-permute-start | bytes 1572872 | tf_op jit(solution)/shard_map/ppermute | solution.py:395
  136.9 3.6 copy-start.15
  140.5 0.8 copy-start.16
  140.5 7.3 %copy-start.6 = (bf16[8,32,2048]{2,1,0:T(8,128)(2,1)}, bf16[8,32,2048]{2,1,0:T(8,128)(2,1)S(1)}, u32[]{:S(2)}) copy-start(bf16[8,32,2048]{2,1,0:T(8,128)(2,1)S(1)} %all-to-all-done.2) | copy-start | bytes 3145732
  141.3 48.0 %all-to-all-start.3 = ((bf16[8,32,2048]{2,1,0:T(8,128)(2,1)}), bf16[8,32,2048]{2,1,0:T(8,128)(2,1)S(1)}, u32[]{:S(2)}, u32[]{:S(2)}) async-start(bf16[8,32,2048]{2,1,0:T(8,128)(2,1)} %short_conv.6), calls=%async_computation.3 | async-start | bytes 2097152 | tf_op jit(solution)/shard_map/all_to_all | solution.py:306
  145.8 82.5 %all-gather.9.cloned.1.call-start = ((), (), s32[]{:S(2)}) async-start(), calls=%async_computation.8 | async-start | bytes 2621440 | tf_op jit(solution)/shard_map/all_gather | solution.py:327
  147.8 2.7 collective-permute-start.8
  149.1 26.5 %collective-permute-start.7 = (bf16[256,1024]{1,0:T(8,128)(2,1)}, bf16[256,1024]{1,0:T(8,128)(2,1)}, u32[]{:S(2)}, u32[]{:S(2)}) collective-permute-start(bf16[256,1024]{1,0:T(8,128)(2,1)} %copy-done.15), channel_id=1, source_target_pairs={{0,2},{2,0},{1,3},{3,1},{4,6},{6,4},{5,7},{7,5},{8,10},{10,8},{9,1... | collective-permute-start | bytes 1572872 | tf_op jit(solution)/shard_map/ppermute | solution.py:379
  150.5 0.7 copy-start.19
  158.3 17.4 %collective-permute-start.9 = (bf16[256,1024]{1,0:T(8,128)(2,1)}, bf16[256,1024]{1,0:T(8,128)(2,1)S(1)}, u32[]{:S(2)}, u32[]{:S(2)}) collective-permute-start(bf16[256,1024]{1,0:T(8,128)(2,1)} %medium_conv.5.refs_0_), channel_id=1, source_target_pairs={{0,4},{4,0},{1,5},{5,1},{2,6},{6,2},{3,7},{7,3},{8,12},{12,8},{9,1... | collective-permute-start | bytes 1572872 | tf_op jit(solution)/shard_map/ppermute | solution.py:394
  160.2 19.0 %collective-permute-start.10 = (bf16[256,1024]{1,0:T(8,128)(2,1)}, bf16[256,1024]{1,0:T(8,128)(2,1)S(1)}, u32[]{:S(2)}, u32[]{:S(2)}) collective-permute-start(bf16[256,1024]{1,0:T(8,128)(2,1)} %medium_conv.5.refs_0_), channel_id=1, source_target_pairs={{0,2},{2,0},{1,3},{3,1},{4,6},{6,4},{5,7},{7,5},{8,10},{10,8},{9,1... | collective-permute-start | bytes 1572872 | tf_op jit(solution)/shard_map/ppermute | solution.py:395
  175.7 17.8 %copy-start.10 = (bf16[256,1024]{1,0:T(8,128)(2,1)}, bf16[256,1024]{1,0:T(8,128)(2,1)S(1)}, u32[]{:S(2)}) copy-start(bf16[256,1024]{1,0:T(8,128)(2,1)S(1)} %collective-permute-done.9.refs_2_) | copy-start | bytes 1572868
  179.2 14.3 %copy-start.11 = (bf16[256,1024]{1,0:T(8,128)(2,1)}, bf16[256,1024]{1,0:T(8,128)(2,1)S(1)}, u32[]{:S(2)}) copy-start(bf16[256,1024]{1,0:T(8,128)(2,1)S(1)} %collective-permute-done.10.refs_1_) | copy-start | bytes 1572868
  189.3 8.3 %copy-start.4 = (bf16[8,32,2048]{2,1,0:T(8,128)(2,1)}, bf16[8,32,2048]{2,1,0:T(8,128)(2,1)S(1)}, u32[]{:S(2)}) copy-start(bf16[8,32,2048]{2,1,0:T(8,128)(2,1)S(1)} %all-to-all-done.3) | copy-start | bytes 3145732
  193.5 34.8 %collective-permute-start.15 = (bf16[1024,1024]{1,0:T(8,128)(2,1)}, bf16[1024,1024]{1,0:T(8,128)(2,1)}, u32[]{:S(2)}, u32[]{:S(2)}) collective-permute-start(bf16[1024,1024]{1,0:T(8,128)(2,1)} %stack.79.refs_0_), channel_id=1, source_target_pairs={{0,1},{1,0},{2,3},{3,2},{4,5},{5,4},{6,7},{7,6},{8,9},{9,8},{10,11... | collective-permute-start | bytes 6291464 | tf_op jit(solution)/shard_map/ppermute | solution.py:367
  193.6 34.7 %all-to-all-start.4 = ((bf16[8,32,2048]{2,1,0:T(8,128)(2,1)}), bf16[8,32,2048]{2,1,0:T(8,128)(2,1)S(1)}, u32[]{:S(2)}, u32[]{:S(2)}) async-start(bf16[8,32,2048]{2,1,0:T(8,128)(2,1)} %short_conv.7), calls=%async_computation.4 | async-start | bytes 2097152 | tf_op jit(solution)/shard_map/all_to_all | solution.py:306
  197.5 118.4 %all-gather.11.cloned.1.call-start = ((), (), s32[]{:S(2)}) async-start(), calls=%async_computation.9 | async-start | bytes 5242880 | tf_op jit(solution)/shard_map/all_gather | solution.py:327
  197.6 3.3 collective-permute-start.12
  199.7 16.9 %collective-permute-start.11 = (bf16[256,1024]{1,0:T(8,128)(2,1)}, bf16[256,1024]{1,0:T(8,128)(2,1)S(1)}, u32[]{:S(2)}, u32[]{:S(2)}) collective-permute-start(bf16[256,1024]{1,0:T(8,128)(2,1)} %copy-done.10), channel_id=1, source_target_pairs={{0,2},{2,0},{1,3},{3,1},{4,6},{6,4},{5,7},{7,5},{8,10},{10,8},{9,1... | collective-permute-start | bytes 1572872 | tf_op jit(solution)/shard_map/ppermute | solution.py:379
  200.9 0.7 copy-start.20
  208.6 19.7 %collective-permute-start.13 = (bf16[256,1024]{1,0:T(8,128)(2,1)}, bf16[256,1024]{1,0:T(8,128)(2,1)S(1)}, u32[]{:S(2)}, u32[]{:S(2)}) collective-permute-start(bf16[256,1024]{1,0:T(8,128)(2,1)} %medium_conv.6.refs_0_), channel_id=1, source_target_pairs={{0,4},{4,0},{1,5},{5,1},{2,6},{6,2},{3,7},{7,3},{8,12},{12,8},{9,1... | collective-permute-start | bytes 1572872 | tf_op jit(solution)/shard_map/ppermute | solution.py:394
  210.3 18.0 %collective-permute-start.14 = (bf16[256,1024]{1,0:T(8,128)(2,1)}, bf16[256,1024]{1,0:T(8,128)(2,1)}, u32[]{:S(2)}, u32[]{:S(2)}) collective-permute-start(bf16[256,1024]{1,0:T(8,128)(2,1)} %medium_conv.6.refs_0_), channel_id=1, source_target_pairs={{0,2},{2,0},{1,3},{3,1},{4,6},{6,4},{5,7},{7,5},{8,10},{10,8},{9,1... | collective-permute-start | bytes 1572872 | tf_op jit(solution)/shard_map/ppermute | solution.py:395
  216.7 11.7 %copy-start.12 = (bf16[256,1024]{1,0:T(8,128)(2,1)}, bf16[256,1024]{1,0:T(8,128)(2,1)S(1)}, u32[]{:S(2)}) copy-start(bf16[256,1024]{1,0:T(8,128)(2,1)S(1)} %collective-permute-done.11.refs_3_) | copy-start | bytes 1572868
  228.3 0.8 copy-start.13
  228.3 4.0 %copy-start.5 = (bf16[8,32,2048]{2,1,0:T(8,128)(2,1)}, bf16[8,32,2048]{2,1,0:T(8,128)(2,1)S(1)}, u32[]{:S(2)}) copy-start(bf16[8,32,2048]{2,1,0:T(8,128)(2,1)S(1)} %all-to-all-done.4) | copy-start | bytes 3145732
  230.2 1.2 copy-start.14
  231.5 14.7 %collective-permute-start.17 = (bf16[256,1024]{1,0:T(8,128)(2,1)S(1)}, bf16[256,1024]{1,0:T(8,128)(2,1)S(1)}, u32[]{:S(2)}, u32[]{:S(2)}) collective-permute-start(bf16[256,1024]{1,0:T(8,128)(2,1)S(1)} %copy-done.14), channel_id=1, source_target_pairs={{0,2},{2,0},{1,3},{3,1},{4,6},{6,4},{5,7},{7,5},{8,10},{10,8},{9,1... | collective-permute-start | bytes 1572872 | tf_op jit(solution)/shard_map/ppermute | solution.py:379
  232.4 3.2 collective-permute-start.16
  235.6 0.7 copy-start.21
  246.1 16.7 %copy-start.17 = (bf16[256,1024]{1,0:T(8,128)(2,1)}, bf16[256,1024]{1,0:T(8,128)(2,1)S(1)}, u32[]{:S(2)}) copy-start(bf16[256,1024]{1,0:T(8,128)(2,1)S(1)} %collective-permute-done.17.refs_3_) | copy-start | bytes 1572868
  246.1 12.6 %collective-permute-start.18 = (bf16[256,1024]{1,0:T(8,128)(2,1)}, bf16[256,1024]{1,0:T(8,128)(2,1)S(1)}, u32[]{:S(2)}, u32[]{:S(2)}) collective-permute-start(bf16[256,1024]{1,0:T(8,128)(2,1)} %medium_conv.7.refs_0_), channel_id=1, source_target_pairs={{0,4},{4,0},{1,5},{5,1},{2,6},{6,2},{3,7},{7,3},{8,12},{12,8},{9,1... | collective-permute-start | bytes 1572872 | tf_op jit(solution)/shard_map/ppermute | solution.py:383
  246.3 34.1 %collective-permute-start.19 = (bf16[256,1024]{1,0:T(8,128)(2,1)}, bf16[256,1024]{1,0:T(8,128)(2,1)}, u32[]{:S(2)}, u32[]{:S(2)}) collective-permute-start(bf16[256,1024]{1,0:T(8,128)(2,1)} %medium_conv.7.refs_0_), channel_id=1, source_target_pairs={{0,2},{2,0},{1,3},{3,1},{4,6},{6,4},{5,7},{7,5},{8,10},{10,8},{9,1... | collective-permute-start | bytes 1572872 | tf_op jit(solution)/shard_map/ppermute | solution.py:384
  257.4 23.0 %collective-permute-start.20 = (bf16[256,1024]{1,0:T(8,128)(2,1)}, bf16[256,1024]{1,0:T(8,128)(2,1)}, u32[]{:S(2)}, u32[]{:S(2)}) collective-permute-start(bf16[256,1024]{1,0:T(8,128)(2,1)} %medium_conv.7.refs_0_), channel_id=1, source_target_pairs={{0,6},{2,4},{4,2},{6,0},{1,7},{3,5},{5,3},{7,1},{8,14},{10,12},{12... | collective-permute-start | bytes 1572872 | tf_op jit(solution)/shard_map/ppermute | solution.py:386
  258.8 4.1 %copy-start.18 = (bf16[256,1024]{1,0:T(8,128)(2,1)}, bf16[256,1024]{1,0:T(8,128)(2,1)S(1)}, u32[]{:S(2)}) copy-start(bf16[256,1024]{1,0:T(8,128)(2,1)S(1)} %collective-permute-done.18.refs_2_) | copy-start | bytes 1572868
  262.9 22.0 %collective-permute-start.21 = (bf16[1024,1024]{1,0:T(8,128)(2,1)}, bf16[1024,1024]{1,0:T(8,128)(2,1)S(1)}, u32[]{:S(2)}, u32[]{:S(2)}) collective-permute-start(bf16[1024,1024]{1,0:T(8,128)(2,1)} %stack.80.refs_1_), channel_id=1, source_target_pairs={{0,1},{1,0},{2,3},{3,2},{4,5},{5,4},{6,7},{7,6},{8,9},{9,8},{10,11... | collective-permute-start | bytes 6291464 | tf_op jit(solution)/shard_map/ppermute | solution.py:367
  273.9 10.9 %collective-permute-start.22 = (bf16[1024,1024]{1,0:T(8,128)(2,1)}, bf16[1024,1024]{1,0:T(8,128)(2,1)}, u32[]{:S(2)}, u32[]{:S(2)}) collective-permute-start(bf16[1024,1024]{1,0:T(8,128)(2,1)} %stack.81.refs_2_), channel_id=1, source_target_pairs={{0,1},{1,0},{2,3},{3,2},{4,5},{5,4},{6,7},{7,6},{8,9},{9,8},{10,11... | collective-permute-start | bytes 6291464 | tf_op jit(solution)/shard_map/ppermute | solution.py:367
  284.3 4.5 %collective-permute-start.23 = (bf16[1024,1024]{1,0:T(8,128)(2,1)}, bf16[1024,1024]{1,0:T(8,128)(2,1)}, u32[]{:S(2)}, u32[]{:S(2)}) collective-permute-start(bf16[1024,1024]{1,0:T(8,128)(2,1)} %stack.82.refs_3_), channel_id=1, source_target_pairs={{0,1},{1,0},{2,3},{3,2},{4,5},{5,4},{6,7},{7,6},{8,9},{9,8},{10,11... | collective-permute-start | bytes 6291464 | tf_op jit(solution)/shard_map/ppermute | solution.py:367
  284.9 4.0 %copy-start.8 = (bf16[1024,1024]{1,0:T(8,128)(2,1)}, bf16[1024,1024]{1,0:T(8,128)(2,1)S(1)}, u32[]{:S(2)}) copy-start(bf16[1024,1024]{1,0:T(8,128)(2,1)S(1)} %collective-permute-done.21.refs_5_) | copy-start | bytes 6291460
  312.3 29.2 %all-to-all-start.5 = ((bf16[8,256,512]{2,1,0:T(8,128)(2,1)}), bf16[8,256,512]{2,1,0:T(8,128)(2,1)S(1)}, u32[]{:S(2)}, u32[]{:S(2)}) async-start(bf16[8,256,512]{2,1,0:T(8,128)(2,1)} %bitcast.85), calls=%async_computation.5 | async-start | bytes 4194304 | tf_op jit(solution)/shard_map/all_to_all | solution.py:413
  341.5 1.3 copy-start.2
  342.8 29.6 %copy-start.3 = (bf16[8,256,512]{2,1,0:T(8,128)(2,1)S(1)}, bf16[8,256,512]{2,1,0:T(8,128)(2,1)}, u32[]{:S(2)}) copy-start(bf16[8,256,512]{2,1,0:T(8,128)(2,1)} %copy-done.2) | copy-start | bytes 6291460
  372.5 3.5 copy-start.1
Sparse Core Ops, SparseCore 0:
  26.0 65.1 all-gather.6
  148.2 72.2 all-gather.8
  231.4 79.6 all-gather.10
